TPU v7x, 512 devices: a whole 4x8x8 slice. The times are simulated.
512 devices in a mesh: pw: 8 (over x, y_lo), pair: 64 (over y_hi, z, core).
Axes of the slice: x: 4, y: 8 (y_hi: 4, y_lo: 2; y = y_hi * 2 + y_lo), z: 8, core: 2. Of those that a mesh axis runs over, the one named last changes fastest.
Arguments:
- valence_pairs: bfloat16 [64, 64, 8192], P('pair', None, 'pw'), may hold values from -0.59765625 to 0.59765625
- conduction_pairs: bfloat16 [64, 256, 8192], P('pair', None, 'pw'), may hold values from -0.59765625 to 0.59765625
- screening: float32 [8192], P('pw'), may hold values from 0.1 to 2
Outputs:
- kernel: float32 [64, 64, 64, 256], P('pair', None, 'pw')
All inputs are finite; a program needn't handle non-finite values.
Results may differ from a plain program's by a relative error of at most 0.0029.
Values may be sent and summed in bfloat16 or wider, within the bound.
No kernel may reach another device: no remote copies, remote signals or barrier semaphores. Data moves between devices by JAX's collectives and lax.ppermute only.
A program may use at most 64 MiB of HBM per device.

v0:
```python
import jax
import jax.numpy as jnp
from jax import lax
from jax.sharding import PartitionSpec as P


def split_up(shard, dim, devices):
    before, after = (shard.shape[:dim], shard.shape[dim + 1 :])
    return jnp.moveaxis(shard.reshape(*before, devices, -1, *after), dim, 0)


def sent_and_summed(shard, axis, dim):
    parts = split_up(shard, dim, lax.axis_size(axis))
    arrived = lax.all_to_all(parts, axis, split_axis=0, concat_axis=0, tiled=True)
    return arrived.sum(axis=0)


def contract(piece, flat_right, band_dev, conduction):
    first, second, width = piece.shape
    product = lax.dot_general(
        piece.reshape(first * second, width),
        flat_right,
        (((1,), (1,)), ((), ())),
        preferred_element_type=jnp.float32,
    )
    return product.reshape(first, second, band_dev, conduction)


def route_rows(terms):
    owned = lax.all_to_all(terms, "pair", split_axis=0, concat_axis=2, tiled=True)
    return owned.transpose(0, 2, 1, 3)


def body(valence_pairs, conduction_pairs, screening):
    screened = (valence_pairs.astype(jnp.float32) * screening[None, None, :]).astype(jnp.bfloat16)
    band_dev, conduction, plane_dev = conduction_pairs.shape
    flat_local = conduction_pairs.reshape(band_dev * conduction, plane_dev)
    partial_value = contract(
        lax.all_gather(screened, "pair", axis=0, tiled=True), flat_local, band_dev, conduction
    )
    terms = sent_and_summed(partial_value, "pw", 1)
    return route_rows(terms)


def solution(mesh):
    placed = (P("pair", None, "pw"), P("pair", None, "pw"), P("pw"))
    return jax.shard_map(
        body, mesh=mesh, in_specs=placed, out_specs=P("pair", None, "pw", None), check_vma=False
    )
```

profile of v0, /device:TPU:1, one launch (start us, length us, event | category | flops | bytes accessed | tf_op | source)
XLA Modules:
  0.0 217.4 jit_solution(5464466841965984867)
XLA Ops:
  6.5 0.0 copy-start
  6.5 0.0 all-gather.2.cloned.1.call-start
  6.5 1.6 multiply_convert_fusion
  8.2 0.0 all-gather.2.cloned.1.call-update
  8.2 112.5 %all-gather.2.cloned.1.call-done = bf16[64,64,1024]{2,1,0:T(8,128)(2,1)} async-done(((bf16[1,64,1024]{2,1,0:T(8,128)(2,1)}), bf16[64,64,1024]{2,1,0:T(8,128)(2,1)}) %all-gather.2.cloned.1.call-update) | async-done | bytes 8388624 | tf_op jit(solution)/shard_map/all_gather | solution.py:39
  120.7 0.0 copy-done
  120.7 5.7 %fusion.2 = f32[8,64,8,1,256]{4,2,0,1,3:T(8,128)S(1)} fusion(bf16[64,64,1024]{2,1,0:T(8,128)(2,1)} %all-gather.2.cloned.1.call-done, bf16[1,256,1024]{2,1,0:T(8,128)(2,1)S(1)} %copy-done), kind=kOutput, calls=%fused_computation.2 | convolution fusion | flops 2147483648 | bytes 13107200 | tf_op jit(solution)/shard_map/dot_general | solution.py:20
  126.5 0.4 copy.4
  126.9 52.5 %all_to_all.23 = f32[8,64,8,1,256]{4,2,1,3,0:T(8,128)} all-to-all(f32[8,64,8,1,256]{4,2,1,3,0:T(8,128)S(1)} %copy.4), channel_id=1, replica_groups=mesh['pw'=8,'pair'=64] {'pw'}, dimensions={0} | all-to-all | bytes 8388608 | tf_op jit(solution)/shard_map/all_to_all | solution.py:14
  179.4 2.5 %reduce_sum.11 = f32[64,8,256]{2,1,0:T(8,128)S(1)} reduce(f32[8,64,8,1,256]{4,2,1,3,0:T(8,128)} %all_to_all.23, f32[]{:T(128)} %constant.0.clone.1), dimensions={0,3}, to_apply=%region_0.0 | reduce | flops 917504 | bytes 4718596 | tf_op jit(solution)/shard_map/reduce_sum | solution.py:15
  182.0 27.8 %all_to_all.24 = f32[64,8,1,256]{3,1,2,0:T(8,128)S(1)} all-to-all(f32[64,8,1,256]{3,1,2,0:T(8,128)S(1)} %bitcast.24), channel_id=1, replica_groups=mesh['pw'=8,'pair'=64] {'pair'}, dimensions={0} | all-to-all | bytes 1048576 | tf_op jit(solution)/shard_map/all_to_all | solution.py:30
  209.8 0.8 copy.7
Async XLA Ops:
  6.5 114.2 %copy-start = (bf16[1,256,1024]{2,1,0:T(8,128)(2,1)S(1)}, bf16[1,256,1024]{2,1,0:T(8,128)(2,1)}, u32[]{:S(2)}) copy-start(bf16[1,256,1024]{2,1,0:T(8,128)(2,1)} %param.4) | copy-start | bytes 1572868
  6.5 114.2 %all-gather.2.cloned.1.call-start = ((), (), s32[]{:S(2)}) async-start(), calls=%async_computation.2 | async-start | bytes 8519680 | tf_op jit(solution)/shard_map/all_gather | solution.py:39
Sparse Core Ops, SparseCore 0:
  10.7 109.9 all-gather.1
where the time goes:
time: 218 us; the launch traced here: 217 us
  waiting for transfers between devices  113 us (52%)
  blocking collectives  80.3 us (37%)
  between operations  13.4 us (6%)
  matrix products  5.75 us (3%)
  other arithmetic  4.16 us (2%)
    all_gather x1, waiting for transfers between devices, body(): lax.all_gather(screened, 'pair', axis=0, tiled=True)  113 us
    all_to_all x1, blocking collectives, sent_and_summed(): lax.all_to_all(parts, axis, split_axis=0, concat_axis=0, tiled=True)  52.5 us
    all_to_all x1, blocking collectives, route_rows(): lax.all_to_all(terms, 'pair', split_axis=0, concat_axis=2, tiled=True)  27.8 us
    dot_general x1, matrix products, contract(): lax.dot_general(piece.reshape(first * second, width), flat_right, (((1,),...  5.75 us
  transfers between devices with their start and end apart: 1, of which 1 were waited for; matrix products, arithmetic and copies ran while one was open for 0% of the time, Pallas kernels for 0%

commit v1 on v0

v1 whole, which is shorter than its diff:
```python
import functools

import jax
import jax.numpy as jnp
from jax import lax
from jax.experimental import pallas as pl
from jax.experimental.pallas import tpu as pltpu
from jax.sharding import Mesh, PartitionSpec as P

BF16 = jnp.bfloat16
F32 = jnp.float32
AXES = ("x", "yl", "yh", "z", "core")
SIZES = (4, 2, 4, 8, 2)
NX, NL, NH, NZ, NC = SIZES


def place(y):
    return (y % NL) * NH + y // NL


def intra(block):
    return lax.ppermute(block, "yl", [(0, 1), (1, 0)])


def inter(block):
    ny = NL * NH
    pairs = []
    for j in range(NH):
        a, b = place(2 * j + 1), place((2 * j + 2) % ny)
        pairs += [(a, b), (b, a)]
    return lax.ppermute(block, ("yl", "yh"), pairs)


def dot(left, right):
    return lax.dot_general(left, right, (((1,), (1,)), ((), ())), preferred_element_type=F32)


def product_kernel(parts, mine_ref, other_ref, *refs):
    rights, out_ref = refs[:-1], refs[-1]
    yl, core = lax.axis_index("yl"), lax.axis_index("core")
    _, nz, rows, width = mine_ref.shape
    nx = NX
    wide = rows // nx
    for which, ref in enumerate((mine_ref, other_ref)):
        target_core = core if which == 0 else 1 - core
        left = {h: ref[yl if h == 0 else 1 - yl].reshape(nz * rows, width) for h in (0, 1)}
        sums = []
        for slot in parts:
            pieces = {}
            for half, index, start in slot:
                pieces.setdefault(start, []).append(dot(left[half], rights[index][...]))
            sums.append(pieces)
        done = []
        for pieces in sums:
            whole = [sum(p[1:], p[0]) for p in (pieces[k] for k in sorted(pieces, key=str) if k is None)]
            halves = [k for k in sorted(k for k in pieces if k is not None)]
            total = whole[0] if whole else None
            if halves:
                joined = jnp.concatenate([pieces[k][0] for k in halves], axis=1)
                total = joined if total is None else total + joined
            done.append(total)
        for zi in range(nz):
            for xi in range(nx):
                at = zi * rows + xi * wide
                block = jnp.concatenate([d[at : at + wide] for d in done], axis=0)
                out_ref[(xi * nz + zi) * NC + target_core] = block.astype(BF16)


def product(mine, other, rights, parts):
    _, nz, rows, width = mine.shape
    wide = rows // NX
    columns = 256
    members = NX * nz * NC
    flops = 2 * 2 * nz * rows * width * 2 * columns * 2
    return pl.pallas_call(
        functools.partial(product_kernel, parts),
        out_shape=jax.ShapeDtypeStruct((members, 2 * wide, columns), BF16),
        in_specs=[pl.BlockSpec(memory_space=pltpu.VMEM)] * (2 + len(rights)),
        out_specs=pl.BlockSpec(memory_space=pltpu.VMEM),
        compiler_params=pltpu.CompilerParams(vmem_limit_bytes=16 * 1024 * 1024),
        cost_estimate=pl.CostEstimate(flops=flops, bytes_accessed=5 * 2**20, transcendentals=0),
    )(mine, other, *rights)


def finish_kernel(first_ref, second_ref, out_ref):
    yh = lax.axis_index("yh")
    step = 1 - 2 * lax.axis_index("yl")
    owners = [lax.rem(yh + NH + k, NH) for k in (0, -step, step, 2)]
    for which, ref in enumerate((first_ref, second_ref)):
        total = ref[0].astype(F32)
        for xi in range(1, NX):
            total = total + ref[xi].astype(F32)
        wide = total.shape[1] // 2
        out_ref[owners[2 * which]] = total[:, :wide]
        out_ref[owners[2 * which + 1]] = total[:, wide:]


def finish(first, second):
    members, tall, columns = first.shape
    rest = members // NX
    first = first.reshape(NX, rest, tall, columns)
    second = second.reshape(NX, rest, tall, columns)
    step = 4
    spec = pl.BlockSpec((NX, step, tall, columns), lambda i: (0, i, 0, 0))
    return pl.pallas_call(
        finish_kernel,
        grid=(rest // step,),
        out_shape=jax.ShapeDtypeStruct((NH, rest, tall // 2, columns), F32),
        in_specs=[spec, spec],
        out_specs=pl.BlockSpec((NH, step, tall // 2, columns), lambda i: (0, i, 0, 0)),
        cost_estimate=pl.CostEstimate(flops=2**19, bytes_accessed=3 * 2**19, transcendentals=0),
    )(first, second)


def body(valence_pairs, conduction_pairs, screening):
    _, second, plane_dev = valence_pairs.shape
    own = conduction_pairs[0]
    half = own.shape[0] // 2

    screened = (valence_pairs[0].astype(F32) * screening[None, :]).astype(BF16)
    wide = second // (NX * NL)
    by_half = screened.reshape(NX, NL, wide, plane_dev).transpose(1, 0, 2, 3)
    by_half = by_half.reshape(NL, 1, NX * wide, plane_dev)
    sent = jnp.broadcast_to(by_half, (NL, NZ, NX * wide, plane_dev))
    sent = sent.reshape(NL * NZ, NX * wide, plane_dev)
    mine = lax.all_to_all(sent, ("yl", "z"), 0, 0, tiled=True)
    f1, b1 = intra(own), inter(own)
    f2, b2 = intra(b1), inter(f1)
    mine, _, _ = lax.optimization_barrier((mine, f2, b2))
    other = lax.ppermute(mine, "core", [(0, 1), (1, 0)])
    mine = mine.reshape(NL, NZ, NX * wide, plane_dev)
    other = other.reshape(NL, NZ, NX * wide, plane_dev)
    f3, b3 = intra(b2), inter(f2)
    g4, h4 = intra(b3[:half]), inter(f3[half:])

    mine, other, _, _ = lax.optimization_barrier((mine, other, f3, b3))
    first = product(
        mine, other, (own, f1, b1, b2),
        (((0, 0, None), (1, 1, None)), ((1, 2, None), (0, 3, None))),
    )
    first = lax.all_to_all(first, ("x", "z", "core"), 0, 0, tiled=True)
    last = product(
        mine, other, (f2, f3, b3, g4, h4),
        (((0, 0, None), (1, 1, None)), ((1, 2, None), (0, 3, 0), (0, 4, 1))),
    )
    last = lax.all_to_all(last, ("x", "z", "core"), 0, 0, tiled=True)
    out = finish(first, last)
    return out.reshape(1, NH * NZ * NC, wide, own.shape[0])


def solution(mesh):
    fine = Mesh(mesh.devices.reshape(SIZES), AXES)
    pair, pw = ("yh", "z", "core"), ("x", "yl")
    placed = (P(pair, None, pw), P(pair, None, pw), P(pw))
    return jax.shard_map(
        body, mesh=fine, in_specs=placed, out_specs=P(pair, None, pw, None), check_vma=False
    )
```

time: 218 us -> 141 us (0.65)
  waiting for transfers between devices: 113 us -> 42.9 us
  starting transfers between devices: 0.01 us -> 55.6 us
  blocking collectives: 80.3 us -> 26.2 us
  between operations: 13.4 us -> 0.18 us
  Pallas kernels: 0 us -> 8 us
  matrix products: 5.75 us -> 0 us
  local copies, waits for them, and re-layouts: 1.19 us -> 6.88 us
  other arithmetic: 4.16 us -> 0.93 us
    all_gather x1 -> x0, waiting for transfers between devices: 113 us -> none  [body(): lax.all_gather(screened, 'pair', axis=0, tiled=True)]
    all_to_all x2 -> x1, blocking collectives: 80.3 us -> 26.2 us  [body(): last = lax.all_to_all(last, ('x', 'z', 'core'), 0, 0, tiled=True)]
    ppermute x0 -> x9, waiting for transfers between devices: none -> 40.2 us  [the longest x4 23.3 us: intra(): return lax.ppermute(block, 'yl', [(0, 1), (1, 0)])]
    ppermute x0 -> x9, starting transfers between devices: none -> 33.1 us  [the longest x4 18.5 us: inter(): return lax.ppermute(block, ('yl', 'yh'), pairs)]
    all_to_all x0 -> x2, starting transfers between devices: none -> 22.6 us  [the longest x1 12.1 us: body(): mine = lax.all_to_all(sent, ('yl', 'z'), 0, 0, tiled=True)]
    pallas_call x0 -> x3, Pallas kernels: none -> 8 us  [the longest x2 4.66 us: product(): pl.pallas_call(functools.partial(product_kernel, parts), out_shape=jax.Sh...]
    dot_general x1 -> x0, matrix products: 5.75 us -> none  [contract(): lax.dot_general(piece.reshape(first * second, width), flat_right, (((1,),...]
    unnamed x3 -> x20, local copies, waits for them, and re-layouts: 0.8 us -> 5.72 us
  transfers between devices with their start and end apart: 1 -> 11, of which waited for: 1 -> 9; matrix products, arithmetic and copies ran while one was open for 0% -> 0% of each run, Pallas kernels for 0% -> 1%
where the time goes in v1:
time: 141 us
  starting transfers between devices  55.6 us (39%)
  waiting for transfers between devices  42.9 us (30%)
  blocking collectives  26.2 us (19%)
  Pallas kernels  8 us (6%)
  local copies, waits for them, and re-layouts  6.88 us (5%)
    all_to_all x1, blocking collectives, body(): last = lax.all_to_all(last, ('x', 'z', 'core'), 0, 0, tiled=True)  26.2 us
    ppermute x4, waiting for transfers between devices, intra(): return lax.ppermute(block, 'yl', [(0, 1), (1, 0)])  23.3 us
    ppermute x4, starting transfers between devices, inter(): return lax.ppermute(block, ('yl', 'yh'), pairs)  18.5 us
    ppermute x4, waiting for transfers between devices, inter(): return lax.ppermute(block, ('yl', 'yh'), pairs)  16.9 us
    all_to_all x1, starting transfers between devices, body(): mine = lax.all_to_all(sent, ('yl', 'z'), 0, 0, tiled=True)  12.1 us
    all_to_all x1, starting transfers between devices, body(): first = lax.all_to_all(first, ('x', 'z', 'core'), 0, 0, tiled=True)  10.5 us
    ppermute x4, starting transfers between devices, intra(): return lax.ppermute(block, 'yl', [(0, 1), (1, 0)])  8.48 us
    ppermute x1, starting transfers between devices, body(): other = lax.ppermute(mine, 'core', [(0, 1), (1, 0)])  6.07 us
  transfers between devices with their start and end apart: 11, of which 9 were waited for; matrix products, arithmetic and copies ran while one was open for 0% of the time, Pallas kernels for 1%

profile of v1, /device:TPU:1, one launch (start us, length us, event | category | flops | bytes accessed | tf_op | source)
XLA Modules:
  0.0 140.7 jit_solution(14225584801818532241)
XLA Ops:
  2.1 12.1 %all-to-all-start = ((bf16[16,32,1024]{2,1,0:T(8,128)(2,1)}), bf16[16,32,1024]{2,1,0:T(8,128)(2,1)S(1)}, u32[]{:S(2)}, u32[]{:S(2)}) async-start(bf16[16,32,1024]{2,1,0:T(8,128)(2,1)} %bitcast.3), calls=%async_computation | async-start | bytes 2097152 | tf_op jit(solution)/shard_map/all_to_all | solution.py:126
  14.2 5.2 %collective-permute-start = (bf16[256,1024]{1,0:T(8,128)(2,1)S(1)}, bf16[256,1024]{1,0:T(8,128)(2,1)S(1)}, u32[]{:S(2)}, u32[]{:S(2)}) collective-permute-start(bf16[256,1024]{1,0:T(8,128)(2,1)S(1)} %bitcast.18), channel_id=1, source_target_pairs={{64,16},{16,64},{80,32},{32,80},{96,48},{48,96},{112,0},{0,112},{6... | collective-permute-start | bytes 1572872 | tf_op jit(solution)/shard_map/ppermute | solution.py:31
  19.4 1.9 %collective-permute-start.2 = (bf16[256,1024]{1,0:T(8,128)(2,1)S(1)}, bf16[256,1024]{1,0:T(8,128)(2,1)S(1)}, u32[]{:S(2)}, u32[]{:S(2)}) collective-permute-start(bf16[256,1024]{1,0:T(8,128)(2,1)S(1)} %bitcast.19), channel_id=1, source_target_pairs={{0,64},{64,0},{1,65},{65,1},{2,66},{66,2},{3,67},{67,3},{4,68},{68... | collective-permute-start | bytes 1572872 | tf_op jit(solution)/shard_map/ppermute | solution.py:22
  21.3 9.1 %collective-permute-done.refs_2_ = bf16[256,1024]{1,0:T(8,128)(2,1)S(1)} collective-permute-done((bf16[256,1024]{1,0:T(8,128)(2,1)S(1)}, bf16[256,1024]{1,0:T(8,128)(2,1)S(1)}, u32[]{:S(2)}, u32[]{:S(2)}) %collective-permute-start) | collective-permute-done | bytes 524320 | tf_op jit(solution)/shard_map/ppermute | solution.py:31
  30.4 1.9 %collective-permute-start.1 = (bf16[256,1024]{1,0:T(8,128)(2,1)S(1)}, bf16[256,1024]{1,0:T(8,128)(2,1)S(1)}, u32[]{:S(2)}, u32[]{:S(2)}) collective-permute-start(bf16[256,1024]{1,0:T(8,128)(2,1)S(1)} %collective-permute-done.refs_2_), channel_id=1, source_target_pairs={{0,64},{64,0},{1,65},{65,1},{2,66},{66,2},{3,67},{67,3},{4,68},{68... | collective-permute-start | bytes 1572872 | tf_op jit(solution)/shard_map/ppermute | solution.py:22
  33.1 5.7 %collective-permute-done.2.refs_1_ = bf16[256,1024]{1,0:T(8,128)(2,1)S(1)} collective-permute-done((bf16[256,1024]{1,0:T(8,128)(2,1)S(1)}, bf16[256,1024]{1,0:T(8,128)(2,1)S(1)}, u32[]{:S(2)}, u32[]{:S(2)}) %collective-permute-start.2) | collective-permute-done | bytes 524320 | tf_op jit(solution)/shard_map/ppermute | solution.py:22
  38.8 4.6 %collective-permute-start.3 = (bf16[256,1024]{1,0:T(8,128)(2,1)S(1)}, bf16[256,1024]{1,0:T(8,128)(2,1)}, u32[]{:S(2)}, u32[]{:S(2)}) collective-permute-start(bf16[256,1024]{1,0:T(8,128)(2,1)S(1)} %collective-permute-done.2.refs_1_), channel_id=1, source_target_pairs={{64,16},{16,64},{80,32},{32,80},{96,48},{48,96},{112,0},{0,112},{6... | collective-permute-start | bytes 1572872 | tf_op jit(solution)/shard_map/ppermute | solution.py:31
  44.3 5.9 %collective-permute-done.1.refs_0_ = bf16[256,1024]{1,0:T(8,128)(2,1)S(1)} collective-permute-done((bf16[256,1024]{1,0:T(8,128)(2,1)S(1)}, bf16[256,1024]{1,0:T(8,128)(2,1)S(1)}, u32[]{:S(2)}, u32[]{:S(2)}) %collective-permute-start.1) | collective-permute-done | bytes 524320 | tf_op jit(solution)/shard_map/ppermute | solution.py:22
  51.0 1.3 collective-permute-done.3.refs_3_
  52.3 6.1 %collective-permute-start.4 = (bf16[16,32,1024]{2,1,0:T(8,128)(2,1)S(1)}, bf16[16,32,1024]{2,1,0:T(8,128)(2,1)S(1)}, u32[]{:S(2)}, u32[]{:S(2)}) collective-permute-start(bf16[16,32,1024]{2,1,0:T(8,128)(2,1)S(1)} %all-to-all-done), channel_id=1, source_target_pairs={{0,1},{1,0},{2,3},{3,2},{4,5},{5,4},{6,7},{7,6},{8,9},{9,8},{10,11... | collective-permute-start | bytes 3145736 | tf_op jit(solution)/shard_map/ppermute | solution.py:130
  58.4 1.9 %collective-permute-start.5 = (bf16[256,1024]{1,0:T(8,128)(2,1)}, bf16[256,1024]{1,0:T(8,128)(2,1)S(1)}, u32[]{:S(2)}, u32[]{:S(2)}) collective-permute-start(bf16[256,1024]{1,0:T(8,128)(2,1)} %collective-permute-done.3.refs_3_), channel_id=1, source_target_pairs={{0,64},{64,0},{1,65},{65,1},{2,66},{66,2},{3,67},{67,3},{4,68},{68... | collective-permute-start | bytes 1572872 | tf_op jit(solution)/shard_map/ppermute | solution.py:22
  60.3 4.6 %collective-permute-start.6 = (bf16[256,1024]{1,0:T(8,128)(2,1)}, bf16[256,1024]{1,0:T(8,128)(2,1)S(1)}, u32[]{:S(2)}, u32[]{:S(2)}) collective-permute-start(bf16[256,1024]{1,0:T(8,128)(2,1)} %copy-done.4), channel_id=1, source_target_pairs={{64,16},{16,64},{80,32},{32,80},{96,48},{48,96},{112,0},{0,112},{6... | collective-permute-start | bytes 1572872 | tf_op jit(solution)/shard_map/ppermute | solution.py:31
  64.9 9.1 %collective-permute-done.5.refs_1_ = bf16[256,1024]{1,0:T(8,128)(2,1)S(1)} collective-permute-done((bf16[256,1024]{1,0:T(8,128)(2,1)}, bf16[256,1024]{1,0:T(8,128)(2,1)S(1)}, u32[]{:S(2)}, u32[]{:S(2)}) %collective-permute-start.5) | collective-permute-done | bytes 524320 | tf_op jit(solution)/shard_map/ppermute | solution.py:22
  74.0 3.0 %collective-permute-done.6.refs_2_ = bf16[256,1024]{1,0:T(8,128)(2,1)S(1)} collective-permute-done((bf16[256,1024]{1,0:T(8,128)(2,1)}, bf16[256,1024]{1,0:T(8,128)(2,1)S(1)}, u32[]{:S(2)}, u32[]{:S(2)}) %collective-permute-start.6) | collective-permute-done | bytes 524320 | tf_op jit(solution)/shard_map/ppermute | solution.py:31
  80.3 3.1 %shard_map.37 = bf16[64,16,256]{2,1,0:T(8,128)(2,1)} custom-call(bf16[2,8,32,1024]{3,2,1,0:T(8,128)(2,1)S(1)} %bitcast.14, bf16[2,8,32,1024]{3,2,1,0:T(8,128)(2,1)S(1)} %bitcast.16, bf16[256,1024]{1,0:T(8,128)(2,1)S(1)} %bitcast.20, bf16[256,1024]{1,0:T(8,128)(2,1)S(1)} %copy-done.9, bf16[256,1024]{1,0:T(8,128)(2,1)S(1)} %copy-done.7, ...), custom_call_target="tpu_custom_call" | custom-call | flops 1073741824 | bytes 5242880 | tf_op jit(solution)/shard_map/pallas_call | solution.py:75
  83.4 10.5 %all-to-all-start.1 = ((bf16[64,16,256]{2,1,0:T(8,128)(2,1)}), bf16[64,16,256]{2,1,0:T(8,128)(2,1)}, u32[]{:S(2)}, u32[]{:S(2)}) async-start(bf16[64,16,256]{2,1,0:T(8,128)(2,1)} %shard_map.37), calls=%async_computation.1 | async-start | bytes 1048576 | tf_op jit(solution)/shard_map/all_to_all | solution.py:141
  94.0 2.7 %collective-permute-start.7 = (bf16[128,1024]{1,0:T(8,128)(2,1)S(1)}, bf16[128,1024]{1,0:T(8,128)(2,1)S(1)}, u32[]{:S(2)}, u32[]{:S(2)}) collective-permute-start(bf16[128,1024]{1,0:T(8,128)(2,1)S(1)} %slice.8), channel_id=1, source_target_pairs={{0,64},{64,0},{1,65},{65,1},{2,66},{66,2},{3,67},{67,3},{4,68},{68... | collective-permute-start | bytes 786440 | tf_op jit(solution)/shard_map/ppermute | solution.py:22
  96.7 4.1 %collective-permute-start.8 = (bf16[128,1024]{1,0:T(8,128)(2,1)S(1)}, bf16[128,1024]{1,0:T(8,128)(2,1)S(1)}, u32[]{:S(2)}, u32[]{:S(2)}) collective-permute-start(bf16[128,1024]{1,0:T(8,128)(2,1)S(1)} %slice.9), channel_id=1, source_target_pairs={{64,16},{16,64},{80,32},{32,80},{96,48},{48,96},{112,0},{0,112},{6... | collective-permute-start | bytes 786440 | tf_op jit(solution)/shard_map/ppermute | solution.py:31
  100.9 2.6 %collective-permute-done.7.refs_3_ = bf16[128,1024]{1,0:T(8,128)(2,1)S(1)} collective-permute-done((bf16[128,1024]{1,0:T(8,128)(2,1)S(1)}, bf16[128,1024]{1,0:T(8,128)(2,1)S(1)}, u32[]{:S(2)}, u32[]{:S(2)}) %collective-permute-start.7) | collective-permute-done | bytes 262176 | tf_op jit(solution)/shard_map/ppermute | solution.py:22
  103.5 3.5 %collective-permute-done.8.refs_4_ = bf16[128,1024]{1,0:T(8,128)(2,1)S(1)} collective-permute-done((bf16[128,1024]{1,0:T(8,128)(2,1)S(1)}, bf16[128,1024]{1,0:T(8,128)(2,1)S(1)}, u32[]{:S(2)}, u32[]{:S(2)}) %collective-permute-start.8) | collective-permute-done | bytes 262176 | tf_op jit(solution)/shard_map/ppermute | solution.py:31
  107.0 1.5 %shard_map.38 = bf16[64,16,256]{2,1,0:T(8,128)(2,1)S(1)} custom-call(bf16[2,8,32,1024]{3,2,1,0:T(8,128)(2,1)S(1)} %bitcast.15, bf16[2,8,32,1024]{3,2,1,0:T(8,128)(2,1)S(1)} %bitcast.17, bf16[256,1024]{1,0:T(8,128)(2,1)S(1)} %copy-done.5, bf16[256,1024]{1,0:T(8,128)(2,1)S(1)} %collective-permute-done.5.refs_1_, bf16[256,1024]{1,0:T(8,128)(2,1)S(1)} %copy-done.1, ...), custom_call_target="tpu_custom_call" | custom-call | flops 1073741824 | bytes 5242880 | tf_op jit(solution)/shard_map/pallas_call | solution.py:75
  108.5 2.6 %all-to-all-done.1 = bf16[64,16,256]{2,1,0:T(8,128)(2,1)} async-done(((bf16[64,16,256]{2,1,0:T(8,128)(2,1)}), bf16[64,16,256]{2,1,0:T(8,128)(2,1)}, u32[]{:S(2)}, u32[]{:S(2)}) %all-to-all-start.1) | async-done | bytes 524320 | tf_op jit(solution)/shard_map/all_to_all | solution.py:141
  111.2 26.2 %all_to_all.15 = bf16[64,16,256]{2,1,0:T(8,128)(2,1)} all-to-all(bf16[64,16,256]{2,1,0:T(8,128)(2,1)S(1)} %shard_map.38), channel_id=1, replica_groups=mesh['x'=4,'yl'=2,'yh'=4,'z'=8,'core'=2] {'x','z','core'}, dimensions={0} | all-to-all | bytes 1048576 | tf_op jit(solution)/shard_map/all_to_all | solution.py:146
  137.3 3.3 %shard_map.39 = f32[4,16,8,256]{3,2,1,0:T(8,128)} custom-call(bf16[4,16,16,256]{3,2,1,0:T(8,128)(2,1)} %bitcast.7.first_ref, bf16[4,16,16,256]{3,2,1,0:T(8,128)(2,1)} %bitcast.21), custom_call_target="tpu_custom_call" | custom-call | flops 524288 | bytes 1572864 | tf_op jit(solution)/shard_map/pallas_call | solution.py:105
  (26 shorter events, 7.8 us)
Async XLA Ops:
  2.1 12.1 %copy-start.2 = (bf16[1,256,1024]{2,1,0:T(8,128)(2,1)S(1)}, bf16[1,256,1024]{2,1,0:T(8,128)(2,1)}, u32[]{:S(2)}) copy-start(bf16[1,256,1024]{2,1,0:T(8,128)(2,1)} %param.4) | copy-start | bytes 1572868
  2.1 50.2 %all-to-all-start = ((bf16[16,32,1024]{2,1,0:T(8,128)(2,1)}), bf16[16,32,1024]{2,1,0:T(8,128)(2,1)S(1)}, u32[]{:S(2)}, u32[]{:S(2)}) async-start(bf16[16,32,1024]{2,1,0:T(8,128)(2,1)} %bitcast.3), calls=%async_computation | async-start | bytes 2097152 | tf_op jit(solution)/shard_map/all_to_all | solution.py:126
  14.2 16.2 %collective-permute-start = (bf16[256,1024]{1,0:T(8,128)(2,1)S(1)}, bf16[256,1024]{1,0:T(8,128)(2,1)S(1)}, u32[]{:S(2)}, u32[]{:S(2)}) collective-permute-start(bf16[256,1024]{1,0:T(8,128)(2,1)S(1)} %bitcast.18), channel_id=1, source_target_pairs={{64,16},{16,64},{80,32},{32,80},{96,48},{48,96},{112,0},{0,112},{6... | collective-permute-start | bytes 1572872 | tf_op jit(solution)/shard_map/ppermute | solution.py:31
  19.4 19.5 %collective-permute-start.2 = (bf16[256,1024]{1,0:T(8,128)(2,1)S(1)}, bf16[256,1024]{1,0:T(8,128)(2,1)S(1)}, u32[]{:S(2)}, u32[]{:S(2)}) collective-permute-start(bf16[256,1024]{1,0:T(8,128)(2,1)S(1)} %bitcast.19), channel_id=1, source_target_pairs={{0,64},{64,0},{1,65},{65,1},{2,66},{66,2},{3,67},{67,3},{4,68},{68... | collective-permute-start | bytes 1572872 | tf_op jit(solution)/shard_map/ppermute | solution.py:22
  30.4 19.8 %collective-permute-start.1 = (bf16[256,1024]{1,0:T(8,128)(2,1)S(1)}, bf16[256,1024]{1,0:T(8,128)(2,1)S(1)}, u32[]{:S(2)}, u32[]{:S(2)}) collective-permute-start(bf16[256,1024]{1,0:T(8,128)(2,1)S(1)} %collective-permute-done.refs_2_), channel_id=1, source_target_pairs={{0,64},{64,0},{1,65},{65,1},{2,66},{66,2},{3,67},{67,3},{4,68},{68... | collective-permute-start | bytes 1572872 | tf_op jit(solution)/shard_map/ppermute | solution.py:22
  32.3 0.8 copy-start.6
  38.8 13.5 %collective-permute-start.3 = (bf16[256,1024]{1,0:T(8,128)(2,1)S(1)}, bf16[256,1024]{1,0:T(8,128)(2,1)}, u32[]{:S(2)}, u32[]{:S(2)}) collective-permute-start(bf16[256,1024]{1,0:T(8,128)(2,1)S(1)} %collective-permute-done.2.refs_1_), channel_id=1, source_target_pairs={{64,16},{16,64},{80,32},{32,80},{96,48},{48,96},{112,0},{0,112},{6... | collective-permute-start | bytes 1572872 | tf_op jit(solution)/shard_map/ppermute | solution.py:31
  43.5 0.8 copy-start.8
  50.2 0.8 copy-start.4
  52.3 24.7 %collective-permute-start.4 = (bf16[16,32,1024]{2,1,0:T(8,128)(2,1)S(1)}, bf16[16,32,1024]{2,1,0:T(8,128)(2,1)S(1)}, u32[]{:S(2)}, u32[]{:S(2)}) collective-permute-start(bf16[16,32,1024]{2,1,0:T(8,128)(2,1)S(1)} %all-to-all-done), channel_id=1, source_target_pairs={{0,1},{1,0},{2,3},{3,2},{4,5},{5,4},{6,7},{7,6},{8,9},{9,8},{10,11... | collective-permute-start | bytes 3145736 | tf_op jit(solution)/shard_map/ppermute | solution.py:130
  58.4 15.6 %collective-permute-start.5 = (bf16[256,1024]{1,0:T(8,128)(2,1)}, bf16[256,1024]{1,0:T(8,128)(2,1)S(1)}, u32[]{:S(2)}, u32[]{:S(2)}) collective-permute-start(bf16[256,1024]{1,0:T(8,128)(2,1)} %collective-permute-done.3.refs_3_), channel_id=1, source_target_pairs={{0,64},{64,0},{1,65},{65,1},{2,66},{66,2},{3,67},{67,3},{4,68},{68... | collective-permute-start | bytes 1572872 | tf_op jit(solution)/shard_map/ppermute | solution.py:22
  60.3 16.7 %collective-permute-start.6 = (bf16[256,1024]{1,0:T(8,128)(2,1)}, bf16[256,1024]{1,0:T(8,128)(2,1)S(1)}, u32[]{:S(2)}, u32[]{:S(2)}) collective-permute-start(bf16[256,1024]{1,0:T(8,128)(2,1)} %copy-done.4), channel_id=1, source_target_pairs={{64,16},{16,64},{80,32},{32,80},{96,48},{48,96},{112,0},{0,112},{6... | collective-permute-start | bytes 1572872 | tf_op jit(solution)/shard_map/ppermute | solution.py:31
  77.0 16.9 %copy-start = (bf16[256,1024]{1,0:T(8,128)(2,1)}, bf16[256,1024]{1,0:T(8,128)(2,1)S(1)}, u32[]{:S(2)}) copy-start(bf16[256,1024]{1,0:T(8,128)(2,1)S(1)} %collective-permute-done.6.refs_2_) | copy-start | bytes 1572868
  77.0 1.2 copy-start.3
  78.2 1.0 copy-start.7
  79.3 1.0 copy-start.9
  83.4 27.7 %all-to-all-start.1 = ((bf16[64,16,256]{2,1,0:T(8,128)(2,1)}), bf16[64,16,256]{2,1,0:T(8,128)(2,1)}, u32[]{:S(2)}, u32[]{:S(2)}) async-start(bf16[64,16,256]{2,1,0:T(8,128)(2,1)} %shard_map.37), calls=%async_computation.1 | async-start | bytes 1048576 | tf_op jit(solution)/shard_map/all_to_all | solution.py:141
  93.9 13.0 %copy-start.5 = (bf16[256,1024]{1,0:T(8,128)(2,1)S(1)}, bf16[256,1024]{1,0:T(8,128)(2,1)}, u32[]{:S(2)}) copy-start(bf16[256,1024]{1,0:T(8,128)(2,1)} %copy-done.4) | copy-start | bytes 1572868
  94.0 13.0 %copy-start.1 = (bf16[256,1024]{1,0:T(8,128)(2,1)S(1)}, bf16[256,1024]{1,0:T(8,128)(2,1)}, u32[]{:S(2)}) copy-start(bf16[256,1024]{1,0:T(8,128)(2,1)} %copy-done) | copy-start | bytes 1572868
  94.0 9.5 %collective-permute-start.7 = (bf16[128,1024]{1,0:T(8,128)(2,1)S(1)}, bf16[128,1024]{1,0:T(8,128)(2,1)S(1)}, u32[]{:S(2)}, u32[]{:S(2)}) collective-permute-start(bf16[128,1024]{1,0:T(8,128)(2,1)S(1)} %slice.8), channel_id=1, source_target_pairs={{0,64},{64,0},{1,65},{65,1},{2,66},{66,2},{3,67},{67,3},{4,68},{68... | collective-permute-start | bytes 786440 | tf_op jit(solution)/shard_map/ppermute | solution.py:22
  96.7 10.2 %collective-permute-start.8 = (bf16[128,1024]{1,0:T(8,128)(2,1)S(1)}, bf16[128,1024]{1,0:T(8,128)(2,1)S(1)}, u32[]{:S(2)}, u32[]{:S(2)}) collective-permute-start(bf16[128,1024]{1,0:T(8,128)(2,1)S(1)} %slice.9), channel_id=1, source_target_pairs={{64,16},{16,64},{80,32},{32,80},{96,48},{48,96},{112,0},{0,112},{6... | collective-permute-start | bytes 786440 | tf_op jit(solution)/shard_map/ppermute | solution.py:31

commit v2 on v1

v2 whole, which is shorter than its diff:
```python
import functools

import jax
import jax.numpy as jnp
from jax import lax
from jax.experimental import pallas as pl
from jax.experimental.pallas import tpu as pltpu
from jax.sharding import Mesh, PartitionSpec as P

BF16 = jnp.bfloat16
F32 = jnp.float32
AXES = ("x", "yl", "yh", "z", "core")
SIZES = (4, 2, 4, 8, 2)
NX, NL, NH, NZ, NC = SIZES


def place(y):
    return (y % NL) * NH + y // NL


def intra(block):
    return lax.ppermute(block, "yl", [(0, 1), (1, 0)])


def inter(block):
    ny = NL * NH
    pairs = []
    for j in range(NH):
        a, b = place(2 * j + 1), place((2 * j + 2) % ny)
        pairs += [(a, b), (b, a)]
    return lax.ppermute(block, ("yl", "yh"), pairs)


def after(value, *others):
    return lax.optimization_barrier((value, *[o[:16] for o in others]))


def dot(left, right):
    return lax.dot_general(left, right, (((1,), (1,)), ((), ())), preferred_element_type=F32)


def product_kernel(halves, unread, *refs):
    count = len(halves)
    rows_refs, pieces = refs[:2], refs[2 : 2 + 2 * count]
    out_ref, left, right, left_sem, right_sem = refs[2 + 2 * count + unread :]
    yl, core = lax.axis_index("yl"), lax.axis_index("core")
    _, nz, rows, width = rows_refs[0].shape
    part = pieces[0].shape[0]
    wide = rows // NX
    lefts = [[None, None], [None, None]]
    for which in range(2):
        for half in range(2):
            source = rows_refs[which].at[yl if half == 0 else 1 - yl]
            lefts[which][half] = pltpu.make_async_copy(
                source, left.at[which, half], left_sem.at[which, half]
            )
    rights = []
    for i in range(count):
        for p in range(2):
            rights.append(
                pltpu.make_async_copy(
                    pieces[2 * i + p], right.at[i, pl.ds(p * part, part)], right_sem.at[i, p]
                )
            )
    first = halves[0]
    lefts[0][first].start()
    rights[0].start()
    rights[1].start()
    lefts[0][1 - first].start()
    for copy in rights[2:4]:
        copy.start()
    lefts[1][first].start()
    lefts[1][1 - first].start()
    for copy in rights[4:]:
        copy.start()
    for which in range(2):
        target_core = core if which == 0 else 1 - core
        done = []
        for slot in range(count // 2):
            total = None
            for i in (2 * slot, 2 * slot + 1):
                if which == 0:
                    rights[2 * i].wait()
                    rights[2 * i + 1].wait()
                if slot == 0:
                    lefts[which][halves[i]].wait()
                term = dot(left[which, halves[i]].reshape(nz * rows, width), right[i])
                total = term if total is None else total + term
            done.append(total)
        for zi in range(nz):
            for xi in range(NX):
                at = zi * rows + xi * wide
                block = jnp.concatenate([d[at : at + wide] for d in done], axis=0)
                out_ref[(xi * nz + zi) * NC + target_core] = block.astype(BF16)


def product(mine, other, blocks, halves, unread):
    _, nz, rows, width = mine.shape
    wide = rows // NX
    columns = 2 * blocks[0][0].shape[0]
    count = len(blocks)
    members = NX * nz * NC
    flops = 2 * 2 * nz * rows * width * columns * count
    anywhere = pl.BlockSpec(memory_space=pltpu.HBM)
    return pl.pallas_call(
        functools.partial(product_kernel, halves, len(unread)),
        out_shape=jax.ShapeDtypeStruct((members, count // 2 * wide, columns), BF16),
        in_specs=[anywhere] * (2 + 2 * count + len(unread)),
        out_specs=pl.BlockSpec(memory_space=pltpu.VMEM),
        scratch_shapes=[
            pltpu.VMEM((2, 2, nz, rows, width), BF16),
            pltpu.VMEM((count, columns, width), BF16),
            pltpu.SemaphoreType.DMA((2, 2)),
            pltpu.SemaphoreType.DMA((count, 2)),
        ],
        compiler_params=pltpu.CompilerParams(vmem_limit_bytes=60 * 1024 * 1024),
        cost_estimate=pl.CostEstimate(flops=flops, bytes_accessed=5 * 2**20, transcendentals=0),
    )(mine, other, *[piece for block in blocks for piece in block], *unread)


def finish_kernel(terms_ref, out_ref):
    yh = lax.axis_index("yh")
    step = 1 - 2 * lax.axis_index("yl")
    total = terms_ref[0].astype(F32)
    for xi in range(1, NX):
        total = total + terms_ref[xi].astype(F32)
    wide = total.shape[1] // NH
    for slot, offset in enumerate((0, -step, step, 2)):
        out_ref[lax.rem(yh + NH + offset, NH)] = total[:, slot * wide : (slot + 1) * wide]


def finish(terms):
    members, tall, columns = terms.shape
    rest = members // NX
    terms = terms.reshape(NX, rest, tall, columns)
    step = rest // 2
    return pl.pallas_call(
        finish_kernel,
        grid=(rest // step,),
        out_shape=jax.ShapeDtypeStruct((NH, rest, tall // NH, columns), F32),
        in_specs=[pl.BlockSpec((NX, step, tall, columns), lambda i: (0, i, 0, 0))],
        out_specs=pl.BlockSpec((NH, step, tall // NH, columns), lambda i: (0, i, 0, 0)),
        cost_estimate=pl.CostEstimate(flops=2**19, bytes_accessed=3 * 2**19, transcendentals=0),
    )(terms)


def body(valence_pairs, conduction_pairs, screening):
    _, second, plane_dev = valence_pairs.shape
    own = conduction_pairs[0]
    cut = own.shape[0] // 2
    own_a, own_b = own[:cut], own[cut:]

    f1a, b1a = intra(own_a), inter(own_a)
    f1b, b1b = intra(own_b), inter(own_b)

    screened = (valence_pairs[0].astype(F32) * screening[None, :]).astype(BF16)
    wide = second // (NX * NL)
    by_half = screened.reshape(NX, NL, wide, plane_dev).transpose(1, 0, 2, 3)
    by_half = by_half.reshape(NL, 1, NX * wide, plane_dev)
    sent = jnp.broadcast_to(by_half, (NL, NZ, NX * wide, plane_dev))
    sent = sent.reshape(NL * NZ, NX * wide, plane_dev)
    mine = lax.all_to_all(sent, ("yl", "z"), 0, 0, tiled=True)

    f2a, b2a = intra(b1a), inter(f1a)
    f2b, b2b = intra(b1b), inter(f1b)
    f3a, b3a = intra(b2a), inter(f2a)
    f3b, b3b = intra(b2b), inter(f2b)
    f4a, b4b = intra(b3a), inter(f3b)

    mine, *rows = after(mine, f3a, b3a, f3b, b3b)
    other = lax.ppermute(mine, "core", [(0, 1), (1, 0)])
    mine = mine.reshape(NL, NZ, NX * wide, plane_dev)
    other = other.reshape(NL, NZ, NX * wide, plane_dev)

    terms = product(
        mine,
        other,
        (
            (own_a, own_b), (f1a, f1b), (b1a, b1b), (b2a, b2b),
            (f2a, f2b), (f3a, f3b), (b3a, b3b), (f4a, b4b),
        ),
        (0, 1, 1, 0, 0, 1, 1, 0),
        rows,
    )
    terms = lax.all_to_all(terms, ("x", "z", "core"), 0, 0, tiled=True)
    out = finish(terms)
    return out.reshape(1, NH * NZ * NC, wide, own.shape[0])


def solution(mesh):
    fine = Mesh(mesh.devices.reshape(SIZES), AXES)
    pair, pw = ("yh", "z", "core"), ("x", "yl")
    placed = (P(pair, None, pw), P(pair, None, pw), P(pw))
    return jax.shard_map(
        body, mesh=fine, in_specs=placed, out_specs=P(pair, None, pw, None), check_vma=False
    )
```

time: 141 us -> 133 us (0.943)
  waiting for transfers between devices: 42.9 us -> 13.5 us
  blocking collectives: 26.2 us -> 39.2 us
  starting transfers between devices: 55.6 us -> 63.4 us
  local copies, waits for them, and re-layouts: 6.88 us -> 4.88 us
  Pallas kernels: 8 us -> 9.96 us
    ppermute x4 -> x7, waiting for transfers between devices: 23.3 us -> 5.81 us  [intra(): return lax.ppermute(block, 'yl', [(0, 1), (1, 0)])]
    all_to_all x1, blocking collectives: 26.2 us -> 39.2 us  [body(): terms = lax.all_to_all(terms, ('x', 'z', 'core'), 0, 0, tiled=True)]
    ppermute x4 -> x7, starting transfers between devices: 18.5 us -> 29.5 us  [inter(): return lax.ppermute(block, ('yl', 'yh'), pairs)]
    all_to_all x1 -> x0, starting transfers between devices: 10.5 us -> none  [body(): first = lax.all_to_all(first, ('x', 'z', 'core'), 0, 0, tiled=True)]
    ppermute x4 -> x7, waiting for transfers between devices: 16.9 us -> 7.69 us  [inter(): return lax.ppermute(block, ('yl', 'yh'), pairs)]
    ppermute x4 -> x7, starting transfers between devices: 8.48 us -> 15.7 us  [intra(): return lax.ppermute(block, 'yl', [(0, 1), (1, 0)])]
    unnamed x20 -> x38, local copies, waits for them, and re-layouts: 5.72 us -> 1.08 us
    pallas_call x2 -> x1, Pallas kernels: 4.66 us -> 7.99 us  [product(): pl.pallas_call(functools.partial(product_kernel, halves, len(unread)), ou...]
  transfers between devices with their start and end apart: 11 -> 16, of which waited for: 9 -> 6; matrix products, arithmetic and copies ran while one was open for 0% -> 2% of each run, Pallas kernels for 1% -> 0%
where the time goes in v2:
time: 133 us; the launch traced here: 132 us
  starting transfers between devices  63.4 us (48%)
  blocking collectives  39.2 us (29%)
  waiting for transfers between devices  13.5 us (10%)
  Pallas kernels  9.96 us (7%)
  local copies, waits for them, and re-layouts  4.88 us (4%)
    all_to_all x1, blocking collectives, body(): terms = lax.all_to_all(terms, ('x', 'z', 'core'), 0, 0, tiled=True)  39.2 us
    ppermute x7, starting transfers between devices, inter(): return lax.ppermute(block, ('yl', 'yh'), pairs)  29.5 us
    ppermute x7, starting transfers between devices, intra(): return lax.ppermute(block, 'yl', [(0, 1), (1, 0)])  15.7 us
    all_to_all x1, starting transfers between devices, body(): mine = lax.all_to_all(sent, ('yl', 'z'), 0, 0, tiled=True)  12.1 us
    pallas_call x1, Pallas kernels, product(): pl.pallas_call(functools.partial(product_kernel, halves, len(unread)), ou...  7.99 us
    ppermute x7, waiting for transfers between devices, inter(): return lax.ppermute(block, ('yl', 'yh'), pairs)  7.69 us
    ppermute x1, starting transfers between devices, body(): other = lax.ppermute(mine, 'core', [(0, 1), (1, 0)])  6.07 us
    ppermute x7, waiting for transfers between devices, intra(): return lax.ppermute(block, 'yl', [(0, 1), (1, 0)])  5.81 us
  transfers between devices with their start and end apart: 16, of which 6 were waited for; matrix products, arithmetic and copies ran while one was open for 2% of the time, Pallas kernels for 0%

profile of v2, /device:TPU:1, one launch (start us, length us, event | category | flops | bytes accessed | tf_op | source)
XLA Modules:
  0.0 132.2 jit_solution(2563620592187786541)
XLA Ops:
  2.0 12.1 %all-to-all-start = ((bf16[16,32,1024]{2,1,0:T(8,128)(2,1)}), bf16[16,32,1024]{2,1,0:T(8,128)(2,1)S(1)}, u32[]{:S(2)}, u32[]{:S(2)}) async-start(bf16[16,32,1024]{2,1,0:T(8,128)(2,1)} %bitcast.3), calls=%async_computation | async-start | bytes 2097152 | tf_op jit(solution)/shard_map/all_to_all | solution.py:162
  14.2 5.2 %collective-permute-start.9 = (bf16[128,1024]{1,0:T(8,128)(2,1)S(1)}, bf16[128,1024]{1,0:T(8,128)(2,1)S(1)}, u32[]{:S(2)}, u32[]{:S(2)}) collective-permute-start(bf16[128,1024]{1,0:T(8,128)(2,1)S(1)} %get-tuple-element.15.refs_3_), channel_id=1, source_target_pairs={{64,16},{16,64},{80,32},{32,80},{96,48},{48,96},{112,0},{0,112},{6... | collective-permute-start | bytes 786440 | tf_op jit(solution)/shard_map/ppermute | solution.py:31
  19.4 1.9 %collective-permute-start.6 = (bf16[128,1024]{1,0:T(8,128)(2,1)S(1)}, bf16[128,1024]{1,0:T(8,128)(2,1)S(1)}, u32[]{:S(2)}, u32[]{:S(2)}) collective-permute-start(bf16[128,1024]{1,0:T(8,128)(2,1)S(1)} %get-tuple-element.15.refs_3_), channel_id=1, source_target_pairs={{0,64},{64,0},{1,65},{65,1},{2,66},{66,2},{3,67},{67,3},{4,68},{68... | collective-permute-start | bytes 786440 | tf_op jit(solution)/shard_map/ppermute | solution.py:22
  21.3 4.0 %collective-permute-start.3 = (bf16[128,1024]{1,0:T(8,128)(2,1)S(1)}, bf16[128,1024]{1,0:T(8,128)(2,1)S(1)}, u32[]{:S(2)}, u32[]{:S(2)}) collective-permute-start(bf16[128,1024]{1,0:T(8,128)(2,1)S(1)} %get-tuple-element.16.refs_2_), channel_id=1, source_target_pairs={{64,16},{16,64},{80,32},{32,80},{96,48},{48,96},{112,0},{0,112},{6... | collective-permute-start | bytes 786440 | tf_op jit(solution)/shard_map/ppermute | solution.py:31
  25.4 2.0 %collective-permute-start = (bf16[128,1024]{1,0:T(8,128)(2,1)S(1)}, bf16[128,1024]{1,0:T(8,128)(2,1)S(1)}, u32[]{:S(2)}, u32[]{:S(2)}) collective-permute-start(bf16[128,1024]{1,0:T(8,128)(2,1)S(1)} %get-tuple-element.16.refs_2_), channel_id=1, source_target_pairs={{0,64},{64,0},{1,65},{65,1},{2,66},{66,2},{3,67},{67,3},{4,68},{68... | collective-permute-start | bytes 786440 | tf_op jit(solution)/shard_map/ppermute | solution.py:22
  27.4 3.3 %collective-permute-start.10 = (bf16[128,1024]{1,0:T(8,128)(2,1)S(1)}, bf16[128,1024]{1,0:T(8,128)(2,1)S(1)}, u32[]{:S(2)}, u32[]{:S(2)}) collective-permute-start(bf16[128,1024]{1,0:T(8,128)(2,1)S(1)} %collective-permute-done.9.refs_7_), channel_id=1, source_target_pairs={{0,64},{64,0},{1,65},{65,1},{2,66},{66,2},{3,67},{67,3},{4,68},{68... | collective-permute-start | bytes 786440 | tf_op jit(solution)/shard_map/ppermute | solution.py:22
  30.7 2.5 %collective-permute-done.6.refs_5_ = bf16[128,1024]{1,0:T(8,128)(2,1)S(1)} collective-permute-done((bf16[128,1024]{1,0:T(8,128)(2,1)S(1)}, bf16[128,1024]{1,0:T(8,128)(2,1)S(1)}, u32[]{:S(2)}, u32[]{:S(2)}) %collective-permute-start.6) | collective-permute-done | bytes 262176 | tf_op jit(solution)/shard_map/ppermute | solution.py:22
  33.2 4.6 %collective-permute-start.7 = (bf16[128,1024]{1,0:T(8,128)(2,1)S(1)}, bf16[128,1024]{1,0:T(8,128)(2,1)S(1)}, u32[]{:S(2)}, u32[]{:S(2)}) collective-permute-start(bf16[128,1024]{1,0:T(8,128)(2,1)S(1)} %collective-permute-done.6.refs_5_), channel_id=1, source_target_pairs={{64,16},{16,64},{80,32},{32,80},{96,48},{48,96},{112,0},{0,112},{6... | collective-permute-start | bytes 786440 | tf_op jit(solution)/shard_map/ppermute | solution.py:31
  37.9 1.9 %collective-permute-start.4 = (bf16[128,1024]{1,0:T(8,128)(2,1)S(1)}, bf16[128,1024]{1,0:T(8,128)(2,1)S(1)}, u32[]{:S(2)}, u32[]{:S(2)}) collective-permute-start(bf16[128,1024]{1,0:T(8,128)(2,1)S(1)} %collective-permute-done.3.refs_6_), channel_id=1, source_target_pairs={{0,64},{64,0},{1,65},{65,1},{2,66},{66,2},{3,67},{67,3},{4,68},{68... | collective-permute-start | bytes 786440 | tf_op jit(solution)/shard_map/ppermute | solution.py:22
  39.8 4.0 %collective-permute-start.1 = (bf16[128,1024]{1,0:T(8,128)(2,1)S(1)}, bf16[128,1024]{1,0:T(8,128)(2,1)S(1)}, u32[]{:S(2)}, u32[]{:S(2)}) collective-permute-start(bf16[128,1024]{1,0:T(8,128)(2,1)S(1)} %collective-permute-done.refs_4_), channel_id=1, source_target_pairs={{64,16},{16,64},{80,32},{32,80},{96,48},{48,96},{112,0},{0,112},{6... | collective-permute-start | bytes 786440 | tf_op jit(solution)/shard_map/ppermute | solution.py:31
  44.4 4.6 %collective-permute-start.11 = (bf16[128,1024]{1,0:T(8,128)(2,1)S(1)}, bf16[128,1024]{1,0:T(8,128)(2,1)S(1)}, u32[]{:S(2)}, u32[]{:S(2)}) collective-permute-start(bf16[128,1024]{1,0:T(8,128)(2,1)S(1)} %collective-permute-done.10.refs_11_), channel_id=1, source_target_pairs={{64,16},{16,64},{80,32},{32,80},{96,48},{48,96},{112,0},{0,112},{6... | collective-permute-start | bytes 786440 | tf_op jit(solution)/shard_map/ppermute | solution.py:31
  49.1 1.9 %collective-permute-start.8 = (bf16[128,1024]{1,0:T(8,128)(2,1)S(1)}, bf16[128,1024]{1,0:T(8,128)(2,1)S(1)}, u32[]{:S(2)}, u32[]{:S(2)}) collective-permute-start(bf16[128,1024]{1,0:T(8,128)(2,1)S(1)} %collective-permute-done.7.refs_9_), channel_id=1, source_target_pairs={{0,64},{64,0},{1,65},{65,1},{2,66},{66,2},{3,67},{67,3},{4,68},{68... | collective-permute-start | bytes 786440 | tf_op jit(solution)/shard_map/ppermute | solution.py:22
  51.1 4.0 %collective-permute-start.5 = (bf16[128,1024]{1,0:T(8,128)(2,1)S(1)}, bf16[128,1024]{1,0:T(8,128)(2,1)S(1)}, u32[]{:S(2)}, u32[]{:S(2)}) collective-permute-start(bf16[128,1024]{1,0:T(8,128)(2,1)S(1)} %collective-permute-done.4.refs_10_), channel_id=1, source_target_pairs={{64,16},{16,64},{80,32},{32,80},{96,48},{48,96},{112,0},{0,112},{6... | collective-permute-start | bytes 786440 | tf_op jit(solution)/shard_map/ppermute | solution.py:31
  55.1 2.5 %collective-permute-start.2 = (bf16[128,1024]{1,0:T(8,128)(2,1)S(1)}, bf16[128,1024]{1,0:T(8,128)(2,1)S(1)}, u32[]{:S(2)}, u32[]{:S(2)}) collective-permute-start(bf16[128,1024]{1,0:T(8,128)(2,1)S(1)} %collective-permute-done.1.refs_8_), channel_id=1, source_target_pairs={{0,64},{64,0},{1,65},{65,1},{2,66},{66,2},{3,67},{67,3},{4,68},{68... | collective-permute-start | bytes 786440 | tf_op jit(solution)/shard_map/ppermute | solution.py:22
  59.0 1.7 %collective-permute-done.5.refs_14_ = bf16[128,1024]{1,0:T(8,128)(2,1)S(1)} collective-permute-done((bf16[128,1024]{1,0:T(8,128)(2,1)S(1)}, bf16[128,1024]{1,0:T(8,128)(2,1)S(1)}, u32[]{:S(2)}, u32[]{:S(2)}) %collective-permute-start.5) | collective-permute-done | bytes 262176 | tf_op jit(solution)/shard_map/ppermute | solution.py:31
  61.4 1.3 %collective-permute-done.2.refs_12_ = bf16[128,1024]{1,0:T(8,128)(2,1)S(1)} collective-permute-done((bf16[128,1024]{1,0:T(8,128)(2,1)S(1)}, bf16[128,1024]{1,0:T(8,128)(2,1)S(1)}, u32[]{:S(2)}, u32[]{:S(2)}) %collective-permute-start.2) | collective-permute-done | bytes 262176 | tf_op jit(solution)/shard_map/ppermute | solution.py:22
  63.5 6.1 %collective-permute-start.12 = (bf16[16,32,1024]{2,1,0:T(8,128)(2,1)S(1)}, bf16[16,32,1024]{2,1,0:T(8,128)(2,1)S(1)}, u32[]{:S(2)}, u32[]{:S(2)}) collective-permute-start(bf16[16,32,1024]{2,1,0:T(8,128)(2,1)S(1)} %all-to-all-done), channel_id=1, source_target_pairs={{0,1},{1,0},{2,3},{3,2},{4,5},{5,4},{6,7},{7,6},{8,9},{9,8},{10,11... | collective-permute-start | bytes 3145736 | tf_op jit(solution)/shard_map/ppermute | solution.py:171
  69.5 2.9 %collective-permute-start.14 = (bf16[128,1024]{1,0:T(8,128)(2,1)S(1)}, bf16[128,1024]{1,0:T(8,128)(2,1)S(1)}, u32[]{:S(2)}, u32[]{:S(2)}) collective-permute-start(bf16[128,1024]{1,0:T(8,128)(2,1)S(1)} %collective-permute-done.8.refs_13_), channel_id=1, source_target_pairs={{64,16},{16,64},{80,32},{32,80},{96,48},{48,96},{112,0},{0,112},{6... | collective-permute-start | bytes 786440 | tf_op jit(solution)/shard_map/ppermute | solution.py:31
  72.5 2.1 %collective-permute-start.13 = (bf16[128,1024]{1,0:T(8,128)(2,1)S(1)}, bf16[128,1024]{1,0:T(8,128)(2,1)S(1)}, u32[]{:S(2)}, u32[]{:S(2)}) collective-permute-start(bf16[128,1024]{1,0:T(8,128)(2,1)S(1)} %collective-permute-done.5.refs_14_), channel_id=1, source_target_pairs={{0,64},{64,0},{1,65},{65,1},{2,66},{66,2},{3,67},{67,3},{4,68},{68... | collective-permute-start | bytes 786440 | tf_op jit(solution)/shard_map/ppermute | solution.py:22
  74.6 5.9 %collective-permute-done.14.refs_17_ = bf16[128,1024]{1,0:T(8,128)(2,1)S(1)} collective-permute-done((bf16[128,1024]{1,0:T(8,128)(2,1)S(1)}, bf16[128,1024]{1,0:T(8,128)(2,1)S(1)}, u32[]{:S(2)}, u32[]{:S(2)}) %collective-permute-start.14) | collective-permute-done | bytes 262176 | tf_op jit(solution)/shard_map/ppermute | solution.py:31
  80.6 1.4 %collective-permute-done.13.refs_16_ = bf16[128,1024]{1,0:T(8,128)(2,1)S(1)} collective-permute-done((bf16[128,1024]{1,0:T(8,128)(2,1)S(1)}, bf16[128,1024]{1,0:T(8,128)(2,1)S(1)}, u32[]{:S(2)}, u32[]{:S(2)}) %collective-permute-start.13) | collective-permute-done | bytes 262176 | tf_op jit(solution)/shard_map/ppermute | solution.py:22
  83.1 8.0 %shard_map.37 = bf16[64,32,256]{2,1,0:T(8,128)(2,1)} custom-call(bf16[2,8,32,1024]{3,2,1,0:T(8,128)(2,1)} %bitcast.17, bf16[2,8,32,1024]{3,2,1,0:T(8,128)(2,1)} %bitcast.19, bf16[128,1024]{1,0:T(8,128)(2,1)} %copy-done.3, bf16[128,1024]{1,0:T(8,128)(2,1)} %copy-done.2, bf16[128,1024]{1,0:T(8,128)(2,1)} %copy-done.12, bf16[128,1024]{1,0:T(8,128)(2,1)} %copy-done.10, ...), custom_call_target="tpu_custom_call" | custom-call | flops 2147483648 | bytes 5242880 | tf_op jit(solution)/shard_map/pallas_call | solution.py:105
  91.1 39.2 %all_to_all.10 = bf16[64,32,256]{2,1,0:T(8,128)(2,1)} all-to-all(bf16[64,32,256]{2,1,0:T(8,128)(2,1)} %shard_map.37), channel_id=1, replica_groups=mesh['x'=4,'yl'=2,'yh'=4,'z'=8,'core'=2] {'x','z','core'}, dimensions={0} | all-to-all | bytes 2097152 | tf_op jit(solution)/shard_map/all_to_all | solution.py:185
  130.3 2.0 %shard_map.38 = f32[4,16,8,256]{3,2,1,0:T(8,128)} custom-call(bf16[4,16,32,256]{3,2,1,0:T(8,128)(2,1)} %bitcast.16), custom_call_target="tpu_custom_call" | custom-call | flops 524288 | bytes 1572864 | tf_op jit(solution)/shard_map/pallas_call | solution.py:137
  (56 shorter events, 6.4 us)
Async XLA Ops:
  2.0 61.4 %all-to-all-start = ((bf16[16,32,1024]{2,1,0:T(8,128)(2,1)}), bf16[16,32,1024]{2,1,0:T(8,128)(2,1)S(1)}, u32[]{:S(2)}, u32[]{:S(2)}) async-start(bf16[16,32,1024]{2,1,0:T(8,128)(2,1)} %bitcast.3), calls=%async_computation | async-start | bytes 2097152 | tf_op jit(solution)/shard_map/all_to_all | solution.py:162
  14.2 68.8 %copy-start.2 = (bf16[128,1024]{1,0:T(8,128)(2,1)}, bf16[128,1024]{1,0:T(8,128)(2,1)S(1)}, u32[]{:S(2)}) copy-start(bf16[128,1024]{1,0:T(8,128)(2,1)S(1)} %get-tuple-element.15.refs_3_) | copy-start | bytes 786436
  14.2 68.8 %copy-start.3 = (bf16[128,1024]{1,0:T(8,128)(2,1)}, bf16[128,1024]{1,0:T(8,128)(2,1)S(1)}, u32[]{:S(2)}) copy-start(bf16[128,1024]{1,0:T(8,128)(2,1)S(1)} %get-tuple-element.16.refs_2_) | copy-start | bytes 786436
  14.2 13.2 %collective-permute-start.9 = (bf16[128,1024]{1,0:T(8,128)(2,1)S(1)}, bf16[128,1024]{1,0:T(8,128)(2,1)S(1)}, u32[]{:S(2)}, u32[]{:S(2)}) collective-permute-start(bf16[128,1024]{1,0:T(8,128)(2,1)S(1)} %get-tuple-element.15.refs_3_), channel_id=1, source_target_pairs={{64,16},{16,64},{80,32},{32,80},{96,48},{48,96},{112,0},{0,112},{6... | collective-permute-start | bytes 786440 | tf_op jit(solution)/shard_map/ppermute | solution.py:31
  19.4 13.8 %collective-permute-start.6 = (bf16[128,1024]{1,0:T(8,128)(2,1)S(1)}, bf16[128,1024]{1,0:T(8,128)(2,1)S(1)}, u32[]{:S(2)}, u32[]{:S(2)}) collective-permute-start(bf16[128,1024]{1,0:T(8,128)(2,1)S(1)} %get-tuple-element.15.refs_3_), channel_id=1, source_target_pairs={{0,64},{64,0},{1,65},{65,1},{2,66},{66,2},{3,67},{67,3},{4,68},{68... | collective-permute-start | bytes 786440 | tf_op jit(solution)/shard_map/ppermute | solution.py:22
  21.3 16.5 %collective-permute-start.3 = (bf16[128,1024]{1,0:T(8,128)(2,1)S(1)}, bf16[128,1024]{1,0:T(8,128)(2,1)S(1)}, u32[]{:S(2)}, u32[]{:S(2)}) collective-permute-start(bf16[128,1024]{1,0:T(8,128)(2,1)S(1)} %get-tuple-element.16.refs_2_), channel_id=1, source_target_pairs={{64,16},{16,64},{80,32},{32,80},{96,48},{48,96},{112,0},{0,112},{6... | collective-permute-start | bytes 786440 | tf_op jit(solution)/shard_map/ppermute | solution.py:31
  25.4 14.4 %collective-permute-start = (bf16[128,1024]{1,0:T(8,128)(2,1)S(1)}, bf16[128,1024]{1,0:T(8,128)(2,1)S(1)}, u32[]{:S(2)}, u32[]{:S(2)}) collective-permute-start(bf16[128,1024]{1,0:T(8,128)(2,1)S(1)} %get-tuple-element.16.refs_2_), channel_id=1, source_target_pairs={{0,64},{64,0},{1,65},{65,1},{2,66},{66,2},{3,67},{67,3},{4,68},{68... | collective-permute-start | bytes 786440 | tf_op jit(solution)/shard_map/ppermute | solution.py:22
  27.4 55.6 %copy-start.9 = (bf16[128,1024]{1,0:T(8,128)(2,1)}, bf16[128,1024]{1,0:T(8,128)(2,1)S(1)}, u32[]{:S(2)}) copy-start(bf16[128,1024]{1,0:T(8,128)(2,1)S(1)} %collective-permute-done.9.refs_7_) | copy-start | bytes 786436
  27.4 17.0 %collective-permute-start.10 = (bf16[128,1024]{1,0:T(8,128)(2,1)S(1)}, bf16[128,1024]{1,0:T(8,128)(2,1)S(1)}, u32[]{:S(2)}, u32[]{:S(2)}) collective-permute-start(bf16[128,1024]{1,0:T(8,128)(2,1)S(1)} %collective-permute-done.9.refs_7_), channel_id=1, source_target_pairs={{0,64},{64,0},{1,65},{65,1},{2,66},{66,2},{3,67},{67,3},{4,68},{68... | collective-permute-start | bytes 786440 | tf_op jit(solution)/shard_map/ppermute | solution.py:22
  33.2 49.8 %copy-start.10 = (bf16[128,1024]{1,0:T(8,128)(2,1)}, bf16[128,1024]{1,0:T(8,128)(2,1)S(1)}, u32[]{:S(2)}) copy-start(bf16[128,1024]{1,0:T(8,128)(2,1)S(1)} %collective-permute-done.6.refs_5_) | copy-start | bytes 786436
  33.2 15.9 %collective-permute-start.7 = (bf16[128,1024]{1,0:T(8,128)(2,1)S(1)}, bf16[128,1024]{1,0:T(8,128)(2,1)S(1)}, u32[]{:S(2)}, u32[]{:S(2)}) collective-permute-start(bf16[128,1024]{1,0:T(8,128)(2,1)S(1)} %collective-permute-done.6.refs_5_), channel_id=1, source_target_pairs={{64,16},{16,64},{80,32},{32,80},{96,48},{48,96},{112,0},{0,112},{6... | collective-permute-start | bytes 786440 | tf_op jit(solution)/shard_map/ppermute | solution.py:31
  37.9 45.1 %copy-start.11 = (bf16[128,1024]{1,0:T(8,128)(2,1)}, bf16[128,1024]{1,0:T(8,128)(2,1)S(1)}, u32[]{:S(2)}) copy-start(bf16[128,1024]{1,0:T(8,128)(2,1)S(1)} %collective-permute-done.3.refs_6_) | copy-start | bytes 786436
  37.9 13.2 %collective-permute-start.4 = (bf16[128,1024]{1,0:T(8,128)(2,1)S(1)}, bf16[128,1024]{1,0:T(8,128)(2,1)S(1)}, u32[]{:S(2)}, u32[]{:S(2)}) collective-permute-start(bf16[128,1024]{1,0:T(8,128)(2,1)S(1)} %collective-permute-done.3.refs_6_), channel_id=1, source_target_pairs={{0,64},{64,0},{1,65},{65,1},{2,66},{66,2},{3,67},{67,3},{4,68},{68... | collective-permute-start | bytes 786440 | tf_op jit(solution)/shard_map/ppermute | solution.py:22
  39.8 15.3 %collective-permute-start.1 = (bf16[128,1024]{1,0:T(8,128)(2,1)S(1)}, bf16[128,1024]{1,0:T(8,128)(2,1)S(1)}, u32[]{:S(2)}, u32[]{:S(2)}) collective-permute-start(bf16[128,1024]{1,0:T(8,128)(2,1)S(1)} %collective-permute-done.refs_4_), channel_id=1, source_target_pairs={{64,16},{16,64},{80,32},{32,80},{96,48},{48,96},{112,0},{0,112},{6... | collective-permute-start | bytes 786440 | tf_op jit(solution)/shard_map/ppermute | solution.py:31
  44.4 13.2 %collective-permute-start.11 = (bf16[128,1024]{1,0:T(8,128)(2,1)S(1)}, bf16[128,1024]{1,0:T(8,128)(2,1)S(1)}, u32[]{:S(2)}, u32[]{:S(2)}) collective-permute-start(bf16[128,1024]{1,0:T(8,128)(2,1)S(1)} %collective-permute-done.10.refs_11_), channel_id=1, source_target_pairs={{64,16},{16,64},{80,32},{32,80},{96,48},{48,96},{112,0},{0,112},{6... | collective-permute-start | bytes 786440 | tf_op jit(solution)/shard_map/ppermute | solution.py:31
  49.1 9.2 %collective-permute-start.8 = (bf16[128,1024]{1,0:T(8,128)(2,1)S(1)}, bf16[128,1024]{1,0:T(8,128)(2,1)S(1)}, u32[]{:S(2)}, u32[]{:S(2)}) collective-permute-start(bf16[128,1024]{1,0:T(8,128)(2,1)S(1)} %collective-permute-done.7.refs_9_), channel_id=1, source_target_pairs={{0,64},{64,0},{1,65},{65,1},{2,66},{66,2},{3,67},{67,3},{4,68},{68... | collective-permute-start | bytes 786440 | tf_op jit(solution)/shard_map/ppermute | solution.py:22
  51.1 9.7 %collective-permute-start.5 = (bf16[128,1024]{1,0:T(8,128)(2,1)S(1)}, bf16[128,1024]{1,0:T(8,128)(2,1)S(1)}, u32[]{:S(2)}, u32[]{:S(2)}) collective-permute-start(bf16[128,1024]{1,0:T(8,128)(2,1)S(1)} %collective-permute-done.4.refs_10_), channel_id=1, source_target_pairs={{64,16},{16,64},{80,32},{32,80},{96,48},{48,96},{112,0},{0,112},{6... | collective-permute-start | bytes 786440 | tf_op jit(solution)/shard_map/ppermute | solution.py:31
  55.1 7.6 %collective-permute-start.2 = (bf16[128,1024]{1,0:T(8,128)(2,1)S(1)}, bf16[128,1024]{1,0:T(8,128)(2,1)S(1)}, u32[]{:S(2)}, u32[]{:S(2)}) collective-permute-start(bf16[128,1024]{1,0:T(8,128)(2,1)S(1)} %collective-permute-done.1.refs_8_), channel_id=1, source_target_pairs={{0,64},{64,0},{1,65},{65,1},{2,66},{66,2},{3,67},{67,3},{4,68},{68... | collective-permute-start | bytes 786440 | tf_op jit(solution)/shard_map/ppermute | solution.py:22
  57.7 25.3 %copy-start.4 = (bf16[128,1024]{1,0:T(8,128)(2,1)}, bf16[128,1024]{1,0:T(8,128)(2,1)S(1)}, u32[]{:S(2)}) copy-start(bf16[128,1024]{1,0:T(8,128)(2,1)S(1)} %collective-permute-done.11.refs_15_) | copy-start | bytes 786436
  58.4 24.7 %copy-start.5 = (bf16[128,1024]{1,0:T(8,128)(2,1)}, bf16[128,1024]{1,0:T(8,128)(2,1)S(1)}, u32[]{:S(2)}) copy-start(bf16[128,1024]{1,0:T(8,128)(2,1)S(1)} %collective-permute-done.8.refs_13_) | copy-start | bytes 786436
  60.8 22.3 %copy-start.6 = (bf16[128,1024]{1,0:T(8,128)(2,1)}, bf16[128,1024]{1,0:T(8,128)(2,1)S(1)}, u32[]{:S(2)}) copy-start(bf16[128,1024]{1,0:T(8,128)(2,1)S(1)} %collective-permute-done.5.refs_14_) | copy-start | bytes 786436
  63.5 18.5 %collective-permute-start.12 = (bf16[16,32,1024]{2,1,0:T(8,128)(2,1)S(1)}, bf16[16,32,1024]{2,1,0:T(8,128)(2,1)S(1)}, u32[]{:S(2)}, u32[]{:S(2)}) collective-permute-start(bf16[16,32,1024]{2,1,0:T(8,128)(2,1)S(1)} %all-to-all-done), channel_id=1, source_target_pairs={{0,1},{1,0},{2,3},{3,2},{4,5},{5,4},{6,7},{7,6},{8,9},{9,8},{10,11... | collective-permute-start | bytes 3145736 | tf_op jit(solution)/shard_map/ppermute | solution.py:171
  69.5 11.0 %collective-permute-start.14 = (bf16[128,1024]{1,0:T(8,128)(2,1)S(1)}, bf16[128,1024]{1,0:T(8,128)(2,1)S(1)}, u32[]{:S(2)}, u32[]{:S(2)}) collective-permute-start(bf16[128,1024]{1,0:T(8,128)(2,1)S(1)} %collective-permute-done.8.refs_13_), channel_id=1, source_target_pairs={{64,16},{16,64},{80,32},{32,80},{96,48},{48,96},{112,0},{0,112},{6... | collective-permute-start | bytes 786440 | tf_op jit(solution)/shard_map/ppermute | solution.py:31
  72.5 9.5 %collective-permute-start.13 = (bf16[128,1024]{1,0:T(8,128)(2,1)S(1)}, bf16[128,1024]{1,0:T(8,128)(2,1)S(1)}, u32[]{:S(2)}, u32[]{:S(2)}) collective-permute-start(bf16[128,1024]{1,0:T(8,128)(2,1)S(1)} %collective-permute-done.5.refs_14_), channel_id=1, source_target_pairs={{0,64},{64,0},{1,65},{65,1},{2,66},{66,2},{3,67},{67,3},{4,68},{68... | collective-permute-start | bytes 786440 | tf_op jit(solution)/shard_map/ppermute | solution.py:22
  (11 other events, 115.6 us)

commit v3 on v0

v3 whole, which is shorter than its diff:
```python
import functools

import jax
import jax.numpy as jnp
from jax import lax
from jax.experimental import pallas as pl
from jax.experimental.pallas import tpu as pltpu
from jax.sharding import Mesh, PartitionSpec as P

BF16 = jnp.bfloat16
F32 = jnp.float32
AXES = ("x", "yl", "yh", "z", "core")
SIZES = (4, 2, 4, 8, 2)
NX, NL, NH, NZ, NC = SIZES
NQ = NX * NL
LANES = 128
MIB = 2**20


def along(block, step):
    return lax.ppermute(block, "yh", [(i, (i + step) % NH) for i in range(NH)])


def dot(left, right):
    return lax.dot_general(left, right, (((1,), (1,)), ((), ())), preferred_element_type=F32)


def product_kernel(cuts, unread, begun, at_row, *refs):
    count, pieces = len(cuts), sum(cuts)
    rows_refs, piece_refs = refs[:2], refs[2 : 2 + pieces]
    out_ref, left, right, held, left_sem, right_sem, out_sem = refs[2 + pieces + unread + begun :]
    core = lax.axis_index("core")
    nz, rows, width = rows_refs[0].shape
    wide = rows // NQ
    lefts = [
        pltpu.make_async_copy(rows_refs[i], left.at[i], left_sem.at[i]) for i in range(2)
    ]
    rights, at = [], 0
    for i, cut in enumerate(cuts):
        group = []
        part = right.shape[1] // cut
        for p in range(cut):
            group.append(
                pltpu.make_async_copy(
                    piece_refs[at], right.at[i, pl.ds(p * part, part)], right_sem.at[at]
                )
            )
            at += 1
        rights.append(group)
    lefts[0].start()
    for copy in rights[0]:
        copy.start()
    lefts[1].start()
    for group in rights[1:]:
        for copy in group:
            copy.start()
    for which in range(2):
        lefts[which].wait()
        target_core = core if which == 0 else 1 - core
        whole = left[which].reshape(nz * rows, width)
        done = []
        for i in range(count):
            if which == 0:
                for copy in rights[i]:
                    copy.wait()
            term = dot(whole, right[i])
            done += [term[:, c : c + LANES] for c in range(0, term.shape[1], LANES)]
        for zi in range(nz):
            for qi in range(NQ):
                at = zi * rows + qi * wide
                block = jnp.concatenate([d[at : at + wide] for d in done], axis=0)
                held[qi, zi * NC + target_core] = block.astype(BF16)
    tall = held.shape[2]
    copy = pltpu.make_async_copy(held, out_ref.at[:, :, pl.ds(at_row, tall)], out_sem)
    copy.start()
    copy.wait()


def product(mine, other, blocks, at_row, height, unread=(), begun=None):
    nz, rows, width = mine.shape
    wide = rows // NQ
    cuts = tuple(len(block) for block in blocks)
    columns = cuts[0] * blocks[0][0].shape[0]
    count = len(blocks)
    tall = count * columns // LANES * wide
    flops = 2 * 2 * nz * rows * width * columns * count
    anywhere = pl.BlockSpec(memory_space=pltpu.HBM)
    operands = [mine, other, *[piece for block in blocks for piece in block], *unread]
    aliases = {}
    if begun is not None:
        aliases = {len(operands): 0}
        operands.append(begun)
    return pl.pallas_call(
        functools.partial(product_kernel, cuts, len(unread), len(aliases), at_row),
        out_shape=jax.ShapeDtypeStruct((NQ, nz * NC, height, LANES), BF16),
        in_specs=[anywhere] * len(operands),
        out_specs=anywhere,
        scratch_shapes=[
            pltpu.VMEM((2, nz, rows, width), BF16),
            pltpu.VMEM((count, columns, width), BF16),
            pltpu.VMEM((NQ, nz * NC, tall, LANES), BF16),
            pltpu.SemaphoreType.DMA((2,)),
            pltpu.SemaphoreType.DMA((sum(cuts),)),
            pltpu.SemaphoreType.DMA,
        ],
        input_output_aliases=aliases,
        compiler_params=pltpu.CompilerParams(vmem_limit_bytes=40 * MIB),
        cost_estimate=pl.CostEstimate(flops=flops, bytes_accessed=5 * MIB, transcendentals=0),
    )(*operands)


def add_kernel(*refs):
    out_ref, at = refs[-1], 0
    for ref in refs[:-1]:
        total = ref[0].astype(F32)
        for qi in range(1, NQ):
            total = total + ref[qi].astype(F32)
        tall = total.shape[1]
        out_ref[:, at : at + tall] = total.astype(BF16)
        at += tall


def add(*terms):
    rest = terms[0].shape[1]
    tall = sum(t.shape[2] for t in terms)
    step = rest // 4
    return pl.pallas_call(
        add_kernel,
        grid=(rest // step,),
        out_shape=jax.ShapeDtypeStruct((rest, tall, LANES), BF16),
        in_specs=[
            pl.BlockSpec((NQ, step, t.shape[2], LANES), lambda i: (0, i, 0, 0)) for t in terms
        ],
        out_specs=pl.BlockSpec((step, tall, LANES), lambda i: (i, 0, 0)),
        cost_estimate=pl.CostEstimate(flops=MIB, bytes_accessed=2 * MIB, transcendentals=0),
    )(*terms)


def finish_kernel(terms_ref, out_ref):
    yh = lax.axis_index("yh")
    wide, columns = out_ref.shape[2:]
    values = terms_ref[...].astype(F32)
    at = 0
    for offset in (0, NH - 1, 1, 2):
        owner = lax.rem(yh + offset, NH)
        for c in range(0, columns, LANES):
            out_ref[owner, :, :, c : c + LANES] = values[:, at : at + wide]
            at += wide


def finish(terms, columns):
    rest, tall, _ = terms.shape
    wide = tall * LANES // columns // NH
    step = rest // 2
    return pl.pallas_call(
        finish_kernel,
        grid=(rest // step,),
        out_shape=jax.ShapeDtypeStruct((NH, rest, wide, columns), F32),
        in_specs=[pl.BlockSpec((step, tall, LANES), lambda i: (i, 0, 0))],
        out_specs=pl.BlockSpec((NH, step, wide, columns), lambda i: (0, i, 0, 0)),
        cost_estimate=pl.CostEstimate(flops=2**17, bytes_accessed=MIB, transcendentals=0),
    )(terms)


def body(valence_pairs, conduction_pairs, screening):
    _, second, plane_dev = valence_pairs.shape
    own = conduction_pairs[0]
    columns = own.shape[0]
    cut = columns // 2

    ahead, back = along(own, 1), along(own, NH - 1)

    screened = (valence_pairs[0].astype(F32) * screening[None, :]).astype(BF16)
    sent = jnp.broadcast_to(screened[None], (NZ, second, plane_dev))
    mine = lax.all_to_all(sent, "z", 0, 0, tiled=True)
    mine, *rows = lax.optimization_barrier((mine, ahead[:16], back[:16]))
    other = lax.ppermute(mine, "core", [(0, 1), (1, 0)])

    far = along(ahead[:cut], 1), along(back[cut:], NH - 1)

    height = NH * columns // LANES * (second // NQ)
    most = (NH - 1) * columns // LANES * (second // NQ)
    terms = product(mine, other, ((own,), (ahead,), (back,)), 0, height, rows)
    terms = product(mine, other, (far,), most, height, (), terms)
    terms = lax.all_to_all(terms, ("x", "yl"), 0, 0, tiled=True)
    terms = lax.all_to_all(add(terms), ("z", "core"), 0, 0, tiled=True)
    out = finish(terms, columns)
    return out.reshape(1, NH * NZ * NC, second // NQ, columns)


def solution(mesh):
    fine = Mesh(mesh.devices.reshape(SIZES), AXES)
    pair, pw = ("yh", "z", "core"), ("x", "yl")
    placed = (P(pair, None, pw), P(pair, None, pw), P(pw))
    return jax.shard_map(
        body, mesh=fine, in_specs=placed, out_specs=P(pair, None, pw, None), check_vma=False
    )
```

time: 218 us -> 127 us (0.58)
  waiting for transfers between devices: 113 us -> 27 us
  starting transfers between devices: 0.01 us -> 28.9 us
  blocking collectives: 80.3 us -> 57.1 us
  between operations: 13.4 us -> 0.1 us
  Pallas kernels: 0 us -> 11.1 us
  matrix products: 5.75 us -> 0 us
  other arithmetic: 4.16 us -> 0.99 us
    all_gather x1 -> x0, waiting for transfers between devices: 113 us -> none  [body(): lax.all_gather(screened, 'pair', axis=0, tiled=True)]
    ppermute x0 -> x5, waiting for transfers between devices: none -> 26.4 us  [the longest x4 26.4 us: along(): return lax.ppermute(block, 'yh', [(i, (i + step) % NH) for i in range(NH)])]
    all_to_all x2, blocking collectives: 80.3 us -> 57.1 us  [the longest x1 37.3 us: body(): terms = lax.all_to_all(terms, ('x', 'yl'), 0, 0, tiled=True)]
    ppermute x0 -> x5, starting transfers between devices: none -> 18 us  [the longest x4 15.6 us: along(): return lax.ppermute(block, 'yh', [(i, (i + step) % NH) for i in range(NH)])]
    pallas_call x0 -> x4, Pallas kernels: none -> 11.1 us  [the longest x2 5.9 us: product(): pl.pallas_call(functools.partial(product_kernel, cuts, len(unread), len(a...]
    all_to_all x0 -> x1, starting transfers between devices: none -> 10.9 us  [body(): mine = lax.all_to_all(sent, 'z', 0, 0, tiled=True)]
    dot_general x1 -> x0, matrix products: 5.75 us -> none  [contract(): lax.dot_general(piece.reshape(first * second, width), flat_right, (((1,),...]
    reduce_sum x1 -> x0, other arithmetic: 2.52 us -> none  [sent_and_summed(): return arrived.sum(axis=0)]
  transfers between devices with their start and end apart: 1 -> 6, of which waited for: 1 -> 4; matrix products, arithmetic and copies ran while one was open for 0% -> 0% of each run, Pallas kernels for 0% -> 3%
where the time goes in v3:
time: 127 us; the launch traced here: 126 us
  blocking collectives  57.1 us (45%)
  starting transfers between devices  28.9 us (23%)
  waiting for transfers between devices  27 us (21%)
  Pallas kernels  11.1 us (9%)
    all_to_all x1, blocking collectives, body(): terms = lax.all_to_all(terms, ('x', 'yl'), 0, 0, tiled=True)  37.3 us
    ppermute x4, waiting for transfers between devices, along(): return lax.ppermute(block, 'yh', [(i, (i + step) % NH) for i in range(NH)])  26.4 us
    all_to_all x1, blocking collectives, body(): terms = lax.all_to_all(add(terms), ('z', 'core'), 0, 0, tiled=True)  19.8 us
    ppermute x4, starting transfers between devices, along(): return lax.ppermute(block, 'yh', [(i, (i + step) % NH) for i in range(NH)])  15.6 us
    all_to_all x1, starting transfers between devices, body(): mine = lax.all_to_all(sent, 'z', 0, 0, tiled=True)  10.9 us
    pallas_call x2, Pallas kernels, product(): pl.pallas_call(functools.partial(product_kernel, cuts, len(unread), len(a...  5.9 us
    pallas_call x1, Pallas kernels, add(): pl.pallas_call(add_kernel, grid=(rest // step,), out_shape=jax.ShapeDtype...  3.52 us
  transfers between devices with their start and end apart: 6, of which 4 were waited for; matrix products, arithmetic and copies ran while one was open for 0% of the time, Pallas kernels for 3%

profile of v3, /device:TPU:1, one launch (start us, length us, event | category | flops | bytes accessed | tf_op | source)
XLA Modules:
  0.0 126.4 jit_solution(13198390753417751904)
XLA Ops:
  0.0 0.0 copy-start
  0.0 1.0 fusion
  1.0 1.1 broadcast_in_dim.10
  2.1 10.9 %all-to-all-start = ((bf16[8,64,1024]{2,1,0:T(8,128)(2,1)}), bf16[8,64,1024]{2,1,0:T(8,128)(2,1)S(1)}, u32[]{:S(2)}, u32[]{:S(2)}) async-start(bf16[8,64,1024]{2,1,0:T(8,128)(2,1)} %broadcast_in_dim.10), calls=%async_computation | async-start | bytes 2097152 | tf_op jit(solution)/shard_map/all_to_all | solution.py:175
  13.0 0.0 copy-done
  13.0 5.9 %collective-permute-start.1 = (bf16[256,1024]{1,0:T(8,128)(2,1)S(1)}, bf16[256,1024]{1,0:T(8,128)(2,1)S(1)}, u32[]{:S(2)}, u32[]{:S(2)}) collective-permute-start(bf16[256,1024]{1,0:T(8,128)(2,1)S(1)} %bitcast.4), channel_id=1, source_target_pairs={{0,48},{16,0},{32,16},{48,32},{1,49},{17,1},{33,17},{49,33},{2,50}... | collective-permute-start | bytes 1572872 | tf_op jit(solution)/shard_map/ppermute | solution.py:21
  18.9 1.9 %collective-permute-start = (bf16[256,1024]{1,0:T(8,128)(2,1)S(1)}, bf16[256,1024]{1,0:T(8,128)(2,1)S(1)}, u32[]{:S(2)}, u32[]{:S(2)}) collective-permute-start(bf16[256,1024]{1,0:T(8,128)(2,1)S(1)} %bitcast.5), channel_id=1, source_target_pairs={{0,16},{16,32},{32,48},{48,0},{1,17},{17,33},{33,49},{49,1},{2,18}... | collective-permute-start | bytes 1572872 | tf_op jit(solution)/shard_map/ppermute | solution.py:21
  20.8 20.7 %collective-permute-done.1.refs_4_ = bf16[256,1024]{1,0:T(8,128)(2,1)S(1)} collective-permute-done((bf16[256,1024]{1,0:T(8,128)(2,1)S(1)}, bf16[256,1024]{1,0:T(8,128)(2,1)S(1)}, u32[]{:S(2)}, u32[]{:S(2)}) %collective-permute-start.1) | collective-permute-done | bytes 524320 | tf_op jit(solution)/shard_map/ppermute | solution.py:21
  41.5 0.0 collective-permute-done.refs_3_
  41.5 0.7 all-to-all-done.refs_0_
  42.1 2.4 %collective-permute-start.2 = (bf16[8,64,1024]{2,1,0:T(8,128)(2,1)S(1)}, bf16[8,64,1024]{2,1,0:T(8,128)(2,1)S(1)}, u32[]{:S(2)}, u32[]{:S(2)}) collective-permute-start(bf16[8,64,1024]{2,1,0:T(8,128)(2,1)S(1)} %all-to-all-done.refs_0_), channel_id=1, source_target_pairs={{0,1},{1,0},{2,3},{3,2},{4,5},{5,4},{6,7},{7,6},{8,9},{9,8},{10,11... | collective-permute-start | bytes 3145736 | tf_op jit(solution)/shard_map/ppermute | solution.py:177
  44.6 5.9 %collective-permute-start.4 = (bf16[128,1024]{1,0:T(8,128)(2,1)S(1)}, bf16[128,1024]{1,0:T(8,128)(2,1)S(1)}, u32[]{:S(2)}, u32[]{:S(2)}) collective-permute-start(bf16[128,1024]{1,0:T(8,128)(2,1)S(1)} %slice.19), channel_id=1, source_target_pairs={{0,48},{16,0},{32,16},{48,32},{1,49},{17,1},{33,17},{49,33},{2,50}... | collective-permute-start | bytes 786440 | tf_op jit(solution)/shard_map/ppermute | solution.py:21
  50.5 1.9 %collective-permute-start.3 = (bf16[128,1024]{1,0:T(8,128)(2,1)S(1)}, bf16[128,1024]{1,0:T(8,128)(2,1)S(1)}, u32[]{:S(2)}, u32[]{:S(2)}) collective-permute-start(bf16[128,1024]{1,0:T(8,128)(2,1)S(1)} %slice.18), channel_id=1, source_target_pairs={{0,16},{16,32},{32,48},{48,0},{1,17},{17,33},{33,49},{49,1},{2,18}... | collective-permute-start | bytes 786440 | tf_op jit(solution)/shard_map/ppermute | solution.py:21
  52.4 0.0 collective-permute-done.2.refs_1_
  52.4 4.1 %shard_map.37.refs_4_ = bf16[8,16,64,128]{3,2,1,0:T(8,128)(2,1)S(1)} custom-call(bf16[8,64,1024]{2,1,0:T(8,128)(2,1)S(1)} %all-to-all-done.refs_0_, bf16[8,64,1024]{2,1,0:T(8,128)(2,1)S(1)} %collective-permute-done.2.refs_1_, bf16[256,1024]{1,0:T(8,128)(2,1)S(1)} %bitcast.6, bf16[256,1024]{1,0:T(8,128)(2,1)S(1)} %collective-permute-done.refs_3_, ...), custom_call_target="tpu_custom_call" | custom-call | flops 1610612736 | bytes 5242880 | tf_op jit(solution)/shard_map/pallas_call | solution.py:93
  56.5 5.1 %collective-permute-done.4.refs_3_ = bf16[128,1024]{1,0:T(8,128)(2,1)S(1)} collective-permute-done((bf16[128,1024]{1,0:T(8,128)(2,1)S(1)}, bf16[128,1024]{1,0:T(8,128)(2,1)S(1)}, u32[]{:S(2)}, u32[]{:S(2)}) %collective-permute-start.4) | collective-permute-done | bytes 262176 | tf_op jit(solution)/shard_map/ppermute | solution.py:21
  61.6 0.6 collective-permute-done.3.refs_2_
  62.2 1.8 %shard_map.38 = bf16[8,16,64,128]{3,2,1,0:T(8,128)(2,1)S(1)} custom-call(bf16[8,64,1024]{2,1,0:T(8,128)(2,1)S(1)} %all-to-all-done.refs_0_, bf16[8,64,1024]{2,1,0:T(8,128)(2,1)S(1)} %collective-permute-done.2.refs_1_, bf16[128,1024]{1,0:T(8,128)(2,1)S(1)} %collective-permute-done.3.refs_2_, ...), custom_call_target="tpu_custom_call", output_to_operand_aliasing={{}: (4, {})} | custom-call | flops 536870912 | bytes 5242880 | tf_op jit(solution)/shard_map/pallas_call | solution.py:93
  64.0 37.3 %all_to_all.15.refs_0_ = bf16[8,16,64,128]{3,2,1,0:T(8,128)(2,1)} all-to-all(bf16[8,16,64,128]{3,2,1,0:T(8,128)(2,1)S(1)} %shard_map.38), channel_id=1, replica_groups=mesh['x'=4,'yl'=2,'yh'=4,'z'=8,'core'=2] {'x','yl'}, dimensions={0} | all-to-all | bytes 4194304 | tf_op jit(solution)/shard_map/all_to_all | solution.py:185
  101.3 3.5 %shard_map.39 = bf16[16,64,128]{2,1,0:T(8,128)(2,1)} custom-call(bf16[8,16,64,128]{3,2,1,0:T(8,128)(2,1)} %all_to_all.15.refs_0_), custom_call_target="tpu_custom_call" | custom-call | flops 1048576 | bytes 2097152 | tf_op jit(solution)/shard_map/pallas_call | solution.py:127
  104.8 19.8 %all_to_all.16.terms_ref = bf16[16,64,128]{2,1,0:T(8,128)(2,1)} all-to-all(bf16[16,64,128]{2,1,0:T(8,128)(2,1)} %shard_map.39), channel_id=1, replica_groups=mesh['x'=4,'yl'=2,'yh'=4,'z'=8,'core'=2] {'z','core'}, dimensions={0} | all-to-all | bytes 524288 | tf_op jit(solution)/shard_map/all_to_all | solution.py:186
  124.6 1.7 %shard_map.40 = f32[4,16,8,256]{3,2,1,0:T(8,128)} custom-call(bf16[16,64,128]{2,1,0:T(8,128)(2,1)} %all_to_all.16.terms_ref), custom_call_target="tpu_custom_call" | custom-call | flops 131072 | bytes 1048576 | tf_op jit(solution)/shard_map/pallas_call | solution.py:155
  (4 shorter events, 0.0 us)
Async XLA Ops:
  0.0 13.0 %copy-start = (bf16[1,256,1024]{2,1,0:T(8,128)(2,1)S(1)}, bf16[1,256,1024]{2,1,0:T(8,128)(2,1)}, u32[]{:S(2)}) copy-start(bf16[1,256,1024]{2,1,0:T(8,128)(2,1)} %param.4) | copy-start | bytes 1572868
  2.1 40.1 %all-to-all-start = ((bf16[8,64,1024]{2,1,0:T(8,128)(2,1)}), bf16[8,64,1024]{2,1,0:T(8,128)(2,1)S(1)}, u32[]{:S(2)}, u32[]{:S(2)}) async-start(bf16[8,64,1024]{2,1,0:T(8,128)(2,1)} %broadcast_in_dim.10), calls=%async_computation | async-start | bytes 2097152 | tf_op jit(solution)/shard_map/all_to_all | solution.py:175
  13.0 28.5 %collective-permute-start.1 = (bf16[256,1024]{1,0:T(8,128)(2,1)S(1)}, bf16[256,1024]{1,0:T(8,128)(2,1)S(1)}, u32[]{:S(2)}, u32[]{:S(2)}) collective-permute-start(bf16[256,1024]{1,0:T(8,128)(2,1)S(1)} %bitcast.4), channel_id=1, source_target_pairs={{0,48},{16,0},{32,16},{48,32},{1,49},{17,1},{33,17},{49,33},{2,50}... | collective-permute-start | bytes 1572872 | tf_op jit(solution)/shard_map/ppermute | solution.py:21
  18.9 22.6 %collective-permute-start = (bf16[256,1024]{1,0:T(8,128)(2,1)S(1)}, bf16[256,1024]{1,0:T(8,128)(2,1)S(1)}, u32[]{:S(2)}, u32[]{:S(2)}) collective-permute-start(bf16[256,1024]{1,0:T(8,128)(2,1)S(1)} %bitcast.5), channel_id=1, source_target_pairs={{0,16},{16,32},{32,48},{48,0},{1,17},{17,33},{33,49},{49,1},{2,18}... | collective-permute-start | bytes 1572872 | tf_op jit(solution)/shard_map/ppermute | solution.py:21
  42.1 10.3 %collective-permute-start.2 = (bf16[8,64,1024]{2,1,0:T(8,128)(2,1)S(1)}, bf16[8,64,1024]{2,1,0:T(8,128)(2,1)S(1)}, u32[]{:S(2)}, u32[]{:S(2)}) collective-permute-start(bf16[8,64,1024]{2,1,0:T(8,128)(2,1)S(1)} %all-to-all-done.refs_0_), channel_id=1, source_target_pairs={{0,1},{1,0},{2,3},{3,2},{4,5},{5,4},{6,7},{7,6},{8,9},{9,8},{10,11... | collective-permute-start | bytes 3145736 | tf_op jit(solution)/shard_map/ppermute | solution.py:177
  44.6 17.1 %collective-permute-start.4 = (bf16[128,1024]{1,0:T(8,128)(2,1)S(1)}, bf16[128,1024]{1,0:T(8,128)(2,1)S(1)}, u32[]{:S(2)}, u32[]{:S(2)}) collective-permute-start(bf16[128,1024]{1,0:T(8,128)(2,1)S(1)} %slice.19), channel_id=1, source_target_pairs={{0,48},{16,0},{32,16},{48,32},{1,49},{17,1},{33,17},{49,33},{2,50}... | collective-permute-start | bytes 786440 | tf_op jit(solution)/shard_map/ppermute | solution.py:21
  50.5 11.7 %collective-permute-start.3 = (bf16[128,1024]{1,0:T(8,128)(2,1)S(1)}, bf16[128,1024]{1,0:T(8,128)(2,1)S(1)}, u32[]{:S(2)}, u32[]{:S(2)}) collective-permute-start(bf16[128,1024]{1,0:T(8,128)(2,1)S(1)} %slice.18), channel_id=1, source_target_pairs={{0,16},{16,32},{32,48},{48,0},{1,17},{17,33},{33,49},{49,1},{2,18}... | collective-permute-start | bytes 786440 | tf_op jit(solution)/shard_map/ppermute | solution.py:21

commit v4 on v0

v4 whole, which is shorter than its diff:
```python
import functools

import jax
import jax.numpy as jnp
from jax import lax
from jax.experimental import pallas as pl
from jax.experimental.pallas import tpu as pltpu
from jax.sharding import Mesh, PartitionSpec as P

BF16 = jnp.bfloat16
F32 = jnp.float32
AXES = ("x", "yl", "yh", "z", "core")
SIZES = (4, 2, 4, 8, 2)
NX, NL, NH, NZ, NC = SIZES
NY = NL * NH
LANES = 128
MIB = 2**20

OWN, R1, L1, R2, L2, R3, L3, FAR = range(8)
SLOTS = (
    ((OWN, OWN, 0), (L1, R1, 1)),
    ((R2, L2, 0), (R1, L1, 1)),
    ((L2, R2, 0), (L3, R3, 1)),
    ((FAR, FAR, 0), (R3, L3, 1)),
)


def place(y):
    return (y % NL) * NH + (y % NY) // NL


def around(block, step):
    pairs = [(place(y), place(y + step + NY)) for y in range(NY)]
    return lax.ppermute(block, ("yl", "yh"), pairs)


def dot(left, right):
    return lax.dot_general(left, right, (((1,), (1,)), ((), ())), preferred_element_type=F32)


def product_kernel(names, slots, ignored, at_row, *refs):
    count = len(names)
    rows_refs, piece_refs = refs[:2], refs[2 : 2 + count]
    out_ref, left, right, held, left_sem, right_sem, out_sem = refs[2 + count + ignored :]
    yl, core = lax.axis_index("yl"), lax.axis_index("core")
    nz, _, rows, width = rows_refs[0].shape
    wide = rows // NX
    blocks = []
    for name, _ in names:
        if name not in blocks:
            blocks.append(name)
    lefts = [
        [
            pltpu.make_async_copy(rows_refs[i].at[:, h], left.at[h, i], left_sem.at[h, i])
            for i in range(2)
        ]
        for h in range(2)
    ]
    rights = {name: [] for name in blocks}
    for n, (name, piece) in enumerate(names):
        target = right.at[blocks.index(name)]
        if piece is not None:
            part = right.shape[1] // 2
            target = target.at[pl.ds(piece * part, part)]
        rights[name].append(pltpu.make_async_copy(piece_refs[n], target, right_sem.at[n]))
    order = []
    for slot in slots:
        for even, odd, half in slot:
            order.append(("left", half))
            order += [("right", name) for name in {even: 0, odd: 0}]
    waits = []
    for step in order:
        if step not in waits:
            waits.append(step)
    copies = {
        step: lefts[step[1]] if step[0] == "left" else rights[step[1]] for step in waits
    }
    for step in waits:
        for copy in copies[step]:
            copy.start()
    done = []
    for slot in slots:
        total = None
        for even, odd, half in slot:
            for step in [("left", half)] + [("right", name) for name in {even: 0, odd: 0}]:
                for copy in copies.pop(step, ()):
                    copy.wait()
            where = blocks.index(even)
            if even != odd:
                where = jnp.where(yl == 0, where, blocks.index(odd))
            term = dot(left[half].reshape(2 * nz * rows, width), right[where])
            total = term if total is None else total + term
        done += [total[:, c : c + LANES] for c in range(0, total.shape[1], LANES)]
    for which in range(2):
        target_core = core if which == 0 else 1 - core
        for zi in range(nz):
            for xi in range(NX):
                at = (which * nz + zi) * rows + xi * wide
                block = jnp.concatenate([d[at : at + wide] for d in done], axis=0)
                held[(xi * nz + zi) * NC + target_core] = block.astype(BF16)
    copy = pltpu.make_async_copy(held, out_ref.at[:, pl.ds(at_row, held.shape[1])], out_sem)
    copy.start()
    copy.wait()


def product(mine, other, pieces, slots, at_row, height, unread=(), begun=None):
    nz, _, rows, width = mine.shape
    wide = rows // NX
    names = tuple(piece[:2] for piece in pieces)
    columns = 2 * pieces[-1][2].shape[0]
    if pieces[-1][1] is None:
        columns = pieces[-1][2].shape[0]
    tall = len(slots) * columns // LANES * wide
    members = NX * nz * NC
    flops = 2 * 2 * nz * rows * width * columns * 2 * len(slots)
    anywhere = pl.BlockSpec(memory_space=pltpu.HBM)
    operands = [mine, other, *[piece[2] for piece in pieces], *unread]
    ignored, aliases = len(unread), {}
    if begun is not None:
        aliases = {len(operands): 0}
        operands.append(begun)
        ignored += 1
    return pl.pallas_call(
        functools.partial(product_kernel, names, slots, ignored, at_row),
        out_shape=jax.ShapeDtypeStruct((members, height, LANES), BF16),
        in_specs=[anywhere] * len(operands),
        out_specs=anywhere,
        scratch_shapes=[
            pltpu.VMEM((2, 2, nz, rows, width), BF16),
            pltpu.VMEM((len({n for n, _ in names}), columns, width), BF16),
            pltpu.VMEM((members, tall, LANES), BF16),
            pltpu.SemaphoreType.DMA((2, 2)),
            pltpu.SemaphoreType.DMA((len(names),)),
            pltpu.SemaphoreType.DMA,
        ],
        input_output_aliases=aliases,
        compiler_params=pltpu.CompilerParams(vmem_limit_bytes=40 * MIB),
        cost_estimate=pl.CostEstimate(flops=flops, bytes_accessed=5 * MIB, transcendentals=0),
    )(*operands)


def finish_kernel(terms_ref, out_ref):
    yh = lax.axis_index("yh")
    step = 1 - 2 * lax.axis_index("yl")
    wide, columns = out_ref.shape[2:]
    total = terms_ref[0].astype(F32)
    for xi in range(1, NX):
        total = total + terms_ref[xi].astype(F32)
    at = 0
    for offset in (0, -step, step, 2):
        owner = lax.rem(yh + NH + offset, NH)
        for c in range(0, columns, LANES):
            out_ref[owner, :, :, c : c + LANES] = total[:, at : at + wide]
            at += wide


def finish(terms, columns):
    members, tall, _ = terms.shape
    rest = members // NX
    wide = tall * LANES // columns // NH
    terms = terms.reshape(NX, rest, tall, LANES)
    step = rest // 2
    return pl.pallas_call(
        finish_kernel,
        grid=(rest // step,),
        out_shape=jax.ShapeDtypeStruct((NH, rest, wide, columns), F32),
        in_specs=[pl.BlockSpec((NX, step, tall, LANES), lambda i: (0, i, 0, 0))],
        out_specs=pl.BlockSpec((NH, step, wide, columns), lambda i: (0, i, 0, 0)),
        cost_estimate=pl.CostEstimate(flops=2**19, bytes_accessed=3 * 2**19, transcendentals=0),
    )(terms)


def body(valence_pairs, conduction_pairs, screening):
    yl = lax.axis_index("yl")
    _, second, plane_dev = valence_pairs.shape
    own = conduction_pairs[0]
    columns = own.shape[0]
    cut = columns // 2
    wide = second // (NX * NL)

    screened = (valence_pairs[0].astype(F32) * screening[None, :]).astype(BF16)
    screened = screened.reshape(NX, NL, wide, plane_dev)
    kept = jnp.where(yl == 0, screened[:, 0], screened[:, 1]).reshape(NX * wide, plane_dev)
    given = jnp.where(yl == 0, screened[:, 1], screened[:, 0]).reshape(NX * wide, plane_dev)
    taken = lax.ppermute(given, "yl", [(0, 1), (1, 0)])
    r1, l1 = around(own, 1), around(own, -1)
    sent = jnp.broadcast_to(jnp.stack([kept, taken]), (NZ, NL, NX * wide, plane_dev))
    sent, *rows = lax.optimization_barrier((sent, r1[:16], l1[:16]))
    mine = lax.all_to_all(sent, "z", 0, 0, tiled=True)

    r2, l2 = around(r1, 1), around(l1, -1)
    r3, l3 = around(r2, 1), around(l2, -1)
    far = around(r3[:cut], 1), around(l3[cut:], -1)

    mine, *more = lax.optimization_barrier((mine, r3[:16], l3[:16]))
    other = lax.ppermute(mine, "core", [(0, 1), (1, 0)])

    per_slot = columns // LANES * wide
    height = len(SLOTS) * per_slot
    near = ((OWN, own), (R1, r1), (L1, l1), (R2, r2), (L2, l2), (R3, r3), (L3, l3))
    terms = product(
        mine, other, [(n, None, b) for n, b in near], SLOTS[:3], 0, height, rows + more
    )
    terms = product(
        mine, other,
        [(R3, None, r3), (L3, None, l3), (FAR, 0, far[0]), (FAR, 1, far[1])],
        SLOTS[3:], 3 * per_slot, height, (), terms,
    )
    terms = lax.all_to_all(terms, ("x", "z", "core"), 0, 0, tiled=True)
    out = finish(terms, columns)
    return out.reshape(1, NH * NZ * NC, wide, columns)


def solution(mesh):
    fine = Mesh(mesh.devices.reshape(SIZES), AXES)
    pair, pw = ("yh", "z", "core"), ("x", "yl")
    placed = (P(pair, None, pw), P(pair, None, pw), P(pw))
    return jax.shard_map(
        body, mesh=fine, in_specs=placed, out_specs=P(pair, None, pw, None), check_vma=False
    )
```

time: 218 us -> 125 us (0.57)
  waiting for transfers between devices: 113 us -> 22.7 us
  starting transfers between devices: 0.01 us -> 48.8 us
  blocking collectives: 80.3 us -> 39.2 us
  between operations: 13.4 us -> 0.25 us
  Pallas kernels: 0 us -> 7.22 us
  matrix products: 5.75 us -> 0 us
  local copies, waits for them, and re-layouts: 1.19 us -> 4.49 us
  other arithmetic: 4.16 us -> 0.96 us
    all_gather x1 -> x0, waiting for transfers between devices: 113 us -> none  [body(): lax.all_gather(screened, 'pair', axis=0, tiled=True)]
    all_to_all x2 -> x1, blocking collectives: 80.3 us -> 39.2 us  [body(): terms = lax.all_to_all(terms, ('x', 'z', 'core'), 0, 0, tiled=True)]
    ppermute x0 -> x10, starting transfers between devices: none -> 34.9 us  [the longest x8 27.3 us: around(): return lax.ppermute(block, ('yl', 'yh'), pairs)]
    ppermute x0 -> x10, waiting for transfers between devices: none -> 22.7 us  [the longest x8 17.9 us: around(): return lax.ppermute(block, ('yl', 'yh'), pairs)]
    all_to_all x0 -> x1, starting transfers between devices: none -> 13.9 us  [body(): mine = lax.all_to_all(sent, 'z', 0, 0, tiled=True)]
    pallas_call x0 -> x3, Pallas kernels: none -> 7.22 us  [the longest x2 5.25 us: product(): pl.pallas_call(functools.partial(product_kernel, names, slots, ignored, a...]
    dot_general x1 -> x0, matrix products: 5.75 us -> none  [contract(): lax.dot_general(piece.reshape(first * second, width), flat_right, (((1,),...]
    unnamed x3 -> x12, local copies, waits for them, and re-layouts: 0.8 us -> 3.32 us
  transfers between devices with their start and end apart: 1 -> 11, of which waited for: 1 -> 5; matrix products, arithmetic and copies ran while one was open for 0% -> 1% of each run, Pallas kernels for 0% -> 3%
where the time goes in v4:
time: 125 us; the launch traced here: 124 us
  starting transfers between devices  48.8 us (39%)
  blocking collectives  39.2 us (31%)
  waiting for transfers between devices  22.7 us (18%)
  Pallas kernels  7.22 us (6%)
  local copies, waits for them, and re-layouts  4.49 us (4%)
    all_to_all x1, blocking collectives, body(): terms = lax.all_to_all(terms, ('x', 'z', 'core'), 0, 0, tiled=True)  39.2 us
    ppermute x8, starting transfers between devices, around(): return lax.ppermute(block, ('yl', 'yh'), pairs)  27.3 us
    ppermute x8, waiting for transfers between devices, around(): return lax.ppermute(block, ('yl', 'yh'), pairs)  17.9 us
    all_to_all x1, starting transfers between devices, body(): mine = lax.all_to_all(sent, 'z', 0, 0, tiled=True)  13.9 us
    ppermute x1, starting transfers between devices, body(): other = lax.ppermute(mine, 'core', [(0, 1), (1, 0)])  5.7 us
    pallas_call x2, Pallas kernels, product(): pl.pallas_call(functools.partial(product_kernel, names, slots, ignored, a...  5.25 us
    ppermute x1, waiting for transfers between devices, body(): taken = lax.ppermute(given, 'yl', [(0, 1), (1, 0)])  4.76 us
    unnamed x12, local copies, waits for them, and re-layouts  3.32 us
  transfers between devices with their start and end apart: 11, of which 5 were waited for; matrix products, arithmetic and copies ran while one was open for 1% of the time, Pallas kernels for 3%

profile of v4, /device:TPU:1, one launch (start us, length us, event | category | flops | bytes accessed | tf_op | source)
XLA Modules:
  0.0 123.6 jit_solution(2915292477564221600)
XLA Ops:
  0.0 4.0 %collective-permute-start.1 = (bf16[256,1024]{1,0:T(8,128)(2,1)}, bf16[256,1024]{1,0:T(8,128)(2,1)S(1)}, u32[]{:S(2)}, u32[]{:S(2)}) collective-permute-start(bf16[256,1024]{1,0:T(8,128)(2,1)} %bitcast.10), channel_id=1, source_target_pairs={{0,64},{64,16},{16,80},{80,32},{32,96},{96,48},{48,112},{112,0},{1... | collective-permute-start | bytes 1572872 | tf_op jit(solution)/shard_map/ppermute | solution.py:34
  4.0 3.8 %collective-permute-start.2 = (bf16[256,1024]{1,0:T(8,128)(2,1)}, bf16[256,1024]{1,0:T(8,128)(2,1)S(1)}, u32[]{:S(2)}, u32[]{:S(2)}) collective-permute-start(bf16[256,1024]{1,0:T(8,128)(2,1)} %bitcast.11), channel_id=1, source_target_pairs={{0,112},{64,0},{16,64},{80,16},{32,80},{96,32},{48,96},{112,48},{1... | collective-permute-start | bytes 1572872 | tf_op jit(solution)/shard_map/ppermute | solution.py:34
  8.5 0.9 fusion
  9.5 1.9 %collective-permute-start = (bf16[32,1024]{1,0:T(8,128)(2,1)S(1)}, bf16[32,1024]{1,0:T(8,128)(2,1)S(1)}, u32[]{:S(2)}, u32[]{:S(2)}) collective-permute-start(bf16[32,1024]{1,0:T(8,128)(2,1)S(1)} %get-tuple-element.18), channel_id=1, source_target_pairs={{0,64},{64,0},{1,65},{65,1},{2,66},{66,2},{3,67},{67,3},{4,68},{68... | collective-permute-start | bytes 196616 | tf_op jit(solution)/shard_map/ppermute | solution.py:185
  11.4 4.8 %collective-permute-done = bf16[32,1024]{1,0:T(8,128)(2,1)S(1)} collective-permute-done((bf16[32,1024]{1,0:T(8,128)(2,1)S(1)}, bf16[32,1024]{1,0:T(8,128)(2,1)S(1)}, u32[]{:S(2)}, u32[]{:S(2)}) %collective-permute-start) | collective-permute-done | bytes 65568 | tf_op jit(solution)/shard_map/ppermute | solution.py:185
  16.3 1.1 broadcast_in_dim.4
  17.4 13.9 %all-to-all-start = ((bf16[8,2,32,1024]{3,2,1,0:T(8,128)(2,1)}), bf16[8,2,32,1024]{3,2,1,0:T(8,128)(2,1)S(1)}, u32[]{:S(2)}, u32[]{:S(2)}) async-start(bf16[8,2,32,1024]{3,2,1,0:T(8,128)(2,1)} %broadcast_in_dim.4), calls=%async_computation | async-start | bytes 2097152 | tf_op jit(solution)/shard_map/all_to_all | solution.py:189
  31.2 1.9 %collective-permute-start.3 = (bf16[256,1024]{1,0:T(8,128)(2,1)S(1)}, bf16[256,1024]{1,0:T(8,128)(2,1)S(1)}, u32[]{:S(2)}, u32[]{:S(2)}) collective-permute-start(bf16[256,1024]{1,0:T(8,128)(2,1)S(1)} %collective-permute-done.1.refs_3_), channel_id=1, source_target_pairs={{0,64},{64,16},{16,80},{80,32},{32,96},{96,48},{48,112},{112,0},{1... | collective-permute-start | bytes 1572872 | tf_op jit(solution)/shard_map/ppermute | solution.py:34
  33.1 4.6 %collective-permute-start.5 = (bf16[256,1024]{1,0:T(8,128)(2,1)S(1)}, bf16[256,1024]{1,0:T(8,128)(2,1)S(1)}, u32[]{:S(2)}, u32[]{:S(2)}) collective-permute-start(bf16[256,1024]{1,0:T(8,128)(2,1)S(1)} %collective-permute-done.2.refs_4_), channel_id=1, source_target_pairs={{0,112},{64,0},{16,64},{80,16},{32,80},{96,32},{48,96},{112,48},{1... | collective-permute-start | bytes 1572872 | tf_op jit(solution)/shard_map/ppermute | solution.py:34
  37.7 7.9 %collective-permute-done.3.refs_5_ = bf16[256,1024]{1,0:T(8,128)(2,1)S(1)} collective-permute-done((bf16[256,1024]{1,0:T(8,128)(2,1)S(1)}, bf16[256,1024]{1,0:T(8,128)(2,1)S(1)}, u32[]{:S(2)}, u32[]{:S(2)}) %collective-permute-start.3) | collective-permute-done | bytes 524320 | tf_op jit(solution)/shard_map/ppermute | solution.py:34
  45.6 2.8 %collective-permute-start.4 = (bf16[256,1024]{1,0:T(8,128)(2,1)S(1)}, bf16[256,1024]{1,0:T(8,128)(2,1)S(1)}, u32[]{:S(2)}, u32[]{:S(2)}) collective-permute-start(bf16[256,1024]{1,0:T(8,128)(2,1)S(1)} %collective-permute-done.3.refs_5_), channel_id=1, source_target_pairs={{0,64},{64,16},{16,80},{80,32},{32,96},{96,48},{48,112},{112,0},{1... | collective-permute-start | bytes 1572872 | tf_op jit(solution)/shard_map/ppermute | solution.py:34
  49.2 3.7 %collective-permute-start.6 = (bf16[256,1024]{1,0:T(8,128)(2,1)S(1)}, bf16[256,1024]{1,0:T(8,128)(2,1)S(1)}, u32[]{:S(2)}, u32[]{:S(2)}) collective-permute-start(bf16[256,1024]{1,0:T(8,128)(2,1)S(1)} %collective-permute-done.5.refs_6_), channel_id=1, source_target_pairs={{0,112},{64,0},{16,64},{80,16},{32,80},{96,32},{48,96},{112,48},{1... | collective-permute-start | bytes 1572872 | tf_op jit(solution)/shard_map/ppermute | solution.py:34
  52.9 0.8 copy-done.3
  53.7 5.3 %collective-permute-done.4.refs_7_.refs_2_ = bf16[256,1024]{1,0:T(8,128)(2,1)S(1)} collective-permute-done((bf16[256,1024]{1,0:T(8,128)(2,1)S(1)}, bf16[256,1024]{1,0:T(8,128)(2,1)S(1)}, u32[]{:S(2)}, u32[]{:S(2)}) %collective-permute-start.4) | collective-permute-done | bytes 524320 | tf_op jit(solution)/shard_map/ppermute | solution.py:34
  59.0 3.5 %collective-permute-done.6.refs_8_.refs_3_ = bf16[256,1024]{1,0:T(8,128)(2,1)S(1)} collective-permute-done((bf16[256,1024]{1,0:T(8,128)(2,1)S(1)}, bf16[256,1024]{1,0:T(8,128)(2,1)S(1)}, u32[]{:S(2)}, u32[]{:S(2)}) %collective-permute-start.6) | collective-permute-done | bytes 524320 | tf_op jit(solution)/shard_map/ppermute | solution.py:34
  62.5 5.7 %collective-permute-start.7 = (bf16[8,2,32,1024]{3,2,1,0:T(8,128)(2,1)S(1)}, bf16[8,2,32,1024]{3,2,1,0:T(8,128)(2,1)S(1)}, u32[]{:S(2)}, u32[]{:S(2)}) collective-permute-start(bf16[8,2,32,1024]{3,2,1,0:T(8,128)(2,1)S(1)} %all-to-all-done.refs_0_), channel_id=1, source_target_pairs={{0,1},{1,0},{2,3},{3,2},{4,5},{5,4},{6,7},{7,6},{8,9},{9,8},{10,11... | collective-permute-start | bytes 3145736 | tf_op jit(solution)/shard_map/ppermute | solution.py:196
  68.3 3.4 %collective-permute-start.8 = (bf16[128,1024]{1,0:T(8,128)(2,1)S(1)}, bf16[128,1024]{1,0:T(8,128)(2,1)S(1)}, u32[]{:S(2)}, u32[]{:S(2)}) collective-permute-start(bf16[128,1024]{1,0:T(8,128)(2,1)S(1)} %slice.40), channel_id=1, source_target_pairs={{0,64},{64,16},{16,80},{80,32},{32,96},{96,48},{48,112},{112,0},{1... | collective-permute-start | bytes 786440 | tf_op jit(solution)/shard_map/ppermute | solution.py:34
  71.7 3.1 %collective-permute-start.9 = (bf16[128,1024]{1,0:T(8,128)(2,1)S(1)}, bf16[128,1024]{1,0:T(8,128)(2,1)S(1)}, u32[]{:S(2)}, u32[]{:S(2)}) collective-permute-start(bf16[128,1024]{1,0:T(8,128)(2,1)S(1)} %slice.41), channel_id=1, source_target_pairs={{0,112},{64,0},{16,64},{80,16},{32,80},{96,32},{48,96},{112,48},{1... | collective-permute-start | bytes 786440 | tf_op jit(solution)/shard_map/ppermute | solution.py:34
  74.8 1.0 copy-done.4
  75.9 4.0 %shard_map.37.refs_6_ = bf16[64,64,128]{2,1,0:T(8,128)(2,1)S(1)} custom-call(bf16[8,2,32,1024]{3,2,1,0:T(8,128)(2,1)S(1)} %all-to-all-done.refs_0_, bf16[8,2,32,1024]{3,2,1,0:T(8,128)(2,1)S(1)} %collective-permute-done.7.refs_1_, bf16[256,1024]{1,0:T(8,128)(2,1)S(1)} %bitcast.12, bf16[256,1024]{1,0:T(8,128)(2,1)S(1)} %collective-permute-done.1.refs_3_, ...), custom_call_target="tpu_custom_call" | custom-call | flops 1610612736 | bytes 5242880 | tf_op jit(solution)/shard_map/pallas_call | solution.py:123
  79.9 1.2 %collective-permute-done.9.refs_5_ = bf16[128,1024]{1,0:T(8,128)(2,1)S(1)} collective-permute-done((bf16[128,1024]{1,0:T(8,128)(2,1)S(1)}, bf16[128,1024]{1,0:T(8,128)(2,1)S(1)}, u32[]{:S(2)}, u32[]{:S(2)}) %collective-permute-start.9) | collective-permute-done | bytes 262176 | tf_op jit(solution)/shard_map/ppermute | solution.py:34
  81.2 1.2 shard_map.38
  82.4 39.2 %all_to_all.10 = bf16[64,64,128]{2,1,0:T(8,128)(2,1)} all-to-all(bf16[64,64,128]{2,1,0:T(8,128)(2,1)S(1)} %shard_map.38), channel_id=1, replica_groups=mesh['x'=4,'yl'=2,'yh'=4,'z'=8,'core'=2] {'x','z','core'}, dimensions={0} | all-to-all | bytes 2097152 | tf_op jit(solution)/shard_map/all_to_all | solution.py:209
  121.6 2.0 %shard_map.39 = f32[4,16,8,256]{3,2,1,0:T(8,128)} custom-call(bf16[4,16,64,128]{3,2,1,0:T(8,128)(2,1)} %bitcast.13), custom_call_target="tpu_custom_call" | custom-call | flops 524288 | bytes 1572864 | tf_op jit(solution)/shard_map/pallas_call | solution.py:163
  (24 shorter events, 1.6 us)
Async XLA Ops:
  0.0 16.2 %collective-permute-start.1 = (bf16[256,1024]{1,0:T(8,128)(2,1)}, bf16[256,1024]{1,0:T(8,128)(2,1)S(1)}, u32[]{:S(2)}, u32[]{:S(2)}) collective-permute-start(bf16[256,1024]{1,0:T(8,128)(2,1)} %bitcast.10), channel_id=1, source_target_pairs={{0,64},{64,16},{16,80},{80,32},{32,96},{96,48},{48,112},{112,0},{1... | collective-permute-start | bytes 1572872 | tf_op jit(solution)/shard_map/ppermute | solution.py:34
  4.0 12.2 %collective-permute-start.2 = (bf16[256,1024]{1,0:T(8,128)(2,1)}, bf16[256,1024]{1,0:T(8,128)(2,1)S(1)}, u32[]{:S(2)}, u32[]{:S(2)}) collective-permute-start(bf16[256,1024]{1,0:T(8,128)(2,1)} %bitcast.11), channel_id=1, source_target_pairs={{0,112},{64,0},{16,64},{80,16},{32,80},{96,32},{48,96},{112,48},{1... | collective-permute-start | bytes 1572872 | tf_op jit(solution)/shard_map/ppermute | solution.py:34
  7.9 0.7 copy-start.5
  9.5 6.7 %collective-permute-start = (bf16[32,1024]{1,0:T(8,128)(2,1)S(1)}, bf16[32,1024]{1,0:T(8,128)(2,1)S(1)}, u32[]{:S(2)}, u32[]{:S(2)}) collective-permute-start(bf16[32,1024]{1,0:T(8,128)(2,1)S(1)} %get-tuple-element.18), channel_id=1, source_target_pairs={{0,64},{64,0},{1,65},{65,1},{2,66},{66,2},{3,67},{67,3},{4,68},{68... | collective-permute-start | bytes 196616 | tf_op jit(solution)/shard_map/ppermute | solution.py:185
  17.4 45.1 %all-to-all-start = ((bf16[8,2,32,1024]{3,2,1,0:T(8,128)(2,1)}), bf16[8,2,32,1024]{3,2,1,0:T(8,128)(2,1)S(1)}, u32[]{:S(2)}, u32[]{:S(2)}) async-start(bf16[8,2,32,1024]{3,2,1,0:T(8,128)(2,1)} %broadcast_in_dim.4), calls=%async_computation | async-start | bytes 2097152 | tf_op jit(solution)/shard_map/all_to_all | solution.py:189
  31.2 14.4 %collective-permute-start.3 = (bf16[256,1024]{1,0:T(8,128)(2,1)S(1)}, bf16[256,1024]{1,0:T(8,128)(2,1)S(1)}, u32[]{:S(2)}, u32[]{:S(2)}) collective-permute-start(bf16[256,1024]{1,0:T(8,128)(2,1)S(1)} %collective-permute-done.1.refs_3_), channel_id=1, source_target_pairs={{0,64},{64,16},{16,80},{80,32},{32,96},{96,48},{48,112},{112,0},{1... | collective-permute-start | bytes 1572872 | tf_op jit(solution)/shard_map/ppermute | solution.py:34
  33.1 16.0 %collective-permute-start.5 = (bf16[256,1024]{1,0:T(8,128)(2,1)S(1)}, bf16[256,1024]{1,0:T(8,128)(2,1)S(1)}, u32[]{:S(2)}, u32[]{:S(2)}) collective-permute-start(bf16[256,1024]{1,0:T(8,128)(2,1)S(1)} %collective-permute-done.2.refs_4_), channel_id=1, source_target_pairs={{0,112},{64,0},{16,64},{80,16},{32,80},{96,32},{48,96},{112,48},{1... | collective-permute-start | bytes 1572872 | tf_op jit(solution)/shard_map/ppermute | solution.py:34
  45.6 13.4 %collective-permute-start.4 = (bf16[256,1024]{1,0:T(8,128)(2,1)S(1)}, bf16[256,1024]{1,0:T(8,128)(2,1)S(1)}, u32[]{:S(2)}, u32[]{:S(2)}) collective-permute-start(bf16[256,1024]{1,0:T(8,128)(2,1)S(1)} %collective-permute-done.3.refs_5_), channel_id=1, source_target_pairs={{0,64},{64,16},{16,80},{80,32},{32,96},{96,48},{48,112},{112,0},{1... | collective-permute-start | bytes 1572872 | tf_op jit(solution)/shard_map/ppermute | solution.py:34
  48.4 0.8 copy-start.1
  49.2 13.3 %collective-permute-start.6 = (bf16[256,1024]{1,0:T(8,128)(2,1)S(1)}, bf16[256,1024]{1,0:T(8,128)(2,1)S(1)}, u32[]{:S(2)}, u32[]{:S(2)}) collective-permute-start(bf16[256,1024]{1,0:T(8,128)(2,1)S(1)} %collective-permute-done.5.refs_6_), channel_id=1, source_target_pairs={{0,112},{64,0},{16,64},{80,16},{32,80},{96,32},{48,96},{112,48},{1... | collective-permute-start | bytes 1572872 | tf_op jit(solution)/shard_map/ppermute | solution.py:34
  52.9 0.8 copy-start.3
  62.5 12.3 %copy-start = (bf16[1,256,1024]{2,1,0:T(8,128)(2,1)S(1)}, bf16[1,256,1024]{2,1,0:T(8,128)(2,1)}, u32[]{:S(2)}) copy-start(bf16[1,256,1024]{2,1,0:T(8,128)(2,1)} %param.4) | copy-start | bytes 1572868
  62.5 12.3 %copy-start.2 = (bf16[256,1024]{1,0:T(8,128)(2,1)S(1)}, bf16[256,1024]{1,0:T(8,128)(2,1)}, u32[]{:S(2)}) copy-start(bf16[256,1024]{1,0:T(8,128)(2,1)} %copy-done.1) | copy-start | bytes 1572868
  62.5 12.3 %collective-permute-start.7 = (bf16[8,2,32,1024]{3,2,1,0:T(8,128)(2,1)S(1)}, bf16[8,2,32,1024]{3,2,1,0:T(8,128)(2,1)S(1)}, u32[]{:S(2)}, u32[]{:S(2)}) collective-permute-start(bf16[8,2,32,1024]{3,2,1,0:T(8,128)(2,1)S(1)} %all-to-all-done.refs_0_), channel_id=1, source_target_pairs={{0,1},{1,0},{2,3},{3,2},{4,5},{5,4},{6,7},{7,6},{8,9},{9,8},{10,11... | collective-permute-start | bytes 3145736 | tf_op jit(solution)/shard_map/ppermute | solution.py:196
  68.3 11.6 %collective-permute-start.8 = (bf16[128,1024]{1,0:T(8,128)(2,1)S(1)}, bf16[128,1024]{1,0:T(8,128)(2,1)S(1)}, u32[]{:S(2)}, u32[]{:S(2)}) collective-permute-start(bf16[128,1024]{1,0:T(8,128)(2,1)S(1)} %slice.40), channel_id=1, source_target_pairs={{0,64},{64,16},{16,80},{80,32},{32,96},{96,48},{48,112},{112,0},{1... | collective-permute-start | bytes 786440 | tf_op jit(solution)/shard_map/ppermute | solution.py:34
  71.7 9.5 %collective-permute-start.9 = (bf16[128,1024]{1,0:T(8,128)(2,1)S(1)}, bf16[128,1024]{1,0:T(8,128)(2,1)S(1)}, u32[]{:S(2)}, u32[]{:S(2)}) collective-permute-start(bf16[128,1024]{1,0:T(8,128)(2,1)S(1)} %slice.41), channel_id=1, source_target_pairs={{0,112},{64,0},{16,64},{80,16},{32,80},{96,32},{48,96},{112,48},{1... | collective-permute-start | bytes 786440 | tf_op jit(solution)/shard_map/ppermute | solution.py:34
  74.8 1.0 copy-start.4

commit v5 on v0

v5 whole, which is shorter than its diff:
```python
import functools

import jax
import jax.numpy as jnp
from jax import lax
from jax.experimental import pallas as pl
from jax.experimental.pallas import tpu as pltpu
from jax.sharding import Mesh, PartitionSpec as P

BF16 = jnp.bfloat16
F32 = jnp.float32
AXES = ("x", "yl", "yh", "z", "core")
SIZES = (4, 2, 4, 8, 2)
NX, NL, NH, NZ, NC = SIZES
LANES = 128
MIB = 2**20

def dot(left, right):
    return lax.dot_general(left, right, (((1,), (1,)), ((), ())), preferred_element_type=F32)


def product_kernel(first, rows_ref, swapped_ref, blocks_ref, out_ref, left, right, left_sem, right_sem):
    yl, core = lax.axis_index("yl"), lax.axis_index("core")
    nz, _, rows, width = rows_ref.shape
    wide = rows // NX
    count = right.shape[0]
    lefts = [
        [
            pltpu.make_async_copy(ref.at[:, h], left.at[h, i], left_sem.at[h, i])
            for i, ref in enumerate((rows_ref, swapped_ref))
        ]
        for h in range(NL)
    ]
    rights = [
        pltpu.make_async_copy(blocks_ref.at[first * NL + n], right.at[n], right_sem.at[n])
        for n in range(count)
    ]
    for copy in [*lefts[0], rights[0], *lefts[1], *rights[1:]]:
        copy.start()
    for copy in [*lefts[0], *lefts[1]]:
        copy.wait()
    done = []
    for n in range(0, count, NL):
        total = None
        for half in range(NL):
            rights[n + half].wait()
            known = left[jnp.where(yl == half, 0, 1)].reshape(2 * nz * rows, width)
            term = dot(known, right[n + half])
            total = term if total is None else total + term
        done += [total[:, c : c + LANES] for c in range(0, total.shape[1], LANES)]
    for which in range(NC):
        target_core = core if which == 0 else 1 - core
        for zi in range(nz):
            for xi in range(NX):
                at = (which * nz + zi) * rows + xi * wide
                block = jnp.concatenate([d[at : at + wide] for d in done], axis=0)
                out_ref[(xi * nz + zi) * NC + target_core] = block.astype(BF16)


def product(mine, other, blocks, first, slots):
    nz, _, rows, width = mine.shape
    columns = blocks.shape[1]
    tall = slots * columns // LANES * rows // NX
    members = NX * nz * NC
    flops = 2 * 2 * nz * rows * width * columns * NL * slots
    anywhere = pl.BlockSpec(memory_space=pltpu.HBM)
    return pl.pallas_call(
        functools.partial(product_kernel, first),
        out_shape=jax.ShapeDtypeStruct((members, tall, LANES), BF16),
        in_specs=[anywhere] * 3,
        out_specs=pl.BlockSpec(memory_space=pltpu.VMEM),
        scratch_shapes=[
            pltpu.VMEM((NL, NC, nz, rows, width), BF16),
            pltpu.VMEM((NL * slots, columns, width), BF16),
            pltpu.SemaphoreType.DMA((NL, NC)),
            pltpu.SemaphoreType.DMA((NL * slots,)),
        ],
        compiler_params=pltpu.CompilerParams(vmem_limit_bytes=50 * MIB),
        cost_estimate=pl.CostEstimate(flops=flops, bytes_accessed=5 * MIB, transcendentals=0),
    )(mine, other, blocks)


def finish_kernel(*refs):
    out_ref, owner = refs[-1], 0
    wide, columns = out_ref.shape[2:]
    for ref in refs[:-1]:
        total = ref[0].astype(F32)
        for xi in range(1, NX):
            total = total + ref[xi].astype(F32)
        at = 0
        while at < total.shape[1]:
            for c in range(0, columns, LANES):
                out_ref[owner, :, :, c : c + LANES] = total[:, at : at + wide]
                at += wide
            owner += 1


def finish(terms, columns, wide):
    rest = terms[0].shape[0] // NX
    terms = [t.reshape(NX, rest, *t.shape[1:]) for t in terms]
    step = rest // 2
    return pl.pallas_call(
        finish_kernel,
        grid=(rest // step,),
        out_shape=jax.ShapeDtypeStruct((NH, rest, wide, columns), F32),
        in_specs=[
            pl.BlockSpec((NX, step, *t.shape[2:]), lambda i: (0, i, 0, 0)) for t in terms
        ],
        out_specs=pl.BlockSpec((NH, step, wide, columns), lambda i: (0, i, 0, 0)),
        cost_estimate=pl.CostEstimate(flops=2**19, bytes_accessed=3 * 2**19, transcendentals=0),
    )(*terms)


def body(valence_pairs, conduction_pairs, screening):
    yl = lax.axis_index("yl")
    _, second, plane_dev = valence_pairs.shape
    own = conduction_pairs[0]
    columns = own.shape[0]
    wide = second // (NX * NL)

    screened = (valence_pairs[0].astype(F32) * screening[None, :]).astype(BF16)
    screened = screened.reshape(NX, NL, wide, plane_dev)
    kept = jnp.where(yl == 0, screened[:, 0], screened[:, 1]).reshape(NX * wide, plane_dev)
    given = jnp.where(yl == 0, screened[:, 1], screened[:, 0]).reshape(NX * wide, plane_dev)
    taken = lax.ppermute(given, "yl", [(0, 1), (1, 0)])
    sent = jnp.broadcast_to(jnp.stack([kept, taken]), (NZ, NL, NX * wide, plane_dev))
    mine = lax.all_to_all(sent, "z", 0, 0, tiled=True)

    other = lax.ppermute(mine, "core", [(0, 1), (1, 0)])
    blocks = lax.all_gather(own, ("yh", "yl"), axis=0, tiled=False)

    terms = product(mine, other, blocks, 0, NH)
    terms = lax.all_to_all(terms, ("x", "z", "core"), 0, 0, tiled=True)
    out = finish([terms], columns, wide)
    return out.reshape(1, NH * NZ * NC, wide, columns)


def solution(mesh):
    fine = Mesh(mesh.devices.reshape(SIZES), AXES)
    pair, pw = ("yh", "z", "core"), ("x", "yl")
    placed = (P(pair, None, pw), P(pair, None, pw), P(pw))
    return jax.shard_map(
        body, mesh=fine, in_specs=placed, out_specs=P(pair, None, pw, None), check_vma=False
    )
```

time: 218 us -> 127 us (0.58)
  waiting for transfers between devices: 113 us -> 18.8 us
  starting transfers between devices: 0.01 us -> 9.81 us
  Pallas kernels: 0 us -> 8.79 us
  matrix products: 5.75 us -> 0 us
  blocking collectives: 80.3 us -> 75.3 us
  other arithmetic: 4.16 us -> 0.97 us
    all_gather x1, waiting for transfers between devices: 113 us -> 14.2 us  [body(): blocks = lax.all_gather(own, ('yh', 'yl'), axis=0, tiled=False)]
    ppermute x0 -> x2, starting transfers between devices: none -> 9.8 us  [the longest x1 5.77 us: body(): other = lax.ppermute(mine, 'core', [(0, 1), (1, 0)])]
    pallas_call x0 -> x2, Pallas kernels: none -> 8.79 us  [the longest x1 6.82 us: product(): pl.pallas_call(functools.partial(product_kernel, first), out_shape=jax.Sh...]
    dot_general x1 -> x0, matrix products: 5.75 us -> none  [contract(): lax.dot_general(piece.reshape(first * second, width), flat_right, (((1,),...]
    all_to_all x2, blocking collectives: 80.3 us -> 75.3 us  [the longest x1 39.5 us: body(): terms = lax.all_to_all(terms, ('x', 'z', 'core'), 0, 0, tiled=True)]
    ppermute x0 -> x2, waiting for transfers between devices: none -> 3.9 us  [the longest x1 2.26 us: body(): other = lax.ppermute(mine, 'core', [(0, 1), (1, 0)])]
    reduce_sum x1 -> x0, other arithmetic: 2.52 us -> none  [sent_and_summed(): return arrived.sum(axis=0)]
  transfers between devices with their start and end apart: 1 -> 3, of which waited for: 1 -> 3; matrix products, arithmetic and copies ran while one was open for 0% -> 1% of each run, Pallas kernels for 0% -> 0%
where the time goes in v5:
time: 127 us
  blocking collectives  75.3 us (59%)
  waiting for transfers between devices  18.8 us (15%)
  between operations  13.4 us (11%)
  starting transfers between devices  9.81 us (8%)
  Pallas kernels  8.79 us (7%)
    all_to_all x1, blocking collectives, body(): terms = lax.all_to_all(terms, ('x', 'z', 'core'), 0, 0, tiled=True)  39.5 us
    all_to_all x1, blocking collectives, body(): mine = lax.all_to_all(sent, 'z', 0, 0, tiled=True)  35.8 us
    all_gather x1, waiting for transfers between devices, body(): blocks = lax.all_gather(own, ('yh', 'yl'), axis=0, tiled=False)  14.2 us
    pallas_call x1, Pallas kernels, product(): pl.pallas_call(functools.partial(product_kernel, first), out_shape=jax.Sh...  6.82 us
    ppermute x1, starting transfers between devices, body(): other = lax.ppermute(mine, 'core', [(0, 1), (1, 0)])  5.77 us
    ppermute x1, starting transfers between devices, body(): taken = lax.ppermute(given, 'yl', [(0, 1), (1, 0)])  4.03 us
  transfers between devices with their start and end apart: 3, of which 3 were waited for; matrix products, arithmetic and copies ran while one was open for 1% of the time, Pallas kernels for 0%

profile of v5, /device:TPU:1, one launch (start us, length us, event | category | flops | bytes accessed | tf_op | source)
XLA Modules:
  0.0 127.2 jit_solution(8084649497125905524)
XLA Ops:
  6.5 0.0 all-gather.2.cloned.1.call-start
  6.5 0.7 all-gather.2.cloned.1.call-update
  7.3 0.9 fusion
  8.2 4.0 %collective-permute-start = (bf16[32,1024]{1,0:T(8,128)(2,1)S(1)}, bf16[32,1024]{1,0:T(8,128)(2,1)S(1)}, u32[]{:S(2)}, u32[]{:S(2)}) collective-permute-start(bf16[32,1024]{1,0:T(8,128)(2,1)S(1)} %get-tuple-element.6), channel_id=1, source_target_pairs={{0,64},{64,0},{1,65},{65,1},{2,66},{66,2},{3,67},{67,3},{4,68},{68... | collective-permute-start | bytes 196616 | tf_op jit(solution)/shard_map/ppermute | solution.py:125
  12.3 1.6 %collective-permute-done = bf16[32,1024]{1,0:T(8,128)(2,1)S(1)} collective-permute-done((bf16[32,1024]{1,0:T(8,128)(2,1)S(1)}, bf16[32,1024]{1,0:T(8,128)(2,1)S(1)}, u32[]{:S(2)}, u32[]{:S(2)}) %collective-permute-start) | collective-permute-done | bytes 65568 | tf_op jit(solution)/shard_map/ppermute | solution.py:125
  13.9 0.1 broadcast_in_dim.4
  14.0 35.8 %all_to_all.10.rows_ref = bf16[8,2,32,1024]{3,2,1,0:T(8,128)(2,1)S(1)} all-to-all(bf16[8,2,32,1024]{3,2,1,0:T(8,128)(2,1)S(1)} %broadcast_in_dim.4), channel_id=1, replica_groups=mesh['x'=4,'yl'=2,'yh'=4,'z'=8,'core'=2] {'z'}, dimensions={0} | all-to-all | bytes 2097152 | tf_op jit(solution)/shard_map/all_to_all | solution.py:127
  49.9 5.8 %collective-permute-start.1 = (bf16[8,2,32,1024]{3,2,1,0:T(8,128)(2,1)S(1)}, bf16[8,2,32,1024]{3,2,1,0:T(8,128)(2,1)S(1)}, u32[]{:S(2)}, u32[]{:S(2)}) collective-permute-start(bf16[8,2,32,1024]{3,2,1,0:T(8,128)(2,1)S(1)} %all_to_all.10.rows_ref), channel_id=1, source_target_pairs={{0,1},{1,0},{2,3},{3,2},{4,5},{5,4},{6,7},{7,6},{8,9},{9,8},{10,11... | collective-permute-start | bytes 3145736 | tf_op jit(solution)/shard_map/ppermute | solution.py:129
  55.6 2.3 %collective-permute-done.1.swapped_ref = bf16[8,2,32,1024]{3,2,1,0:T(8,128)(2,1)S(1)} collective-permute-done((bf16[8,2,32,1024]{3,2,1,0:T(8,128)(2,1)S(1)}, bf16[8,2,32,1024]{3,2,1,0:T(8,128)(2,1)S(1)}, u32[]{:S(2)}, u32[]{:S(2)}) %collective-permute-start.1) | collective-permute-done | bytes 1048608 | tf_op jit(solution)/shard_map/ppermute | solution.py:129
  57.9 14.2 %all-gather.2.cloned.1.call-done.blocks_ref = bf16[8,256,1024]{2,1,0:T(8,128)(2,1)} async-done(((bf16[1,256,1024]{2,1,0:T(8,128)(2,1)}), bf16[8,256,1024]{2,1,0:T(8,128)(2,1)}) %all-gather.2.cloned.1.call-update) | async-done | bytes 4194320 | tf_op jit(solution)/shard_map/all_gather | solution.py:130
  72.1 6.8 %shard_map.37 = bf16[64,64,128]{2,1,0:T(8,128)(2,1)S(1)} custom-call(bf16[8,2,32,1024]{3,2,1,0:T(8,128)(2,1)S(1)} %all_to_all.10.rows_ref, bf16[8,2,32,1024]{3,2,1,0:T(8,128)(2,1)S(1)} %collective-permute-done.1.swapped_ref, bf16[8,256,1024]{2,1,0:T(8,128)(2,1)} %all-gather.2.cloned.1.call-done.blocks_ref), custom_call_target="tpu_custom_call" | custom-call | flops 2147483648 | bytes 5242880 | tf_op jit(solution)/shard_map/pallas_call | solution.py:67
  78.9 39.5 %all_to_all.11 = bf16[64,64,128]{2,1,0:T(8,128)(2,1)} all-to-all(bf16[64,64,128]{2,1,0:T(8,128)(2,1)S(1)} %shard_map.37), channel_id=1, replica_groups=mesh['x'=4,'yl'=2,'yh'=4,'z'=8,'core'=2] {'x','z','core'}, dimensions={0} | all-to-all | bytes 2097152 | tf_op jit(solution)/shard_map/all_to_all | solution.py:133
  118.4 2.0 %shard_map.38 = f32[4,16,8,256]{3,2,1,0:T(8,128)} custom-call(bf16[4,16,64,128]{3,2,1,0:T(8,128)(2,1)} %bitcast.9), custom_call_target="tpu_custom_call" | custom-call | flops 524288 | bytes 1572864 | tf_op jit(solution)/shard_map/pallas_call | solution.py:102
  (2 shorter events, 0.0 us)
Async XLA Ops:
  6.5 65.6 %all-gather.2.cloned.1.call-start = ((), (), s32[]{:S(2)}) async-start(), calls=%async_computation.2 | async-start | bytes 4718592 | tf_op jit(solution)/shard_map/all_gather | solution.py:130
  8.2 5.7 %collective-permute-start = (bf16[32,1024]{1,0:T(8,128)(2,1)S(1)}, bf16[32,1024]{1,0:T(8,128)(2,1)S(1)}, u32[]{:S(2)}, u32[]{:S(2)}) collective-permute-start(bf16[32,1024]{1,0:T(8,128)(2,1)S(1)} %get-tuple-element.6), channel_id=1, source_target_pairs={{0,64},{64,0},{1,65},{65,1},{2,66},{66,2},{3,67},{67,3},{4,68},{68... | collective-permute-start | bytes 196616 | tf_op jit(solution)/shard_map/ppermute | solution.py:125
  49.9 8.0 %collective-permute-start.1 = (bf16[8,2,32,1024]{3,2,1,0:T(8,128)(2,1)S(1)}, bf16[8,2,32,1024]{3,2,1,0:T(8,128)(2,1)S(1)}, u32[]{:S(2)}, u32[]{:S(2)}) collective-permute-start(bf16[8,2,32,1024]{3,2,1,0:T(8,128)(2,1)S(1)} %all_to_all.10.rows_ref), channel_id=1, source_target_pairs={{0,1},{1,0},{2,3},{3,2},{4,5},{5,4},{6,7},{7,6},{8,9},{9,8},{10,11... | collective-permute-start | bytes 3145736 | tf_op jit(solution)/shard_map/ppermute | solution.py:129
Sparse Core Ops, SparseCore 0:
  9.4 62.6 all-gather.1

commit v6 on v4

--- a/solution.py
+++ b/solution.py
@@ -40,21 +40,17 @@
 
 def product_kernel(names, slots, ignored, at_row, *refs):
     count = len(names)
-    rows_refs, piece_refs = refs[:2], refs[2 : 2 + count]
-    out_ref, left, right, held, left_sem, right_sem, out_sem = refs[2 + count + ignored :]
-    yl, core = lax.axis_index("yl"), lax.axis_index("core")
-    nz, _, rows, width = rows_refs[0].shape
+    rows_ref, piece_refs = refs[0], refs[1 : 1 + count]
+    out_ref, left, right, held, left_sem, right_sem, out_sem = refs[1 + count + ignored :]
+    yl = lax.axis_index("yl")
+    nz, _, rows, width = rows_ref.shape
     wide = rows // NX
     blocks = []
     for name, _ in names:
         if name not in blocks:
             blocks.append(name)
     lefts = [
-        [
-            pltpu.make_async_copy(rows_refs[i].at[:, h], left.at[h, i], left_sem.at[h, i])
-            for i in range(2)
-        ]
-        for h in range(2)
+        [pltpu.make_async_copy(rows_ref.at[:, h], left.at[h], left_sem.at[h])] for h in range(2)
     ]
     rights = {name: [] for name in blocks}
     for n, (name, piece) in enumerate(names):
@@ -88,22 +84,20 @@
             where = blocks.index(even)
             if even != odd:
                 where = jnp.where(yl == 0, where, blocks.index(odd))
-            term = dot(left[half].reshape(2 * nz * rows, width), right[where])
+            term = dot(left[half].reshape(nz * rows, width), right[where])
             total = term if total is None else total + term
         done += [total[:, c : c + LANES] for c in range(0, total.shape[1], LANES)]
-    for which in range(2):
-        target_core = core if which == 0 else 1 - core
-        for zi in range(nz):
-            for xi in range(NX):
-                at = (which * nz + zi) * rows + xi * wide
-                block = jnp.concatenate([d[at : at + wide] for d in done], axis=0)
-                held[(xi * nz + zi) * NC + target_core] = block.astype(BF16)
+    for owner in range(nz):
+        for xi in range(NX):
+            at = owner * rows + xi * wide
+            block = jnp.concatenate([d[at : at + wide] for d in done], axis=0)
+            held[xi * nz + owner] = block.astype(BF16)
     copy = pltpu.make_async_copy(held, out_ref.at[:, pl.ds(at_row, held.shape[1])], out_sem)
     copy.start()
     copy.wait()
 
 
-def product(mine, other, pieces, slots, at_row, height, unread=(), begun=None):
+def product(mine, pieces, slots, at_row, height, unread=(), begun=None):
     nz, _, rows, width = mine.shape
     wide = rows // NX
     names = tuple(piece[:2] for piece in pieces)
@@ -111,10 +105,10 @@
     if pieces[-1][1] is None:
         columns = pieces[-1][2].shape[0]
     tall = len(slots) * columns // LANES * wide
-    members = NX * nz * NC
-    flops = 2 * 2 * nz * rows * width * columns * 2 * len(slots)
+    members = NX * nz
+    flops = 2 * nz * rows * width * columns * 2 * len(slots)
     anywhere = pl.BlockSpec(memory_space=pltpu.HBM)
-    operands = [mine, other, *[piece[2] for piece in pieces], *unread]
+    operands = [mine, *[piece[2] for piece in pieces], *unread]
     ignored, aliases = len(unread), {}
     if begun is not None:
         aliases = {len(operands): 0}
@@ -126,15 +120,15 @@
         in_specs=[anywhere] * len(operands),
         out_specs=anywhere,
         scratch_shapes=[
-            pltpu.VMEM((2, 2, nz, rows, width), BF16),
+            pltpu.VMEM((2, nz, rows, width), BF16),
             pltpu.VMEM((len({n for n, _ in names}), columns, width), BF16),
             pltpu.VMEM((members, tall, LANES), BF16),
-            pltpu.SemaphoreType.DMA((2, 2)),
+            pltpu.SemaphoreType.DMA((2,)),
             pltpu.SemaphoreType.DMA((len(names),)),
             pltpu.SemaphoreType.DMA,
         ],
         input_output_aliases=aliases,
-        compiler_params=pltpu.CompilerParams(vmem_limit_bytes=40 * MIB),
+        compiler_params=pltpu.CompilerParams(vmem_limit_bytes=60 * MIB),
         cost_estimate=pl.CostEstimate(flops=flops, bytes_accessed=5 * MIB, transcendentals=0),
     )(*operands)
 
@@ -184,25 +178,21 @@
     given = jnp.where(yl == 0, screened[:, 1], screened[:, 0]).reshape(NX * wide, plane_dev)
     taken = lax.ppermute(given, "yl", [(0, 1), (1, 0)])
     r1, l1 = around(own, 1), around(own, -1)
-    sent = jnp.broadcast_to(jnp.stack([kept, taken]), (NZ, NL, NX * wide, plane_dev))
-    sent, *rows = lax.optimization_barrier((sent, r1[:16], l1[:16]))
-    mine = lax.all_to_all(sent, "z", 0, 0, tiled=True)
+    sent = jnp.broadcast_to(jnp.stack([kept, taken]), (NZ * NC, NL, NX * wide, plane_dev))
+    mine = lax.all_to_all(sent, ("z", "core"), 0, 0, tiled=True)
 
     r2, l2 = around(r1, 1), around(l1, -1)
     r3, l3 = around(r2, 1), around(l2, -1)
     far = around(r3[:cut], 1), around(l3[cut:], -1)
-
-    mine, *more = lax.optimization_barrier((mine, r3[:16], l3[:16]))
-    other = lax.ppermute(mine, "core", [(0, 1), (1, 0)])
 
     per_slot = columns // LANES * wide
     height = len(SLOTS) * per_slot
     near = ((OWN, own), (R1, r1), (L1, l1), (R2, r2), (L2, l2), (R3, r3), (L3, l3))
     terms = product(
-        mine, other, [(n, None, b) for n, b in near], SLOTS[:3], 0, height, rows + more
+        mine, [(n, None, b) for n, b in near], SLOTS[:3], 0, height
     )
     terms = product(
-        mine, other,
+        mine,
         [(R3, None, r3), (L3, None, l3), (FAR, 0, far[0]), (FAR, 1, far[1])],
         SLOTS[3:], 3 * per_slot, height, (), terms,
     )

time: 125 us -> 133 us (1.064)
  waiting for transfers between devices: 22.7 us -> 29.7 us
  starting transfers between devices: 48.8 us -> 42.9 us
  Pallas kernels: 7.22 us -> 12.3 us
  blocking collectives: 39.2 us -> 41.2 us
    ppermute x8, waiting for transfers between devices: 17.9 us -> 28 us  [around(): return lax.ppermute(block, ('yl', 'yh'), pairs)]
    ppermute x1 -> x0, starting transfers between devices: 5.7 us -> none  [body(): other = lax.ppermute(mine, 'core', [(0, 1), (1, 0)])]
    pallas_call x2, Pallas kernels: 5.25 us -> 10.3 us  [product(): pl.pallas_call(functools.partial(product_kernel, names, slots, ignored, a...]
    ppermute x1, waiting for transfers between devices: 4.76 us -> 1.64 us  [body(): taken = lax.ppermute(given, 'yl', [(0, 1), (1, 0)])]
    ppermute x1, starting transfers between devices: 1.92 us -> 4.03 us  [body(): taken = lax.ppermute(given, 'yl', [(0, 1), (1, 0)])]
    all_to_all x1, blocking collectives: 39.2 us -> 41.2 us  [body(): terms = lax.all_to_all(terms, ('x', 'z', 'core'), 0, 0, tiled=True)]
    slice x2, local copies, waits for them, and re-layouts: 0.04 us -> 1.57 us  [body(): far = (around(r3[:cut], 1), around(l3[cut:], -1))]
    all_to_all x1, starting transfers between devices: 13.9 us -> 12.4 us  [body(): mine = lax.all_to_all(sent, ('z', 'core'), 0, 0, tiled=True)]
  transfers between devices with their start and end apart: 11 -> 10, of which waited for: 5 -> 4; matrix products, arithmetic and copies ran while one was open for 1% -> 1% of each run, Pallas kernels for 3% -> 5%
where the time goes in v6:
time: 133 us; the launch traced here: 132 us
  starting transfers between devices  42.9 us (32%)
  blocking collectives  41.2 us (31%)
  waiting for transfers between devices  29.7 us (22%)
  Pallas kernels  12.3 us (9%)
  local copies, waits for them, and re-layouts  5.22 us (4%)
    all_to_all x1, blocking collectives, body(): terms = lax.all_to_all(terms, ('x', 'z', 'core'), 0, 0, tiled=True)  41.2 us
    ppermute x8, waiting for transfers between devices, around(): return lax.ppermute(block, ('yl', 'yh'), pairs)  28 us
    ppermute x8, starting transfers between devices, around(): return lax.ppermute(block, ('yl', 'yh'), pairs)  26.5 us
    all_to_all x1, starting transfers between devices, body(): mine = lax.all_to_all(sent, ('z', 'core'), 0, 0, tiled=True)  12.4 us
    pallas_call x2, Pallas kernels, product(): pl.pallas_call(functools.partial(product_kernel, names, slots, ignored, a...  10.3 us
    ppermute x1, starting transfers between devices, body(): taken = lax.ppermute(given, 'yl', [(0, 1), (1, 0)])  4.03 us
  transfers between devices with their start and end apart: 10, of which 4 were waited for; matrix products, arithmetic and copies ran while one was open for 1% of the time, Pallas kernels for 5%

profile of v6, /device:TPU:1, one launch (start us, length us, event | category | flops | bytes accessed | tf_op | source)
XLA Modules:
  0.0 132.5 jit_solution(3375140095459698937)
XLA Ops:
  0.0 0.9 fusion
  1.0 4.0 %collective-permute-start = (bf16[32,1024]{1,0:T(8,128)(2,1)S(1)}, bf16[32,1024]{1,0:T(8,128)(2,1)S(1)}, u32[]{:S(2)}, u32[]{:S(2)}) collective-permute-start(bf16[32,1024]{1,0:T(8,128)(2,1)S(1)} %get-tuple-element.6), channel_id=1, source_target_pairs={{0,64},{64,0},{1,65},{65,1},{2,66},{66,2},{3,67},{67,3},{4,68},{68... | collective-permute-start | bytes 196616 | tf_op jit(solution)/shard_map/ppermute | solution.py:179
  5.0 1.6 %collective-permute-done = bf16[32,1024]{1,0:T(8,128)(2,1)S(1)} collective-permute-done((bf16[32,1024]{1,0:T(8,128)(2,1)S(1)}, bf16[32,1024]{1,0:T(8,128)(2,1)S(1)}, u32[]{:S(2)}, u32[]{:S(2)}) %collective-permute-start) | collective-permute-done | bytes 65568 | tf_op jit(solution)/shard_map/ppermute | solution.py:179
  6.7 1.6 %broadcast_in_dim.4 = bf16[16,2,32,1024]{3,2,1,0:T(8,128)(2,1)} broadcast(bf16[2,32,1024]{2,1,0:T(8,128)(2,1)S(1)} %pad_maximum_fusion), dimensions={1,2,3} | broadcast | bytes 2228224 | tf_op jit(solution)/shard_map/broadcast_in_dim | solution.py:181
  8.3 12.4 %all-to-all-start = ((bf16[16,2,32,1024]{3,2,1,0:T(8,128)(2,1)}), bf16[16,2,32,1024]{3,2,1,0:T(8,128)(2,1)S(1)}, u32[]{:S(2)}, u32[]{:S(2)}) async-start(bf16[16,2,32,1024]{3,2,1,0:T(8,128)(2,1)} %broadcast_in_dim.4), calls=%async_computation | async-start | bytes 4194304 | tf_op jit(solution)/shard_map/all_to_all | solution.py:182
  20.7 3.2 %collective-permute-start.1 = (bf16[256,1024]{1,0:T(8,128)(2,1)S(1)}, bf16[256,1024]{1,0:T(8,128)(2,1)S(1)}, u32[]{:S(2)}, u32[]{:S(2)}) collective-permute-start(bf16[256,1024]{1,0:T(8,128)(2,1)S(1)} %bitcast.12), channel_id=1, source_target_pairs={{0,64},{64,16},{16,80},{80,32},{32,96},{96,48},{48,112},{112,0},{1... | collective-permute-start | bytes 1572872 | tf_op jit(solution)/shard_map/ppermute | solution.py:34
  23.9 3.8 %collective-permute-start.4 = (bf16[256,1024]{1,0:T(8,128)(2,1)S(1)}, bf16[256,1024]{1,0:T(8,128)(2,1)S(1)}, u32[]{:S(2)}, u32[]{:S(2)}) collective-permute-start(bf16[256,1024]{1,0:T(8,128)(2,1)S(1)} %bitcast.13), channel_id=1, source_target_pairs={{0,112},{64,0},{16,64},{80,16},{32,80},{96,32},{48,96},{112,48},{1... | collective-permute-start | bytes 1572872 | tf_op jit(solution)/shard_map/ppermute | solution.py:34
  27.8 10.2 %collective-permute-done.1.refs_2_ = bf16[256,1024]{1,0:T(8,128)(2,1)S(1)} collective-permute-done((bf16[256,1024]{1,0:T(8,128)(2,1)S(1)}, bf16[256,1024]{1,0:T(8,128)(2,1)S(1)}, u32[]{:S(2)}, u32[]{:S(2)}) %collective-permute-start.1) | collective-permute-done | bytes 524320 | tf_op jit(solution)/shard_map/ppermute | solution.py:34
  38.0 1.9 %collective-permute-start.2 = (bf16[256,1024]{1,0:T(8,128)(2,1)S(1)}, bf16[256,1024]{1,0:T(8,128)(2,1)S(1)}, u32[]{:S(2)}, u32[]{:S(2)}) collective-permute-start(bf16[256,1024]{1,0:T(8,128)(2,1)S(1)} %collective-permute-done.1.refs_2_), channel_id=1, source_target_pairs={{0,64},{64,16},{16,80},{80,32},{32,96},{96,48},{48,112},{112,0},{1... | collective-permute-start | bytes 1572872 | tf_op jit(solution)/shard_map/ppermute | solution.py:34
  39.9 4.6 %collective-permute-start.5 = (bf16[256,1024]{1,0:T(8,128)(2,1)S(1)}, bf16[256,1024]{1,0:T(8,128)(2,1)S(1)}, u32[]{:S(2)}, u32[]{:S(2)}) collective-permute-start(bf16[256,1024]{1,0:T(8,128)(2,1)S(1)} %collective-permute-done.4.refs_3_), channel_id=1, source_target_pairs={{0,112},{64,0},{16,64},{80,16},{32,80},{96,32},{48,96},{112,48},{1... | collective-permute-start | bytes 1572872 | tf_op jit(solution)/shard_map/ppermute | solution.py:34
  44.5 9.4 %collective-permute-done.2.refs_4_ = bf16[256,1024]{1,0:T(8,128)(2,1)S(1)} collective-permute-done((bf16[256,1024]{1,0:T(8,128)(2,1)S(1)}, bf16[256,1024]{1,0:T(8,128)(2,1)S(1)}, u32[]{:S(2)}, u32[]{:S(2)}) %collective-permute-start.2) | collective-permute-done | bytes 524320 | tf_op jit(solution)/shard_map/ppermute | solution.py:34
  53.9 1.9 %collective-permute-start.3 = (bf16[256,1024]{1,0:T(8,128)(2,1)S(1)}, bf16[256,1024]{1,0:T(8,128)(2,1)S(1)}, u32[]{:S(2)}, u32[]{:S(2)}) collective-permute-start(bf16[256,1024]{1,0:T(8,128)(2,1)S(1)} %collective-permute-done.2.refs_4_), channel_id=1, source_target_pairs={{0,64},{64,16},{16,80},{80,32},{32,96},{96,48},{48,112},{112,0},{1... | collective-permute-start | bytes 1572872 | tf_op jit(solution)/shard_map/ppermute | solution.py:34
  55.8 4.6 %collective-permute-start.6 = (bf16[256,1024]{1,0:T(8,128)(2,1)S(1)}, bf16[256,1024]{1,0:T(8,128)(2,1)S(1)}, u32[]{:S(2)}, u32[]{:S(2)}) collective-permute-start(bf16[256,1024]{1,0:T(8,128)(2,1)S(1)} %collective-permute-done.5.refs_5_), channel_id=1, source_target_pairs={{0,112},{64,0},{16,64},{80,16},{32,80},{96,32},{48,96},{112,48},{1... | collective-permute-start | bytes 1572872 | tf_op jit(solution)/shard_map/ppermute | solution.py:34
  60.4 8.4 %collective-permute-done.3.refs_6_.refs_1_ = bf16[256,1024]{1,0:T(8,128)(2,1)S(1)} collective-permute-done((bf16[256,1024]{1,0:T(8,128)(2,1)S(1)}, bf16[256,1024]{1,0:T(8,128)(2,1)S(1)}, u32[]{:S(2)}, u32[]{:S(2)}) %collective-permute-start.3) | collective-permute-done | bytes 524320 | tf_op jit(solution)/shard_map/ppermute | solution.py:34
  68.8 0.8 slice.20
  69.6 1.9 %collective-permute-start.7 = (bf16[128,1024]{1,0:T(8,128)(2,1)}, bf16[128,1024]{1,0:T(8,128)(2,1)S(1)}, u32[]{:S(2)}, u32[]{:S(2)}) collective-permute-start(bf16[128,1024]{1,0:T(8,128)(2,1)} %slice.20), channel_id=1, source_target_pairs={{0,64},{64,16},{16,80},{80,32},{32,96},{96,48},{48,112},{112,0},{1... | collective-permute-start | bytes 786440 | tf_op jit(solution)/shard_map/ppermute | solution.py:34
  71.6 0.8 slice.21
  72.4 4.6 %collective-permute-start.8 = (bf16[128,1024]{1,0:T(8,128)(2,1)}, bf16[128,1024]{1,0:T(8,128)(2,1)}, u32[]{:S(2)}, u32[]{:S(2)}) collective-permute-start(bf16[128,1024]{1,0:T(8,128)(2,1)} %slice.21), channel_id=1, source_target_pairs={{0,112},{64,0},{16,64},{80,16},{32,80},{96,32},{48,96},{112,48},{1... | collective-permute-start | bytes 786440 | tf_op jit(solution)/shard_map/ppermute | solution.py:34
  77.0 1.3 %copy-done = bf16[16,2,32,1024]{3,2,1,0:T(8,128)(2,1)} copy-done((bf16[16,2,32,1024]{3,2,1,0:T(8,128)(2,1)}, bf16[16,2,32,1024]{3,2,1,0:T(8,128)(2,1)S(1)}, u32[]{:S(2)}) %copy-start) | copy-done | bytes 2097176
  78.3 6.8 %shard_map.37.refs_5_ = bf16[64,64,128]{2,1,0:T(8,128)(2,1)} custom-call(bf16[16,2,32,1024]{3,2,1,0:T(8,128)(2,1)} %copy-done, bf16[256,1024]{1,0:T(8,128)(2,1)} %bitcast.11, bf16[256,1024]{1,0:T(8,128)(2,1)} %copy-done.4, bf16[256,1024]{1,0:T(8,128)(2,1)} %copy-done.5, bf16[256,1024]{1,0:T(8,128)(2,1)} %copy-done.6, bf16[256,1024]{1,0:T(8,128)(2,1)} %copy-done.7, ...), custom_call_target="tpu_custom_call" | custom-call | flops 1610612736 | bytes 5242880 | tf_op jit(solution)/shard_map/pallas_call | solution.py:117
  85.1 0.7 copy-done.8
  85.8 3.5 %shard_map.38 = bf16[64,64,128]{2,1,0:T(8,128)(2,1)} custom-call(bf16[16,2,32,1024]{3,2,1,0:T(8,128)(2,1)} %copy-done, bf16[256,1024]{1,0:T(8,128)(2,1)} %copy-done.1, bf16[256,1024]{1,0:T(8,128)(2,1)} %copy-done.2, bf16[128,1024]{1,0:T(8,128)(2,1)} %copy-done.8, bf16[128,1024]{1,0:T(8,128)(2,1)} %collective-permute-done.8.refs_4_, ...), custom_call_target="tpu_custom_call", output_to_operand_aliasing={{}: (5, {})} | custom-call | flops 536870912 | bytes 5242880 | tf_op jit(solution)/shard_map/pallas_call | solution.py:117
  89.4 41.2 %all_to_all.10 = bf16[64,64,128]{2,1,0:T(8,128)(2,1)} all-to-all(bf16[64,64,128]{2,1,0:T(8,128)(2,1)} %shard_map.38), channel_id=1, replica_groups=mesh['x'=4,'yl'=2,'yh'=4,'z'=8,'core'=2] {'x','z','core'}, dimensions={0} | all-to-all | bytes 2097152 | tf_op jit(solution)/shard_map/all_to_all | solution.py:199
  130.5 2.0 %shard_map.39 = f32[4,16,8,256]{3,2,1,0:T(8,128)} custom-call(bf16[4,16,64,128]{3,2,1,0:T(8,128)(2,1)} %bitcast.10), custom_call_target="tpu_custom_call" | custom-call | flops 524288 | bytes 1572864 | tf_op jit(solution)/shard_map/pallas_call | solution.py:157
  (24 shorter events, 0.1 us)
Async XLA Ops:
  1.0 5.7 %collective-permute-start = (bf16[32,1024]{1,0:T(8,128)(2,1)S(1)}, bf16[32,1024]{1,0:T(8,128)(2,1)S(1)}, u32[]{:S(2)}, u32[]{:S(2)}) collective-permute-start(bf16[32,1024]{1,0:T(8,128)(2,1)S(1)} %get-tuple-element.6), channel_id=1, source_target_pairs={{0,64},{64,0},{1,65},{65,1},{2,66},{66,2},{3,67},{67,3},{4,68},{68... | collective-permute-start | bytes 196616 | tf_op jit(solution)/shard_map/ppermute | solution.py:179
  8.3 12.4 %copy-start.3 = (bf16[1,256,1024]{2,1,0:T(8,128)(2,1)S(1)}, bf16[1,256,1024]{2,1,0:T(8,128)(2,1)}, u32[]{:S(2)}) copy-start(bf16[1,256,1024]{2,1,0:T(8,128)(2,1)} %param.4) | copy-start | bytes 1572868
  8.3 68.7 %all-to-all-start = ((bf16[16,2,32,1024]{3,2,1,0:T(8,128)(2,1)}), bf16[16,2,32,1024]{3,2,1,0:T(8,128)(2,1)S(1)}, u32[]{:S(2)}, u32[]{:S(2)}) async-start(bf16[16,2,32,1024]{3,2,1,0:T(8,128)(2,1)} %broadcast_in_dim.4), calls=%async_computation | async-start | bytes 4194304 | tf_op jit(solution)/shard_map/all_to_all | solution.py:182
  20.7 17.3 %collective-permute-start.1 = (bf16[256,1024]{1,0:T(8,128)(2,1)S(1)}, bf16[256,1024]{1,0:T(8,128)(2,1)S(1)}, u32[]{:S(2)}, u32[]{:S(2)}) collective-permute-start(bf16[256,1024]{1,0:T(8,128)(2,1)S(1)} %bitcast.12), channel_id=1, source_target_pairs={{0,64},{64,16},{16,80},{80,32},{32,96},{96,48},{48,112},{112,0},{1... | collective-permute-start | bytes 1572872 | tf_op jit(solution)/shard_map/ppermute | solution.py:34
  23.9 16.0 %collective-permute-start.4 = (bf16[256,1024]{1,0:T(8,128)(2,1)S(1)}, bf16[256,1024]{1,0:T(8,128)(2,1)S(1)}, u32[]{:S(2)}, u32[]{:S(2)}) collective-permute-start(bf16[256,1024]{1,0:T(8,128)(2,1)S(1)} %bitcast.13), channel_id=1, source_target_pairs={{0,112},{64,0},{16,64},{80,16},{32,80},{96,32},{48,96},{112,48},{1... | collective-permute-start | bytes 1572872 | tf_op jit(solution)/shard_map/ppermute | solution.py:34
  38.0 17.8 %copy-start.4 = (bf16[256,1024]{1,0:T(8,128)(2,1)}, bf16[256,1024]{1,0:T(8,128)(2,1)S(1)}, u32[]{:S(2)}) copy-start(bf16[256,1024]{1,0:T(8,128)(2,1)S(1)} %collective-permute-done.1.refs_2_) | copy-start | bytes 1572868
  38.0 15.9 %collective-permute-start.2 = (bf16[256,1024]{1,0:T(8,128)(2,1)S(1)}, bf16[256,1024]{1,0:T(8,128)(2,1)S(1)}, u32[]{:S(2)}, u32[]{:S(2)}) collective-permute-start(bf16[256,1024]{1,0:T(8,128)(2,1)S(1)} %collective-permute-done.1.refs_2_), channel_id=1, source_target_pairs={{0,64},{64,16},{16,80},{80,32},{32,96},{96,48},{48,112},{112,0},{1... | collective-permute-start | bytes 1572872 | tf_op jit(solution)/shard_map/ppermute | solution.py:34
  39.9 20.5 %copy-start.5 = (bf16[256,1024]{1,0:T(8,128)(2,1)}, bf16[256,1024]{1,0:T(8,128)(2,1)S(1)}, u32[]{:S(2)}) copy-start(bf16[256,1024]{1,0:T(8,128)(2,1)S(1)} %collective-permute-done.4.refs_3_) | copy-start | bytes 1572868
  39.9 15.9 %collective-permute-start.5 = (bf16[256,1024]{1,0:T(8,128)(2,1)S(1)}, bf16[256,1024]{1,0:T(8,128)(2,1)S(1)}, u32[]{:S(2)}, u32[]{:S(2)}) collective-permute-start(bf16[256,1024]{1,0:T(8,128)(2,1)S(1)} %collective-permute-done.4.refs_3_), channel_id=1, source_target_pairs={{0,112},{64,0},{16,64},{80,16},{32,80},{96,32},{48,96},{112,48},{1... | collective-permute-start | bytes 1572872 | tf_op jit(solution)/shard_map/ppermute | solution.py:34
  53.9 6.5 %copy-start.6 = (bf16[256,1024]{1,0:T(8,128)(2,1)}, bf16[256,1024]{1,0:T(8,128)(2,1)S(1)}, u32[]{:S(2)}) copy-start(bf16[256,1024]{1,0:T(8,128)(2,1)S(1)} %collective-permute-done.2.refs_4_) | copy-start | bytes 1572868
  53.9 15.0 %collective-permute-start.3 = (bf16[256,1024]{1,0:T(8,128)(2,1)S(1)}, bf16[256,1024]{1,0:T(8,128)(2,1)S(1)}, u32[]{:S(2)}, u32[]{:S(2)}) collective-permute-start(bf16[256,1024]{1,0:T(8,128)(2,1)S(1)} %collective-permute-done.2.refs_4_), channel_id=1, source_target_pairs={{0,64},{64,16},{16,80},{80,32},{32,96},{96,48},{48,112},{112,0},{1... | collective-permute-start | bytes 1572872 | tf_op jit(solution)/shard_map/ppermute | solution.py:34
  55.8 16.5 %copy-start.7 = (bf16[256,1024]{1,0:T(8,128)(2,1)}, bf16[256,1024]{1,0:T(8,128)(2,1)S(1)}, u32[]{:S(2)}) copy-start(bf16[256,1024]{1,0:T(8,128)(2,1)S(1)} %collective-permute-done.5.refs_5_) | copy-start | bytes 1572868
  55.8 15.7 %collective-permute-start.6 = (bf16[256,1024]{1,0:T(8,128)(2,1)S(1)}, bf16[256,1024]{1,0:T(8,128)(2,1)S(1)}, u32[]{:S(2)}, u32[]{:S(2)}) collective-permute-start(bf16[256,1024]{1,0:T(8,128)(2,1)S(1)} %collective-permute-done.5.refs_5_), channel_id=1, source_target_pairs={{0,112},{64,0},{16,64},{80,16},{32,80},{96,32},{48,96},{112,48},{1... | collective-permute-start | bytes 1572872 | tf_op jit(solution)/shard_map/ppermute | solution.py:34
  68.8 8.1 %copy-start.1 = (bf16[256,1024]{1,0:T(8,128)(2,1)}, bf16[256,1024]{1,0:T(8,128)(2,1)S(1)}, u32[]{:S(2)}) copy-start(bf16[256,1024]{1,0:T(8,128)(2,1)S(1)} %collective-permute-done.3.refs_6_.refs_1_) | copy-start | bytes 1572868
  69.6 15.5 %collective-permute-start.7 = (bf16[128,1024]{1,0:T(8,128)(2,1)}, bf16[128,1024]{1,0:T(8,128)(2,1)S(1)}, u32[]{:S(2)}, u32[]{:S(2)}) collective-permute-start(bf16[128,1024]{1,0:T(8,128)(2,1)} %slice.20), channel_id=1, source_target_pairs={{0,64},{64,16},{16,80},{80,32},{32,96},{96,48},{48,112},{112,0},{1... | collective-permute-start | bytes 786440 | tf_op jit(solution)/shard_map/ppermute | solution.py:34
  71.6 5.4 %copy-start.2 = (bf16[256,1024]{1,0:T(8,128)(2,1)}, bf16[256,1024]{1,0:T(8,128)(2,1)S(1)}, u32[]{:S(2)}) copy-start(bf16[256,1024]{1,0:T(8,128)(2,1)S(1)} %collective-permute-done.6.refs_7_.refs_2_) | copy-start | bytes 1572868
  72.4 12.8 %collective-permute-start.8 = (bf16[128,1024]{1,0:T(8,128)(2,1)}, bf16[128,1024]{1,0:T(8,128)(2,1)}, u32[]{:S(2)}, u32[]{:S(2)}) collective-permute-start(bf16[128,1024]{1,0:T(8,128)(2,1)} %slice.21), channel_id=1, source_target_pairs={{0,112},{64,0},{16,64},{80,16},{32,80},{96,32},{48,96},{112,48},{1... | collective-permute-start | bytes 786440 | tf_op jit(solution)/shard_map/ppermute | solution.py:34
  77.0 1.3 %copy-start = (bf16[16,2,32,1024]{3,2,1,0:T(8,128)(2,1)}, bf16[16,2,32,1024]{3,2,1,0:T(8,128)(2,1)S(1)}, u32[]{:S(2)}) copy-start(bf16[16,2,32,1024]{3,2,1,0:T(8,128)(2,1)S(1)} %all-to-all-done.refs_0_) | copy-start | bytes 6291460
  85.1 0.7 copy-start.8

commit v7 on v3

--- a/solution.py
+++ b/solution.py
@@ -23,6 +23,19 @@
 
 def dot(left, right):
     return lax.dot_general(left, right, (((1,), (1,)), ((), ())), preferred_element_type=F32)
+
+
+def mark_kernel(seen_ref, out_ref):
+    out_ref[...] = seen_ref[...]
+
+
+def mark(seen):
+    return pl.pallas_call(
+        mark_kernel,
+        out_shape=jax.ShapeDtypeStruct(seen.shape, seen.dtype),
+        compiler_params=pltpu.CompilerParams(vmem_limit_bytes=MIB),
+        cost_estimate=pl.CostEstimate(flops=10**11, bytes_accessed=10**8, transcendentals=0),
+    )(seen)
 
 
 def product_kernel(cuts, unread, begun, at_row, *refs):
@@ -94,7 +107,7 @@
         functools.partial(product_kernel, cuts, len(unread), len(aliases), at_row),
         out_shape=jax.ShapeDtypeStruct((NQ, nz * NC, height, LANES), BF16),
         in_specs=[anywhere] * len(operands),
-        out_specs=anywhere,
+        out_specs=pl.BlockSpec(memory_space=pl.ANY),
         scratch_shapes=[
             pltpu.VMEM((2, nz, rows, width), BF16),
             pltpu.VMEM((count, columns, width), BF16),
@@ -104,7 +117,7 @@
             pltpu.SemaphoreType.DMA,
         ],
         input_output_aliases=aliases,
-        compiler_params=pltpu.CompilerParams(vmem_limit_bytes=40 * MIB),
+        compiler_params=pltpu.CompilerParams(vmem_limit_bytes=24 * MIB),
         cost_estimate=pl.CostEstimate(flops=flops, bytes_accessed=5 * MIB, transcendentals=0),
     )(*operands)
 
@@ -132,6 +145,7 @@
             pl.BlockSpec((NQ, step, t.shape[2], LANES), lambda i: (0, i, 0, 0)) for t in terms
         ],
         out_specs=pl.BlockSpec((step, tall, LANES), lambda i: (i, 0, 0)),
+        compiler_params=pltpu.CompilerParams(vmem_limit_bytes=8 * MIB),
         cost_estimate=pl.CostEstimate(flops=MIB, bytes_accessed=2 * MIB, transcendentals=0),
     )(*terms)
 
@@ -158,6 +172,7 @@
         out_shape=jax.ShapeDtypeStruct((NH, rest, wide, columns), F32),
         in_specs=[pl.BlockSpec((step, tall, LANES), lambda i: (i, 0, 0))],
         out_specs=pl.BlockSpec((NH, step, wide, columns), lambda i: (0, i, 0, 0)),
+        compiler_params=pltpu.CompilerParams(vmem_limit_bytes=8 * MIB),
         cost_estimate=pl.CostEstimate(flops=2**17, bytes_accessed=MIB, transcendentals=0),
     )(terms)
 
@@ -173,14 +188,15 @@
     screened = (valence_pairs[0].astype(F32) * screening[None, :]).astype(BF16)
     sent = jnp.broadcast_to(screened[None], (NZ, second, plane_dev))
     mine = lax.all_to_all(sent, "z", 0, 0, tiled=True)
-    mine, *rows = lax.optimization_barrier((mine, ahead[:16], back[:16]))
+    mine, *rows = lax.optimization_barrier((mine, ahead[:16], back[:16], mark(screening[None])))
     other = lax.ppermute(mine, "core", [(0, 1), (1, 0)])
 
     far = along(ahead[:cut], 1), along(back[cut:], NH - 1)
+    other, *more = lax.optimization_barrier((other, mark(back[:16])))
 
     height = NH * columns // LANES * (second // NQ)
     most = (NH - 1) * columns // LANES * (second // NQ)
-    terms = product(mine, other, ((own,), (ahead,), (back,)), 0, height, rows)
+    terms = product(mine, other, ((own,), (ahead,), (back,)), 0, height, rows + more)
     terms = product(mine, other, (far,), most, height, (), terms)
     terms = lax.all_to_all(terms, ("x", "yl"), 0, 0, tiled=True)
     terms = lax.all_to_all(add(terms), ("z", "core"), 0, 0, tiled=True)

time: 127 us -> 110 us (0.87)
  blocking collectives: 57.1 us -> 47.8 us
  waiting for transfers between devices: 27 us -> 22.5 us
  Pallas kernels: 11.1 us -> 7.2 us
    ppermute x4, waiting for transfers between devices: 26.4 us -> 7.44 us  [along(): return lax.ppermute(block, 'yh', [(i, (i + step) % NH) for i in range(NH)])]
    all_to_all x1, waiting for transfers between devices: 0.68 us -> 12.8 us  [body(): mine = lax.all_to_all(sent, 'z', 0, 0, tiled=True)]
    all_to_all x1, blocking collectives: 37.3 us -> 30 us  [body(): terms = lax.all_to_all(terms, ('x', 'yl'), 0, 0, tiled=True)]
    pallas_call x1, Pallas kernels: 3.52 us -> 0.49 us  [add(): pl.pallas_call(add_kernel, grid=(rest // step,), out_shape=jax.ShapeDtype...]
    ppermute x1, waiting for transfers between devices: 0.01 us -> 2.25 us  [body(): other = lax.ppermute(mine, 'core', [(0, 1), (1, 0)])]
    all_to_all x1, blocking collectives: 19.8 us -> 17.8 us  [body(): terms = lax.all_to_all(add(terms), ('z', 'core'), 0, 0, tiled=True)]
    ppermute x4, starting transfers between devices: 15.6 us -> 16.9 us  [along(): return lax.ppermute(block, 'yh', [(i, (i + step) % NH) for i in range(NH)])]
  transfers between devices with their start and end apart: 6 -> 6, of which waited for: 4 -> 3; matrix products, arithmetic and copies ran while one was open for 0% -> 3% of each run, Pallas kernels for 3% -> 4%
where the time goes in v7:
time: 110 us
  blocking collectives  47.8 us (43%)
  starting transfers between devices  29.4 us (27%)
  waiting for transfers between devices  22.5 us (20%)
  Pallas kernels  7.2 us (7%)
  local copies, waits for them, and re-layouts  1.85 us (2%)
    all_to_all x1, blocking collectives, body(): terms = lax.all_to_all(terms, ('x', 'yl'), 0, 0, tiled=True)  30 us
    all_to_all x1, blocking collectives, body(): terms = lax.all_to_all(add(terms), ('z', 'core'), 0, 0, tiled=True)  17.8 us
    ppermute x4, starting transfers between devices, along(): return lax.ppermute(block, 'yh', [(i, (i + step) % NH) for i in range(NH)])  16.9 us
    all_to_all x1, waiting for transfers between devices, body(): mine = lax.all_to_all(sent, 'z', 0, 0, tiled=True)  12.8 us
    all_to_all x1, starting transfers between devices, body(): mine = lax.all_to_all(sent, 'z', 0, 0, tiled=True)  10 us
    ppermute x4, waiting for transfers between devices, along(): return lax.ppermute(block, 'yh', [(i, (i + step) % NH) for i in range(NH)])  7.44 us
    pallas_call x2, Pallas kernels, product(): pl.pallas_call(functools.partial(product_kernel, cuts, len(unread), len(a...  5.89 us
    ppermute x1, starting transfers between devices, body(): other = lax.ppermute(mine, 'core', [(0, 1), (1, 0)])  2.39 us
  transfers between devices with their start and end apart: 6, of which 3 were waited for; matrix products, arithmetic and copies ran while one was open for 3% of the time, Pallas kernels for 4%

profile of v7, /device:TPU:1, one launch (start us, length us, event | category | flops | bytes accessed | tf_op | source)
XLA Modules:
  0.0 109.8 jit_solution(1440587476796583918)
XLA Ops:
  0.0 6.8 %collective-permute-start.1 = (bf16[256,1024]{1,0:T(8,128)(2,1)}, bf16[256,1024]{1,0:T(8,128)(2,1)S(1)}, u32[]{:S(2)}, u32[]{:S(2)}) collective-permute-start(bf16[256,1024]{1,0:T(8,128)(2,1)} %bitcast.6), channel_id=1, source_target_pairs={{0,48},{16,0},{32,16},{48,32},{1,49},{17,1},{33,17},{49,33},{2,50}... | collective-permute-start | bytes 1572872 | tf_op jit(solution)/shard_map/ppermute | solution.py:21
  6.8 1.9 %collective-permute-start = (bf16[256,1024]{1,0:T(8,128)(2,1)}, bf16[256,1024]{1,0:T(8,128)(2,1)S(1)}, u32[]{:S(2)}, u32[]{:S(2)}) collective-permute-start(bf16[256,1024]{1,0:T(8,128)(2,1)} %bitcast.7), channel_id=1, source_target_pairs={{0,16},{16,32},{32,48},{48,0},{1,17},{17,33},{33,49},{49,1},{2,18}... | collective-permute-start | bytes 1572872 | tf_op jit(solution)/shard_map/ppermute | solution.py:21
  8.8 0.9 fusion
  9.7 1.1 broadcast_in_dim.13
  10.8 10.0 %all-to-all-start = ((bf16[8,64,1024]{2,1,0:T(8,128)(2,1)}), bf16[8,64,1024]{2,1,0:T(8,128)(2,1)S(1)}, u32[]{:S(2)}, u32[]{:S(2)}) async-start(bf16[8,64,1024]{2,1,0:T(8,128)(2,1)} %broadcast_in_dim.13), calls=%async_computation | async-start | bytes 2097152 | tf_op jit(solution)/shard_map/all_to_all | solution.py:190
  20.8 0.0 copy-done
  20.9 7.4 %collective-permute-done.1.refs_4_ = bf16[256,1024]{1,0:T(8,128)(2,1)S(1)} collective-permute-done((bf16[256,1024]{1,0:T(8,128)(2,1)}, bf16[256,1024]{1,0:T(8,128)(2,1)S(1)}, u32[]{:S(2)}, u32[]{:S(2)}) %collective-permute-start.1) | collective-permute-done | bytes 524320 | tf_op jit(solution)/shard_map/ppermute | solution.py:21
  28.3 6.3 %collective-permute-start.4 = (bf16[128,1024]{1,0:T(8,128)(2,1)S(1)}, bf16[128,1024]{1,0:T(8,128)(2,1)S(1)}, u32[]{:S(2)}, u32[]{:S(2)}) collective-permute-start(bf16[128,1024]{1,0:T(8,128)(2,1)S(1)} %slice.20), channel_id=1, source_target_pairs={{0,48},{16,0},{32,16},{48,32},{1,49},{17,1},{33,17},{49,33},{2,50}... | collective-permute-start | bytes 786440 | tf_op jit(solution)/shard_map/ppermute | solution.py:21
  34.6 0.0 collective-permute-done.refs_3_
  34.6 0.7 slice.19
  35.3 1.9 %collective-permute-start.3 = (bf16[128,1024]{1,0:T(8,128)(2,1)}, bf16[128,1024]{1,0:T(8,128)(2,1)S(1)}, u32[]{:S(2)}, u32[]{:S(2)}) collective-permute-start(bf16[128,1024]{1,0:T(8,128)(2,1)} %slice.19), channel_id=1, source_target_pairs={{0,16},{16,32},{32,48},{48,0},{1,17},{17,33},{33,49},{49,1},{2,18}... | collective-permute-start | bytes 786440 | tf_op jit(solution)/shard_map/ppermute | solution.py:21
  37.3 0.0 copy-start.1
  37.3 12.8 %all-to-all-done.refs_0_ = bf16[8,64,1024]{2,1,0:T(8,128)(2,1)S(1)} async-done(((bf16[8,64,1024]{2,1,0:T(8,128)(2,1)}), bf16[8,64,1024]{2,1,0:T(8,128)(2,1)S(1)}, u32[]{:S(2)}, u32[]{:S(2)}) %all-to-all-start) | async-done | bytes 1048608 | tf_op jit(solution)/shard_map/all_to_all | solution.py:190
  50.0 2.4 %collective-permute-start.2 = (bf16[8,64,1024]{2,1,0:T(8,128)(2,1)S(1)}, bf16[8,64,1024]{2,1,0:T(8,128)(2,1)S(1)}, u32[]{:S(2)}, u32[]{:S(2)}) collective-permute-start(bf16[8,64,1024]{2,1,0:T(8,128)(2,1)S(1)} %all-to-all-done.refs_0_), channel_id=1, source_target_pairs={{0,1},{1,0},{2,3},{3,2},{4,5},{5,4},{6,7},{7,6},{8,9},{9,8},{10,11... | collective-permute-start | bytes 3145736 | tf_op jit(solution)/shard_map/ppermute | solution.py:192
  52.4 2.3 %collective-permute-done.2.refs_1_ = bf16[8,64,1024]{2,1,0:T(8,128)(2,1)S(1)} collective-permute-done((bf16[8,64,1024]{2,1,0:T(8,128)(2,1)S(1)}, bf16[8,64,1024]{2,1,0:T(8,128)(2,1)S(1)}, u32[]{:S(2)}, u32[]{:S(2)}) %collective-permute-start.2) | collective-permute-done | bytes 1048608 | tf_op jit(solution)/shard_map/ppermute | solution.py:192
  54.7 0.0 copy-done.1
  54.7 4.1 %shard_map.39.refs_4_ = bf16[8,16,64,128]{3,2,1,0:T(8,128)(2,1)S(1)} custom-call(bf16[8,64,1024]{2,1,0:T(8,128)(2,1)S(1)} %all-to-all-done.refs_0_, bf16[8,64,1024]{2,1,0:T(8,128)(2,1)S(1)} %collective-permute-done.2.refs_1_, bf16[256,1024]{1,0:T(8,128)(2,1)S(1)} %bitcast.8, bf16[256,1024]{1,0:T(8,128)(2,1)S(1)} %collective-permute-done.refs_3_, ...), custom_call_target="tpu_custom_call" | custom-call | flops 1610612736 | bytes 5242880 | tf_op jit(solution)/shard_map/pallas_call | solution.py:106
  58.8 0.0 collective-permute-done.4.refs_3_
  58.8 0.0 collective-permute-done.3.refs_2_
  58.8 1.8 %shard_map.40 = bf16[8,16,64,128]{3,2,1,0:T(8,128)(2,1)S(1)} custom-call(bf16[8,64,1024]{2,1,0:T(8,128)(2,1)S(1)} %all-to-all-done.refs_0_, bf16[8,64,1024]{2,1,0:T(8,128)(2,1)S(1)} %collective-permute-done.2.refs_1_, bf16[128,1024]{1,0:T(8,128)(2,1)S(1)} %collective-permute-done.3.refs_2_, ...), custom_call_target="tpu_custom_call", output_to_operand_aliasing={{}: (4, {})} | custom-call | flops 536870912 | bytes 5242880 | tf_op jit(solution)/shard_map/pallas_call | solution.py:106
  60.6 30.0 %all_to_all.15.refs_0_ = bf16[8,16,64,128]{3,2,1,0:T(8,128)(2,1)S(1)} all-to-all(bf16[8,16,64,128]{3,2,1,0:T(8,128)(2,1)S(1)} %shard_map.40), channel_id=1, replica_groups=mesh['x'=4,'yl'=2,'yh'=4,'z'=8,'core'=2] {'x','yl'}, dimensions={0} | all-to-all | bytes 4194304 | tf_op jit(solution)/shard_map/all_to_all | solution.py:201
  90.6 0.5 shard_map.41
  91.1 17.8 %all_to_all.16.terms_ref = bf16[16,64,128]{2,1,0:T(8,128)(2,1)S(1)} all-to-all(bf16[16,64,128]{2,1,0:T(8,128)(2,1)S(1)} %shard_map.41), channel_id=1, replica_groups=mesh['x'=4,'yl'=2,'yh'=4,'z'=8,'core'=2] {'z','core'}, dimensions={0} | all-to-all | bytes 524288 | tf_op jit(solution)/shard_map/all_to_all | solution.py:202
  108.9 0.8 shard_map.42
  (6 shorter events, 0.0 us)
Async XLA Ops:
  0.0 20.8 %copy-start = (f32[1024]{0:T(1024)S(1)}, f32[1024]{0:T(1024)}, u32[]{:S(2)}) copy-start(f32[1024]{0:T(1024)} %param.5) | copy-start | bytes 12292
  0.0 28.3 %collective-permute-start.1 = (bf16[256,1024]{1,0:T(8,128)(2,1)}, bf16[256,1024]{1,0:T(8,128)(2,1)S(1)}, u32[]{:S(2)}, u32[]{:S(2)}) collective-permute-start(bf16[256,1024]{1,0:T(8,128)(2,1)} %bitcast.6), channel_id=1, source_target_pairs={{0,48},{16,0},{32,16},{48,32},{1,49},{17,1},{33,17},{49,33},{2,50}... | collective-permute-start | bytes 1572872 | tf_op jit(solution)/shard_map/ppermute | solution.py:21
  6.8 27.7 %collective-permute-start = (bf16[256,1024]{1,0:T(8,128)(2,1)}, bf16[256,1024]{1,0:T(8,128)(2,1)S(1)}, u32[]{:S(2)}, u32[]{:S(2)}) collective-permute-start(bf16[256,1024]{1,0:T(8,128)(2,1)} %bitcast.7), channel_id=1, source_target_pairs={{0,16},{16,32},{32,48},{48,0},{1,17},{17,33},{33,49},{49,1},{2,18}... | collective-permute-start | bytes 1572872 | tf_op jit(solution)/shard_map/ppermute | solution.py:21
  10.8 39.2 %all-to-all-start = ((bf16[8,64,1024]{2,1,0:T(8,128)(2,1)}), bf16[8,64,1024]{2,1,0:T(8,128)(2,1)S(1)}, u32[]{:S(2)}, u32[]{:S(2)}) async-start(bf16[8,64,1024]{2,1,0:T(8,128)(2,1)} %broadcast_in_dim.13), calls=%async_computation | async-start | bytes 2097152 | tf_op jit(solution)/shard_map/all_to_all | solution.py:190
  28.3 30.5 %collective-permute-start.4 = (bf16[128,1024]{1,0:T(8,128)(2,1)S(1)}, bf16[128,1024]{1,0:T(8,128)(2,1)S(1)}, u32[]{:S(2)}, u32[]{:S(2)}) collective-permute-start(bf16[128,1024]{1,0:T(8,128)(2,1)S(1)} %slice.20), channel_id=1, source_target_pairs={{0,48},{16,0},{32,16},{48,32},{1,49},{17,1},{33,17},{49,33},{2,50}... | collective-permute-start | bytes 786440 | tf_op jit(solution)/shard_map/ppermute | solution.py:21
  35.3 23.5 %collective-permute-start.3 = (bf16[128,1024]{1,0:T(8,128)(2,1)}, bf16[128,1024]{1,0:T(8,128)(2,1)S(1)}, u32[]{:S(2)}, u32[]{:S(2)}) collective-permute-start(bf16[128,1024]{1,0:T(8,128)(2,1)} %slice.19), channel_id=1, source_target_pairs={{0,16},{16,32},{32,48},{48,0},{1,17},{17,33},{33,49},{49,1},{2,18}... | collective-permute-start | bytes 786440 | tf_op jit(solution)/shard_map/ppermute | solution.py:21
  37.3 17.4 %copy-start.1 = (bf16[1,256,1024]{2,1,0:T(8,128)(2,1)S(1)}, bf16[1,256,1024]{2,1,0:T(8,128)(2,1)}, u32[]{:S(2)}) copy-start(bf16[1,256,1024]{2,1,0:T(8,128)(2,1)} %param.4) | copy-start | bytes 1572868
  50.0 4.7 %collective-permute-start.2 = (bf16[8,64,1024]{2,1,0:T(8,128)(2,1)S(1)}, bf16[8,64,1024]{2,1,0:T(8,128)(2,1)S(1)}, u32[]{:S(2)}, u32[]{:S(2)}) collective-permute-start(bf16[8,64,1024]{2,1,0:T(8,128)(2,1)S(1)} %all-to-all-done.refs_0_), channel_id=1, source_target_pairs={{0,1},{1,0},{2,3},{3,2},{4,5},{5,4},{6,7},{7,6},{8,9},{9,8},{10,11... | collective-permute-start | bytes 3145736 | tf_op jit(solution)/shard_map/ppermute | solution.py:192

commit v8 on v7

--- a/solution.py
+++ b/solution.py
@@ -23,6 +23,21 @@
 
 def dot(left, right):
     return lax.dot_general(left, right, (((1,), (1,)), ((), ())), preferred_element_type=F32)
+
+
+def screen_kernel(pairs_ref, screening_ref, out_ref):
+    screened = (pairs_ref[...].astype(F32) * screening_ref[...]).astype(BF16)
+    for i in range(out_ref.shape[0]):
+        out_ref[i] = screened
+
+
+def screen(pairs, screening, copies):
+    return pl.pallas_call(
+        screen_kernel,
+        out_shape=jax.ShapeDtypeStruct((copies, *pairs.shape), BF16),
+        compiler_params=pltpu.CompilerParams(vmem_limit_bytes=4 * MIB),
+        cost_estimate=pl.CostEstimate(flops=2**16, bytes_accessed=MIB, transcendentals=0),
+    )(pairs, screening[None])
 
 
 def mark_kernel(seen_ref, out_ref):
@@ -50,15 +65,15 @@
     ]
     rights, at = [], 0
     for i, cut in enumerate(cuts):
-        group = []
-        part = right.shape[1] // cut
-        for p in range(cut):
+        group, top = [], 0
+        for _ in range(cut):
+            part = piece_refs[at].shape[0]
             group.append(
                 pltpu.make_async_copy(
-                    piece_refs[at], right.at[i, pl.ds(p * part, part)], right_sem.at[at]
+                    piece_refs[at], right.at[i, pl.ds(top, part)], right_sem.at[at]
                 )
             )
-            at += 1
+            at, top = at + 1, top + part
         rights.append(group)
     lefts[0].start()
     for copy in rights[0]:
@@ -67,20 +82,20 @@
     for group in rights[1:]:
         for copy in group:
             copy.start()
+    for copy in lefts:
+        copy.wait()
+    whole = left[...].reshape(2 * nz * rows, width)
+    done = []
+    for i in range(count):
+        for copy in rights[i]:
+            copy.wait()
+        term = dot(whole, right[i])
+        done += [term[:, c : c + LANES] for c in range(0, term.shape[1], LANES)]
     for which in range(2):
-        lefts[which].wait()
         target_core = core if which == 0 else 1 - core
-        whole = left[which].reshape(nz * rows, width)
-        done = []
-        for i in range(count):
-            if which == 0:
-                for copy in rights[i]:
-                    copy.wait()
-            term = dot(whole, right[i])
-            done += [term[:, c : c + LANES] for c in range(0, term.shape[1], LANES)]
         for zi in range(nz):
             for qi in range(NQ):
-                at = zi * rows + qi * wide
+                at = (which * nz + zi) * rows + qi * wide
                 block = jnp.concatenate([d[at : at + wide] for d in done], axis=0)
                 held[qi, zi * NC + target_core] = block.astype(BF16)
     tall = held.shape[2]
@@ -93,7 +108,7 @@
     nz, rows, width = mine.shape
     wide = rows // NQ
     cuts = tuple(len(block) for block in blocks)
-    columns = cuts[0] * blocks[0][0].shape[0]
+    columns = sum(piece.shape[0] for piece in blocks[0])
     count = len(blocks)
     tall = count * columns // LANES * wide
     flops = 2 * 2 * nz * rows * width * columns * count
@@ -117,7 +132,7 @@
             pltpu.SemaphoreType.DMA,
         ],
         input_output_aliases=aliases,
-        compiler_params=pltpu.CompilerParams(vmem_limit_bytes=24 * MIB),
+        compiler_params=pltpu.CompilerParams(vmem_limit_bytes=14 * MIB),
         cost_estimate=pl.CostEstimate(flops=flops, bytes_accessed=5 * MIB, transcendentals=0),
     )(*operands)
 
@@ -181,12 +196,11 @@
     _, second, plane_dev = valence_pairs.shape
     own = conduction_pairs[0]
     columns = own.shape[0]
-    cut = columns // 2
+    cut = columns * 5 // 8
 
     ahead, back = along(own, 1), along(own, NH - 1)
 
-    screened = (valence_pairs[0].astype(F32) * screening[None, :]).astype(BF16)
-    sent = jnp.broadcast_to(screened[None], (NZ, second, plane_dev))
+    sent = screen(valence_pairs[0], screening, NZ)
     mine = lax.all_to_all(sent, "z", 0, 0, tiled=True)
     mine, *rows = lax.optimization_barrier((mine, ahead[:16], back[:16], mark(screening[None])))
     other = lax.ppermute(mine, "core", [(0, 1), (1, 0)])

time: 110 us -> 112 us (1.018)
  blocking collectives: 47.8 us -> 49.5 us
    all_to_all x1, blocking collectives: 17.8 us -> 19.5 us  [body(): terms = lax.all_to_all(add(terms), ('z', 'core'), 0, 0, tiled=True)]
    unnamed x4 -> x8, local copies, waits for them, and re-layouts: 0.01 us -> 1.59 us
  transfers between devices with their start and end apart: 6 -> 6, of which waited for: 3 -> 3; matrix products, arithmetic and copies ran while one was open for 3% -> 1% of each run, Pallas kernels for 4% -> 5%
where the time goes in v8:
time: 112 us
  blocking collectives  49.5 us (44%)
  starting transfers between devices  29.2 us (26%)
  waiting for transfers between devices  22.6 us (20%)
  Pallas kernels  7.84 us (7%)
  local copies, waits for them, and re-layouts  2.32 us (2%)
    all_to_all x1, blocking collectives, body(): terms = lax.all_to_all(terms, ('x', 'yl'), 0, 0, tiled=True)  30 us
    all_to_all x1, blocking collectives, body(): terms = lax.all_to_all(add(terms), ('z', 'core'), 0, 0, tiled=True)  19.5 us
    ppermute x4, starting transfers between devices, along(): return lax.ppermute(block, 'yh', [(i, (i + step) % NH) for i in range(NH)])  16.8 us
    all_to_all x1, waiting for transfers between devices, body(): mine = lax.all_to_all(sent, 'z', 0, 0, tiled=True)  13.4 us
    all_to_all x1, starting transfers between devices, body(): mine = lax.all_to_all(sent, 'z', 0, 0, tiled=True)  10 us
    ppermute x4, waiting for transfers between devices, along(): return lax.ppermute(block, 'yh', [(i, (i + step) % NH) for i in range(NH)])  6.96 us
    pallas_call x2, Pallas kernels, product(): pl.pallas_call(functools.partial(product_kernel, cuts, len(unread), len(a...  5.47 us
    ppermute x1, starting transfers between devices, body(): other = lax.ppermute(mine, 'core', [(0, 1), (1, 0)])  2.39 us
  transfers between devices with their start and end apart: 6, of which 3 were waited for; matrix products, arithmetic and copies ran while one was open for 1% of the time, Pallas kernels for 5%

profile of v8, /device:TPU:1, one launch (start us, length us, event | category | flops | bytes accessed | tf_op | source)
XLA Modules:
  0.0 111.6 jit_solution(7157491495537406025)
XLA Ops:
  0.0 6.8 %collective-permute-start.1 = (bf16[256,1024]{1,0:T(8,128)(2,1)}, bf16[256,1024]{1,0:T(8,128)(2,1)S(1)}, u32[]{:S(2)}, u32[]{:S(2)}) collective-permute-start(bf16[256,1024]{1,0:T(8,128)(2,1)} %bitcast.7), channel_id=1, source_target_pairs={{0,48},{16,0},{32,16},{48,32},{1,49},{17,1},{33,17},{49,33},{2,50}... | collective-permute-start | bytes 1572872 | tf_op jit(solution)/shard_map/ppermute | solution.py:21
  6.8 1.9 %collective-permute-start = (bf16[256,1024]{1,0:T(8,128)(2,1)}, bf16[256,1024]{1,0:T(8,128)(2,1)S(1)}, u32[]{:S(2)}, u32[]{:S(2)}) collective-permute-start(bf16[256,1024]{1,0:T(8,128)(2,1)} %bitcast.8), channel_id=1, source_target_pairs={{0,16},{16,32},{32,48},{48,0},{1,17},{17,33},{33,49},{49,1},{2,18}... | collective-permute-start | bytes 1572872 | tf_op jit(solution)/shard_map/ppermute | solution.py:21
  8.8 0.0 copy-start
  8.8 0.9 copy-done
  9.7 0.7 copy-done.1
  10.4 1.1 shard_map.37
  11.4 10.0 %all-to-all-start = ((bf16[8,64,1024]{2,1,0:T(8,128)(2,1)}), bf16[8,64,1024]{2,1,0:T(8,128)(2,1)S(1)}, u32[]{:S(2)}, u32[]{:S(2)}) async-start(bf16[8,64,1024]{2,1,0:T(8,128)(2,1)} %shard_map.37), calls=%async_computation | async-start | bytes 2097152 | tf_op jit(solution)/shard_map/all_to_all | solution.py:204
  21.5 7.0 %collective-permute-done.1.refs_4_ = bf16[256,1024]{1,0:T(8,128)(2,1)S(1)} collective-permute-done((bf16[256,1024]{1,0:T(8,128)(2,1)}, bf16[256,1024]{1,0:T(8,128)(2,1)S(1)}, u32[]{:S(2)}, u32[]{:S(2)}) %collective-permute-start.1) | collective-permute-done | bytes 524320 | tf_op jit(solution)/shard_map/ppermute | solution.py:21
  28.4 0.7 slice.20
  29.1 6.1 %collective-permute-start.4 = (bf16[96,1024]{1,0:T(8,128)(2,1)}, bf16[96,1024]{1,0:T(8,128)(2,1)S(1)}, u32[]{:S(2)}, u32[]{:S(2)}) collective-permute-start(bf16[96,1024]{1,0:T(8,128)(2,1)} %slice.20), channel_id=1, source_target_pairs={{0,48},{16,0},{32,16},{48,32},{1,49},{17,1},{33,17},{49,33},{2,50}... | collective-permute-start | bytes 589832 | tf_op jit(solution)/shard_map/ppermute | solution.py:21
  35.2 0.0 collective-permute-done.refs_3_
  35.3 1.9 %collective-permute-start.3 = (bf16[160,1024]{1,0:T(8,128)(2,1)S(1)}, bf16[160,1024]{1,0:T(8,128)(2,1)S(1)}, u32[]{:S(2)}, u32[]{:S(2)}) collective-permute-start(bf16[160,1024]{1,0:T(8,128)(2,1)S(1)} %slice.19), channel_id=1, source_target_pairs={{0,16},{16,32},{32,48},{48,0},{1,17},{17,33},{33,49},{49,1},{2,18}... | collective-permute-start | bytes 983048 | tf_op jit(solution)/shard_map/ppermute | solution.py:21
  37.2 0.0 copy-start.3
  37.2 13.4 %all-to-all-done.refs_0_ = bf16[8,64,1024]{2,1,0:T(8,128)(2,1)S(1)} async-done(((bf16[8,64,1024]{2,1,0:T(8,128)(2,1)}), bf16[8,64,1024]{2,1,0:T(8,128)(2,1)S(1)}, u32[]{:S(2)}, u32[]{:S(2)}) %all-to-all-start) | async-done | bytes 1048608 | tf_op jit(solution)/shard_map/all_to_all | solution.py:204
  50.7 2.4 %collective-permute-start.2 = (bf16[8,64,1024]{2,1,0:T(8,128)(2,1)S(1)}, bf16[8,64,1024]{2,1,0:T(8,128)(2,1)S(1)}, u32[]{:S(2)}, u32[]{:S(2)}) collective-permute-start(bf16[8,64,1024]{2,1,0:T(8,128)(2,1)S(1)} %all-to-all-done.refs_0_), channel_id=1, source_target_pairs={{0,1},{1,0},{2,3},{3,2},{4,5},{5,4},{6,7},{7,6},{8,9},{9,8},{10,11... | collective-permute-start | bytes 3145736 | tf_op jit(solution)/shard_map/ppermute | solution.py:206
  53.1 2.3 %collective-permute-done.2.refs_1_ = bf16[8,64,1024]{2,1,0:T(8,128)(2,1)S(1)} collective-permute-done((bf16[8,64,1024]{2,1,0:T(8,128)(2,1)S(1)}, bf16[8,64,1024]{2,1,0:T(8,128)(2,1)S(1)}, u32[]{:S(2)}, u32[]{:S(2)}) %collective-permute-start.2) | collective-permute-done | bytes 1048608 | tf_op jit(solution)/shard_map/ppermute | solution.py:206
  55.3 4.0 %shard_map.40.refs_4_ = bf16[8,16,64,128]{3,2,1,0:T(8,128)(2,1)S(1)} custom-call(bf16[8,64,1024]{2,1,0:T(8,128)(2,1)S(1)} %all-to-all-done.refs_0_, bf16[8,64,1024]{2,1,0:T(8,128)(2,1)S(1)} %collective-permute-done.2.refs_1_, bf16[256,1024]{1,0:T(8,128)(2,1)S(1)} %bitcast.9, bf16[256,1024]{1,0:T(8,128)(2,1)S(1)} %collective-permute-done.refs_3_, ...), custom_call_target="tpu_custom_call" | custom-call | flops 1610612736 | bytes 5242880 | tf_op jit(solution)/shard_map/pallas_call | solution.py:121
  59.3 0.0 collective-permute-done.4.refs_3_
  59.3 0.0 collective-permute-done.3.refs_2_
  59.3 1.5 %shard_map.41 = bf16[8,16,64,128]{3,2,1,0:T(8,128)(2,1)S(1)} custom-call(bf16[8,64,1024]{2,1,0:T(8,128)(2,1)S(1)} %all-to-all-done.refs_0_, bf16[8,64,1024]{2,1,0:T(8,128)(2,1)S(1)} %collective-permute-done.2.refs_1_, bf16[160,1024]{1,0:T(8,128)(2,1)S(1)} %collective-permute-done.3.refs_2_, ...), custom_call_target="tpu_custom_call", output_to_operand_aliasing={{}: (4, {})} | custom-call | flops 536870912 | bytes 5242880 | tf_op jit(solution)/shard_map/pallas_call | solution.py:121
  60.8 30.0 %all_to_all.15.refs_0_ = bf16[8,16,64,128]{3,2,1,0:T(8,128)(2,1)S(1)} all-to-all(bf16[8,16,64,128]{3,2,1,0:T(8,128)(2,1)S(1)} %shard_map.41), channel_id=1, replica_groups=mesh['x'=4,'yl'=2,'yh'=4,'z'=8,'core'=2] {'x','yl'}, dimensions={0} | all-to-all | bytes 4194304 | tf_op jit(solution)/shard_map/all_to_all | solution.py:215
  90.8 0.5 shard_map.42
  91.3 19.5 %all_to_all.16.terms_ref = bf16[16,64,128]{2,1,0:T(8,128)(2,1)S(1)} all-to-all(bf16[16,64,128]{2,1,0:T(8,128)(2,1)S(1)} %shard_map.42), channel_id=1, replica_groups=mesh['x'=4,'yl'=2,'yh'=4,'z'=8,'core'=2] {'z','core'}, dimensions={0} | all-to-all | bytes 524288 | tf_op jit(solution)/shard_map/all_to_all | solution.py:216
  110.8 0.8 shard_map.43
  (9 shorter events, 0.0 us)
Async XLA Ops:
  0.0 21.5 %copy-start.2 = (f32[1024]{0:T(1024)S(1)}, f32[1024]{0:T(1024)}, u32[]{:S(2)}) copy-start(f32[1024]{0:T(1024)} %param.5) | copy-start | bytes 12292
  0.0 28.4 %collective-permute-start.1 = (bf16[256,1024]{1,0:T(8,128)(2,1)}, bf16[256,1024]{1,0:T(8,128)(2,1)S(1)}, u32[]{:S(2)}, u32[]{:S(2)}) collective-permute-start(bf16[256,1024]{1,0:T(8,128)(2,1)} %bitcast.7), channel_id=1, source_target_pairs={{0,48},{16,0},{32,16},{48,32},{1,49},{17,1},{33,17},{49,33},{2,50}... | collective-permute-start | bytes 1572872 | tf_op jit(solution)/shard_map/ppermute | solution.py:21
  6.8 28.4 %collective-permute-start = (bf16[256,1024]{1,0:T(8,128)(2,1)}, bf16[256,1024]{1,0:T(8,128)(2,1)S(1)}, u32[]{:S(2)}, u32[]{:S(2)}) collective-permute-start(bf16[256,1024]{1,0:T(8,128)(2,1)} %bitcast.8), channel_id=1, source_target_pairs={{0,16},{16,32},{32,48},{48,0},{1,17},{17,33},{33,49},{49,1},{2,18}... | collective-permute-start | bytes 1572872 | tf_op jit(solution)/shard_map/ppermute | solution.py:21
  8.8 0.9 copy-start
  9.7 0.7 copy-start.1
  11.4 39.2 %all-to-all-start = ((bf16[8,64,1024]{2,1,0:T(8,128)(2,1)}), bf16[8,64,1024]{2,1,0:T(8,128)(2,1)S(1)}, u32[]{:S(2)}, u32[]{:S(2)}) async-start(bf16[8,64,1024]{2,1,0:T(8,128)(2,1)} %shard_map.37), calls=%async_computation | async-start | bytes 2097152 | tf_op jit(solution)/shard_map/all_to_all | solution.py:204
  29.1 30.2 %collective-permute-start.4 = (bf16[96,1024]{1,0:T(8,128)(2,1)}, bf16[96,1024]{1,0:T(8,128)(2,1)S(1)}, u32[]{:S(2)}, u32[]{:S(2)}) collective-permute-start(bf16[96,1024]{1,0:T(8,128)(2,1)} %slice.20), channel_id=1, source_target_pairs={{0,48},{16,0},{32,16},{48,32},{1,49},{17,1},{33,17},{49,33},{2,50}... | collective-permute-start | bytes 589832 | tf_op jit(solution)/shard_map/ppermute | solution.py:21
  35.3 24.0 %collective-permute-start.3 = (bf16[160,1024]{1,0:T(8,128)(2,1)S(1)}, bf16[160,1024]{1,0:T(8,128)(2,1)S(1)}, u32[]{:S(2)}, u32[]{:S(2)}) collective-permute-start(bf16[160,1024]{1,0:T(8,128)(2,1)S(1)} %slice.19), channel_id=1, source_target_pairs={{0,16},{16,32},{32,48},{48,0},{1,17},{17,33},{33,49},{49,1},{2,18}... | collective-permute-start | bytes 983048 | tf_op jit(solution)/shard_map/ppermute | solution.py:21
  37.2 18.1 %copy-start.3 = (bf16[1,256,1024]{2,1,0:T(8,128)(2,1)S(1)}, bf16[1,256,1024]{2,1,0:T(8,128)(2,1)}, u32[]{:S(2)}) copy-start(bf16[1,256,1024]{2,1,0:T(8,128)(2,1)} %param.4) | copy-start | bytes 1572868
  50.7 4.7 %collective-permute-start.2 = (bf16[8,64,1024]{2,1,0:T(8,128)(2,1)S(1)}, bf16[8,64,1024]{2,1,0:T(8,128)(2,1)S(1)}, u32[]{:S(2)}, u32[]{:S(2)}) collective-permute-start(bf16[8,64,1024]{2,1,0:T(8,128)(2,1)S(1)} %all-to-all-done.refs_0_), channel_id=1, source_target_pairs={{0,1},{1,0},{2,3},{3,2},{4,5},{5,4},{6,7},{7,6},{8,9},{9,8},{10,11... | collective-permute-start | bytes 3145736 | tf_op jit(solution)/shard_map/ppermute | solution.py:206

commit v9 on v8

--- a/solution.py
+++ b/solution.py
@@ -15,6 +15,7 @@
 NQ = NX * NL
 LANES = 128
 MIB = 2**20
+LONG = 10**11
 
 
 def along(block, step):
@@ -23,21 +24,6 @@
 
 def dot(left, right):
     return lax.dot_general(left, right, (((1,), (1,)), ((), ())), preferred_element_type=F32)
-
-
-def screen_kernel(pairs_ref, screening_ref, out_ref):
-    screened = (pairs_ref[...].astype(F32) * screening_ref[...]).astype(BF16)
-    for i in range(out_ref.shape[0]):
-        out_ref[i] = screened
-
-
-def screen(pairs, screening, copies):
-    return pl.pallas_call(
-        screen_kernel,
-        out_shape=jax.ShapeDtypeStruct((copies, *pairs.shape), BF16),
-        compiler_params=pltpu.CompilerParams(vmem_limit_bytes=4 * MIB),
-        cost_estimate=pl.CostEstimate(flops=2**16, bytes_accessed=MIB, transcendentals=0),
-    )(pairs, screening[None])
 
 
 def mark_kernel(seen_ref, out_ref):
@@ -49,19 +35,19 @@
         mark_kernel,
         out_shape=jax.ShapeDtypeStruct(seen.shape, seen.dtype),
         compiler_params=pltpu.CompilerParams(vmem_limit_bytes=MIB),
-        cost_estimate=pl.CostEstimate(flops=10**11, bytes_accessed=10**8, transcendentals=0),
+        cost_estimate=pl.CostEstimate(flops=LONG, bytes_accessed=10**8, transcendentals=0),
     )(seen)
 
 
-def product_kernel(cuts, unread, begun, at_row, *refs):
-    count, pieces = len(cuts), sum(cuts)
-    rows_refs, piece_refs = refs[:2], refs[2 : 2 + pieces]
-    out_ref, left, right, held, left_sem, right_sem, out_sem = refs[2 + pieces + unread + begun :]
+def product_kernel(sides, cuts, ignored, at_row, *refs):
+    count, pieces, width = len(cuts), sum(cuts), len(sides)
+    rows_refs, piece_refs = refs[:width], refs[width : width + pieces]
+    out_ref, left, right, held, left_sem, right_sem, out_sem = refs[width + pieces + ignored :]
     core = lax.axis_index("core")
-    nz, rows, width = rows_refs[0].shape
+    nz, rows, planes = rows_refs[0].shape
     wide = rows // NQ
     lefts = [
-        pltpu.make_async_copy(rows_refs[i], left.at[i], left_sem.at[i]) for i in range(2)
+        pltpu.make_async_copy(rows_refs[i], left.at[i], left_sem.at[i]) for i in range(width)
     ]
     rights, at = [], 0
     for i, cut in enumerate(cuts):
@@ -75,61 +61,61 @@
             )
             at, top = at + 1, top + part
         rights.append(group)
-    lefts[0].start()
-    for copy in rights[0]:
+    for copy in [*lefts, *[copy for group in rights for copy in group]]:
         copy.start()
-    lefts[1].start()
-    for group in rights[1:]:
-        for copy in group:
-            copy.start()
     for copy in lefts:
         copy.wait()
-    whole = left[...].reshape(2 * nz * rows, width)
+    whole = left[...].reshape(width * nz * rows, planes)
     done = []
     for i in range(count):
         for copy in rights[i]:
             copy.wait()
         term = dot(whole, right[i])
         done += [term[:, c : c + LANES] for c in range(0, term.shape[1], LANES)]
-    for which in range(2):
-        target_core = core if which == 0 else 1 - core
+    tall = held.shape[3]
+    copies = []
+    for n, side in enumerate(sides):
         for zi in range(nz):
             for qi in range(NQ):
-                at = (which * nz + zi) * rows + qi * wide
+                at = (n * nz + zi) * rows + qi * wide
                 block = jnp.concatenate([d[at : at + wide] for d in done], axis=0)
-                held[qi, zi * NC + target_core] = block.astype(BF16)
-    tall = held.shape[2]
-    copy = pltpu.make_async_copy(held, out_ref.at[:, :, pl.ds(at_row, tall)], out_sem)
-    copy.start()
-    copy.wait()
-
-
-def product(mine, other, blocks, at_row, height, unread=(), begun=None):
-    nz, rows, width = mine.shape
+                held[n, qi, zi] = block.astype(BF16)
+        owner = core if side == 0 else 1 - core
+        target = out_ref.at[:, :, owner, pl.ds(at_row, tall)]
+        copies.append(pltpu.make_async_copy(held.at[n], target, out_sem.at[n]))
+        copies[-1].start()
+    for copy in copies:
+        copy.wait()
+
+
+def product(lefts, sides, blocks, at_row, height, unread=(), begun=None, flops=None):
+    nz, rows, width = lefts[0].shape
     wide = rows // NQ
     cuts = tuple(len(block) for block in blocks)
     columns = sum(piece.shape[0] for piece in blocks[0])
     count = len(blocks)
     tall = count * columns // LANES * wide
-    flops = 2 * 2 * nz * rows * width * columns * count
+    if flops is None:
+        flops = 2 * len(lefts) * nz * rows * width * columns * count
     anywhere = pl.BlockSpec(memory_space=pltpu.HBM)
-    operands = [mine, other, *[piece for block in blocks for piece in block], *unread]
-    aliases = {}
+    operands = [*lefts, *[piece for block in blocks for piece in block], *unread]
+    ignored, aliases = len(unread), {}
     if begun is not None:
         aliases = {len(operands): 0}
         operands.append(begun)
-    return pl.pallas_call(
-        functools.partial(product_kernel, cuts, len(unread), len(aliases), at_row),
-        out_shape=jax.ShapeDtypeStruct((NQ, nz * NC, height, LANES), BF16),
+        ignored += 1
+    return pl.pallas_call(
+        functools.partial(product_kernel, sides, cuts, ignored, at_row),
+        out_shape=jax.ShapeDtypeStruct((NQ, nz, NC, height, LANES), BF16),
         in_specs=[anywhere] * len(operands),
         out_specs=pl.BlockSpec(memory_space=pl.ANY),
         scratch_shapes=[
-            pltpu.VMEM((2, nz, rows, width), BF16),
+            pltpu.VMEM((len(lefts), nz, rows, width), BF16),
             pltpu.VMEM((count, columns, width), BF16),
-            pltpu.VMEM((NQ, nz * NC, tall, LANES), BF16),
-            pltpu.SemaphoreType.DMA((2,)),
+            pltpu.VMEM((len(lefts), NQ, nz, tall, LANES), BF16),
+            pltpu.SemaphoreType.DMA((len(lefts),)),
             pltpu.SemaphoreType.DMA((sum(cuts),)),
-            pltpu.SemaphoreType.DMA,
+            pltpu.SemaphoreType.DMA((len(lefts),)),
         ],
         input_output_aliases=aliases,
         compiler_params=pltpu.CompilerParams(vmem_limit_bytes=14 * MIB),
@@ -196,22 +182,25 @@
     _, second, plane_dev = valence_pairs.shape
     own = conduction_pairs[0]
     columns = own.shape[0]
-    cut = columns * 5 // 8
+    cut = columns * 3 // 8
 
     ahead, back = along(own, 1), along(own, NH - 1)
 
-    sent = screen(valence_pairs[0], screening, NZ)
+    screened = (valence_pairs[0].astype(F32) * screening[None, :]).astype(BF16)
+    sent = jnp.broadcast_to(screened[None], (NZ, second, plane_dev))
     mine = lax.all_to_all(sent, "z", 0, 0, tiled=True)
-    mine, *rows = lax.optimization_barrier((mine, ahead[:16], back[:16], mark(screening[None])))
+    mine, *rows = lax.optimization_barrier((mine, back[:16], ahead[:16], mark(screening[None])))
     other = lax.ppermute(mine, "core", [(0, 1), (1, 0)])
 
     far = along(ahead[:cut], 1), along(back[cut:], NH - 1)
-    other, *more = lax.optimization_barrier((other, mark(back[:16])))
 
     height = NH * columns // LANES * (second // NQ)
     most = (NH - 1) * columns // LANES * (second // NQ)
-    terms = product(mine, other, ((own,), (ahead,), (back,)), 0, height, rows + more)
-    terms = product(mine, other, (far,), most, height, (), terms)
+    near = ((own,), (ahead,), (back,))
+    terms = product([mine], (0,), near, 0, height, rows, None, LONG)
+    terms = product([other], (1,), near, 0, height, (), terms)
+    terms = product([mine, other], (0, 1), (far,), most, height, (), terms)
+    terms = terms.reshape(NQ, NZ * NC, height, LANES)
     terms = lax.all_to_all(terms, ("x", "yl"), 0, 0, tiled=True)
     terms = lax.all_to_all(add(terms), ("z", "core"), 0, 0, tiled=True)
     out = finish(terms, columns)

time: 112 us -> 107 us (0.955)
  blocking collectives: 49.5 us -> 46.5 us
  waiting for transfers between devices: 22.6 us -> 20.2 us
    all_to_all x1, blocking collectives: 19.5 us -> 16.4 us  [body(): terms = lax.all_to_all(add(terms), ('z', 'core'), 0, 0, tiled=True)]
    ppermute x1, waiting for transfers between devices: 2.25 us -> 0.01 us  [body(): other = lax.ppermute(mine, 'core', [(0, 1), (1, 0)])]
    unnamed x8 -> x4, local copies, waits for them, and re-layouts: 1.59 us -> 0.01 us
  transfers between devices with their start and end apart: 6 -> 6, of which waited for: 3 -> 2; matrix products, arithmetic and copies ran while one was open for 1% -> 3% of each run, Pallas kernels for 5% -> 4%
where the time goes in v9:
time: 107 us
  blocking collectives  46.5 us (43%)
  starting transfers between devices  29.4 us (27%)
  waiting for transfers between devices  20.2 us (19%)
  Pallas kernels  7.58 us (7%)
  local copies, waits for them, and re-layouts  1.83 us (2%)
    all_to_all x1, blocking collectives, body(): terms = lax.all_to_all(terms, ('x', 'yl'), 0, 0, tiled=True)  30.2 us
    ppermute x4, starting transfers between devices, along(): return lax.ppermute(block, 'yh', [(i, (i + step) % NH) for i in range(NH)])  16.9 us
    all_to_all x1, blocking collectives, body(): terms = lax.all_to_all(add(terms), ('z', 'core'), 0, 0, tiled=True)  16.4 us
    all_to_all x1, waiting for transfers between devices, body(): mine = lax.all_to_all(sent, 'z', 0, 0, tiled=True)  12.8 us
    all_to_all x1, starting transfers between devices, body(): mine = lax.all_to_all(sent, 'z', 0, 0, tiled=True)  10 us
    ppermute x4, waiting for transfers between devices, along(): return lax.ppermute(block, 'yh', [(i, (i + step) % NH) for i in range(NH)])  7.43 us
    pallas_call x3, Pallas kernels, product(): pl.pallas_call(functools.partial(product_kernel, sides, cuts, ignored, at...  6.28 us
    ppermute x1, starting transfers between devices, body(): other = lax.ppermute(mine, 'core', [(0, 1), (1, 0)])  2.39 us
  transfers between devices with their start and end apart: 6, of which 2 were waited for; matrix products, arithmetic and copies ran while one was open for 3% of the time, Pallas kernels for 4%

profile of v9, /device:TPU:1, one launch (start us, length us, event | category | flops | bytes accessed | tf_op | source)
XLA Modules:
  0.0 106.6 jit_solution(5404174362276364799)
XLA Ops:
  0.0 6.8 %collective-permute-start = (bf16[256,1024]{1,0:T(8,128)(2,1)}, bf16[256,1024]{1,0:T(8,128)(2,1)S(1)}, u32[]{:S(2)}, u32[]{:S(2)}) collective-permute-start(bf16[256,1024]{1,0:T(8,128)(2,1)} %bitcast.7), channel_id=1, source_target_pairs={{0,48},{16,0},{32,16},{48,32},{1,49},{17,1},{33,17},{49,33},{2,50}... | collective-permute-start | bytes 1572872 | tf_op jit(solution)/shard_map/ppermute | solution.py:22
  6.8 1.9 %collective-permute-start.1 = (bf16[256,1024]{1,0:T(8,128)(2,1)}, bf16[256,1024]{1,0:T(8,128)(2,1)S(1)}, u32[]{:S(2)}, u32[]{:S(2)}) collective-permute-start(bf16[256,1024]{1,0:T(8,128)(2,1)} %bitcast.8), channel_id=1, source_target_pairs={{0,16},{16,32},{32,48},{48,0},{1,17},{17,33},{33,49},{49,1},{2,18}... | collective-permute-start | bytes 1572872 | tf_op jit(solution)/shard_map/ppermute | solution.py:22
  8.8 0.9 fusion
  9.7 1.1 %broadcast_in_dim.13 = bf16[8,64,1024]{2,1,0:T(8,128)(2,1)} broadcast(bf16[64,1024]{1,0:T(8,128)(2,1)S(1)} %fusion), dimensions={1,2} | broadcast | bytes 1179648 | tf_op jit(solution)/shard_map/broadcast_in_dim | solution.py:190
  10.8 10.0 %all-to-all-start = ((bf16[8,64,1024]{2,1,0:T(8,128)(2,1)}), bf16[8,64,1024]{2,1,0:T(8,128)(2,1)S(1)}, u32[]{:S(2)}, u32[]{:S(2)}) async-start(bf16[8,64,1024]{2,1,0:T(8,128)(2,1)} %broadcast_in_dim.13), calls=%async_computation | async-start | bytes 2097152 | tf_op jit(solution)/shard_map/all_to_all | solution.py:191
  20.8 0.0 copy-done.1
  20.8 0.0 copy-start
  20.9 7.4 %collective-permute-done.refs_3_ = bf16[256,1024]{1,0:T(8,128)(2,1)S(1)} collective-permute-done((bf16[256,1024]{1,0:T(8,128)(2,1)}, bf16[256,1024]{1,0:T(8,128)(2,1)S(1)}, u32[]{:S(2)}, u32[]{:S(2)}) %collective-permute-start) | collective-permute-done | bytes 524320 | tf_op jit(solution)/shard_map/ppermute | solution.py:22
  28.3 6.3 %collective-permute-start.4 = (bf16[160,1024]{1,0:T(8,128)(2,1)S(1)}, bf16[160,1024]{1,0:T(8,128)(2,1)S(1)}, u32[]{:S(2)}, u32[]{:S(2)}) collective-permute-start(bf16[160,1024]{1,0:T(8,128)(2,1)S(1)} %slice.19), channel_id=1, source_target_pairs={{0,48},{16,0},{32,16},{48,32},{1,49},{17,1},{33,17},{49,33},{2,50}... | collective-permute-start | bytes 983048 | tf_op jit(solution)/shard_map/ppermute | solution.py:22
  34.6 0.0 collective-permute-done.1.refs_2_
  34.6 0.7 slice.18
  35.3 1.9 %collective-permute-start.3 = (bf16[96,1024]{1,0:T(8,128)(2,1)}, bf16[96,1024]{1,0:T(8,128)(2,1)S(1)}, u32[]{:S(2)}, u32[]{:S(2)}) collective-permute-start(bf16[96,1024]{1,0:T(8,128)(2,1)} %slice.18), channel_id=1, source_target_pairs={{0,16},{16,32},{32,48},{48,0},{1,17},{17,33},{33,49},{49,1},{2,18}... | collective-permute-start | bytes 589832 | tf_op jit(solution)/shard_map/ppermute | solution.py:22
  37.2 12.8 %all-to-all-done.refs_0_ = bf16[8,64,1024]{2,1,0:T(8,128)(2,1)S(1)} async-done(((bf16[8,64,1024]{2,1,0:T(8,128)(2,1)}), bf16[8,64,1024]{2,1,0:T(8,128)(2,1)S(1)}, u32[]{:S(2)}, u32[]{:S(2)}) %all-to-all-start) | async-done | bytes 1048608 | tf_op jit(solution)/shard_map/all_to_all | solution.py:191
  50.0 2.4 %collective-permute-start.2 = (bf16[8,64,1024]{2,1,0:T(8,128)(2,1)S(1)}, bf16[8,64,1024]{2,1,0:T(8,128)(2,1)S(1)}, u32[]{:S(2)}, u32[]{:S(2)}) collective-permute-start(bf16[8,64,1024]{2,1,0:T(8,128)(2,1)S(1)} %all-to-all-done.refs_0_), channel_id=1, source_target_pairs={{0,1},{1,0},{2,3},{3,2},{4,5},{5,4},{6,7},{7,6},{8,9},{9,8},{10,11... | collective-permute-start | bytes 3145736 | tf_op jit(solution)/shard_map/ppermute | solution.py:193
  52.4 2.4 %shard_map.38.refs_4_ = bf16[8,8,2,64,128]{4,3,2,1,0:T(8,128)(2,1)S(1)} custom-call(bf16[8,64,1024]{2,1,0:T(8,128)(2,1)S(1)} %all-to-all-done.refs_0_, bf16[256,1024]{1,0:T(8,128)(2,1)S(1)} %bitcast.9, bf16[256,1024]{1,0:T(8,128)(2,1)S(1)} %collective-permute-done.1.refs_2_, bf16[256,1024]{1,0:T(8,128)(2,1)S(1)} %collective-permute-done.refs_3_, ...), custom_call_target="tpu_custom_call" | custom-call | flops 99999997952 | bytes 5242880 | tf_op jit(solution)/shard_map/pallas_call | solution.py:107
  54.8 0.0 collective-permute-done.2.refs_0_.refs_1_
  54.8 2.4 %shard_map.39.refs_4_ = bf16[8,8,2,64,128]{4,3,2,1,0:T(8,128)(2,1)S(1)} custom-call(bf16[8,64,1024]{2,1,0:T(8,128)(2,1)S(1)} %collective-permute-done.2.refs_0_.refs_1_, bf16[256,1024]{1,0:T(8,128)(2,1)S(1)} %bitcast.10, bf16[256,1024]{1,0:T(8,128)(2,1)S(1)} %collective-permute-done.1.refs_2_, ...), custom_call_target="tpu_custom_call", output_to_operand_aliasing={{}: (4, {})} | custom-call | flops 805306368 | bytes 5242880 | tf_op jit(solution)/shard_map/pallas_call | solution.py:107
  57.2 0.0 collective-permute-done.3.refs_2_
  57.2 0.0 collective-permute-done.4.refs_3_
  57.2 1.5 %shard_map.40 = bf16[8,8,2,64,128]{4,3,2,1,0:T(8,128)(2,1)S(1)} custom-call(bf16[8,64,1024]{2,1,0:T(8,128)(2,1)S(1)} %all-to-all-done.refs_0_, bf16[8,64,1024]{2,1,0:T(8,128)(2,1)S(1)} %collective-permute-done.2.refs_0_.refs_1_, bf16[96,1024]{1,0:T(8,128)(2,1)S(1)} %collective-permute-done.3.refs_2_, ...), custom_call_target="tpu_custom_call", output_to_operand_aliasing={{}: (4, {})} | custom-call | flops 536870912 | bytes 5242880 | tf_op jit(solution)/shard_map/pallas_call | solution.py:107
  58.8 30.2 %all_to_all.15.refs_0_ = bf16[8,16,64,128]{3,2,1,0:T(8,128)(2,1)S(1)} all-to-all(bf16[8,16,64,128]{3,2,1,0:T(8,128)(2,1)S(1)} %bitcast.6), channel_id=1, replica_groups=mesh['x'=4,'yl'=2,'yh'=4,'z'=8,'core'=2] {'x','yl'}, dimensions={0} | all-to-all | bytes 4194304 | tf_op jit(solution)/shard_map/all_to_all | solution.py:204
  88.9 0.5 shard_map.41
  89.4 16.4 %all_to_all.16.terms_ref = bf16[16,64,128]{2,1,0:T(8,128)(2,1)S(1)} all-to-all(bf16[16,64,128]{2,1,0:T(8,128)(2,1)S(1)} %shard_map.41), channel_id=1, replica_groups=mesh['x'=4,'yl'=2,'yh'=4,'z'=8,'core'=2] {'z','core'}, dimensions={0} | all-to-all | bytes 524288 | tf_op jit(solution)/shard_map/all_to_all | solution.py:205
  105.8 0.8 shard_map.42
  (6 shorter events, 0.0 us)
Async XLA Ops:
  0.0 20.8 %copy-start.1 = (f32[1024]{0:T(1024)S(1)}, f32[1024]{0:T(1024)}, u32[]{:S(2)}) copy-start(f32[1024]{0:T(1024)} %param.5) | copy-start | bytes 12292
  0.0 28.3 %collective-permute-start = (bf16[256,1024]{1,0:T(8,128)(2,1)}, bf16[256,1024]{1,0:T(8,128)(2,1)S(1)}, u32[]{:S(2)}, u32[]{:S(2)}) collective-permute-start(bf16[256,1024]{1,0:T(8,128)(2,1)} %bitcast.7), channel_id=1, source_target_pairs={{0,48},{16,0},{32,16},{48,32},{1,49},{17,1},{33,17},{49,33},{2,50}... | collective-permute-start | bytes 1572872 | tf_op jit(solution)/shard_map/ppermute | solution.py:22
  6.8 27.7 %collective-permute-start.1 = (bf16[256,1024]{1,0:T(8,128)(2,1)}, bf16[256,1024]{1,0:T(8,128)(2,1)S(1)}, u32[]{:S(2)}, u32[]{:S(2)}) collective-permute-start(bf16[256,1024]{1,0:T(8,128)(2,1)} %bitcast.8), channel_id=1, source_target_pairs={{0,16},{16,32},{32,48},{48,0},{1,17},{17,33},{33,49},{49,1},{2,18}... | collective-permute-start | bytes 1572872 | tf_op jit(solution)/shard_map/ppermute | solution.py:22
  10.8 39.2 %all-to-all-start = ((bf16[8,64,1024]{2,1,0:T(8,128)(2,1)}), bf16[8,64,1024]{2,1,0:T(8,128)(2,1)S(1)}, u32[]{:S(2)}, u32[]{:S(2)}) async-start(bf16[8,64,1024]{2,1,0:T(8,128)(2,1)} %broadcast_in_dim.13), calls=%async_computation | async-start | bytes 2097152 | tf_op jit(solution)/shard_map/all_to_all | solution.py:191
  20.8 31.6 %copy-start = (bf16[1,256,1024]{2,1,0:T(8,128)(2,1)S(1)}, bf16[1,256,1024]{2,1,0:T(8,128)(2,1)}, u32[]{:S(2)}) copy-start(bf16[1,256,1024]{2,1,0:T(8,128)(2,1)} %param.4) | copy-start | bytes 1572868
  28.3 28.9 %collective-permute-start.4 = (bf16[160,1024]{1,0:T(8,128)(2,1)S(1)}, bf16[160,1024]{1,0:T(8,128)(2,1)S(1)}, u32[]{:S(2)}, u32[]{:S(2)}) collective-permute-start(bf16[160,1024]{1,0:T(8,128)(2,1)S(1)} %slice.19), channel_id=1, source_target_pairs={{0,48},{16,0},{32,16},{48,32},{1,49},{17,1},{33,17},{49,33},{2,50}... | collective-permute-start | bytes 983048 | tf_op jit(solution)/shard_map/ppermute | solution.py:22
  35.3 21.9 %collective-permute-start.3 = (bf16[96,1024]{1,0:T(8,128)(2,1)}, bf16[96,1024]{1,0:T(8,128)(2,1)S(1)}, u32[]{:S(2)}, u32[]{:S(2)}) collective-permute-start(bf16[96,1024]{1,0:T(8,128)(2,1)} %slice.18), channel_id=1, source_target_pairs={{0,16},{16,32},{32,48},{48,0},{1,17},{17,33},{33,49},{49,1},{2,18}... | collective-permute-start | bytes 589832 | tf_op jit(solution)/shard_map/ppermute | solution.py:22
  50.0 4.8 %collective-permute-start.2 = (bf16[8,64,1024]{2,1,0:T(8,128)(2,1)S(1)}, bf16[8,64,1024]{2,1,0:T(8,128)(2,1)S(1)}, u32[]{:S(2)}, u32[]{:S(2)}) collective-permute-start(bf16[8,64,1024]{2,1,0:T(8,128)(2,1)S(1)} %all-to-all-done.refs_0_), channel_id=1, source_target_pairs={{0,1},{1,0},{2,3},{3,2},{4,5},{5,4},{6,7},{7,6},{8,9},{9,8},{10,11... | collective-permute-start | bytes 3145736 | tf_op jit(solution)/shard_map/ppermute | solution.py:193

commit v10 on v9

--- a/solution.py
+++ b/solution.py
@@ -18,8 +18,11 @@
 LONG = 10**11
 
 
-def along(block, step):
-    return lax.ppermute(block, "yh", [(i, (i + step) % NH) for i in range(NH)])
+def swap(block, first):
+    pairs = []
+    for i in range(first, NH + first, 2):
+        pairs += [(i, (i + 1) % NH), ((i + 1) % NH, i)]
+    return lax.ppermute(block, "yh", pairs)
 
 
 def dot(left, right):
@@ -153,11 +156,12 @@
 
 def finish_kernel(terms_ref, out_ref):
     yh = lax.axis_index("yh")
+    step = 1 - 2 * lax.rem(yh, 2)
     wide, columns = out_ref.shape[2:]
     values = terms_ref[...].astype(F32)
     at = 0
-    for offset in (0, NH - 1, 1, 2):
-        owner = lax.rem(yh + offset, NH)
+    for offset in (0, step, -step, 2):
+        owner = lax.rem(yh + NH + offset, NH)
         for c in range(0, columns, LANES):
             out_ref[owner, :, :, c : c + LANES] = values[:, at : at + wide]
             at += wide
@@ -184,19 +188,19 @@
     columns = own.shape[0]
     cut = columns * 3 // 8
 
-    ahead, back = along(own, 1), along(own, NH - 1)
+    even, odd = swap(own, 0), swap(own, 1)
 
     screened = (valence_pairs[0].astype(F32) * screening[None, :]).astype(BF16)
     sent = jnp.broadcast_to(screened[None], (NZ, second, plane_dev))
     mine = lax.all_to_all(sent, "z", 0, 0, tiled=True)
-    mine, *rows = lax.optimization_barrier((mine, back[:16], ahead[:16], mark(screening[None])))
+    mine, *rows = lax.optimization_barrier((mine, odd[:16], even[:16], mark(screening[None])))
     other = lax.ppermute(mine, "core", [(0, 1), (1, 0)])
 
-    far = along(ahead[:cut], 1), along(back[cut:], NH - 1)
+    far = swap(even[:cut], 1), swap(odd[cut:], 0)
 
     height = NH * columns // LANES * (second // NQ)
     most = (NH - 1) * columns // LANES * (second // NQ)
-    near = ((own,), (ahead,), (back,))
+    near = ((own,), (even,), (odd,))
     terms = product([mine], (0,), near, 0, height, rows, None, LONG)
     terms = product([other], (1,), near, 0, height, (), terms)
     terms = product([mine, other], (0, 1), (far,), most, height, (), terms)

time: 107 us -> 108 us (level)
  starting transfers between devices: 29.4 us -> 31 us
    ppermute x4, starting transfers between devices: 16.9 us -> 18.6 us  [swap(): return lax.ppermute(block, 'yh', pairs)]
where the time goes in v10:
time: 108 us
  blocking collectives  46.1 us (43%)
  starting transfers between devices  31 us (29%)
  waiting for transfers between devices  20.4 us (19%)
  Pallas kernels  7.59 us (7%)
  local copies, waits for them, and re-layouts  1.83 us (2%)
    all_to_all x1, blocking collectives, body(): terms = lax.all_to_all(terms, ('x', 'yl'), 0, 0, tiled=True)  30.2 us
    ppermute x4, starting transfers between devices, swap(): return lax.ppermute(block, 'yh', pairs)  18.6 us
    all_to_all x1, blocking collectives, body(): terms = lax.all_to_all(add(terms), ('z', 'core'), 0, 0, tiled=True)  15.9 us
    all_to_all x1, waiting for transfers between devices, body(): mine = lax.all_to_all(sent, 'z', 0, 0, tiled=True)  13.1 us
    all_to_all x1, starting transfers between devices, body(): mine = lax.all_to_all(sent, 'z', 0, 0, tiled=True)  10 us
    ppermute x4, waiting for transfers between devices, swap(): return lax.ppermute(block, 'yh', pairs)  7.24 us
    pallas_call x3, Pallas kernels, product(): pl.pallas_call(functools.partial(product_kernel, sides, cuts, ignored, at...  6.28 us
    ppermute x1, starting transfers between devices, body(): other = lax.ppermute(mine, 'core', [(0, 1), (1, 0)])  2.39 us
  transfers between devices with their start and end apart: 6, of which 2 were waited for; matrix products, arithmetic and copies ran while one was open for 3% of the time, Pallas kernels for 4%

profile of v10, /device:TPU:1, one launch (start us, length us, event | category | flops | bytes accessed | tf_op | source)
XLA Modules:
  0.0 108.0 jit_solution(17010270469196010586)
XLA Ops:
  0.0 6.8 %collective-permute-start = (bf16[256,1024]{1,0:T(8,128)(2,1)}, bf16[256,1024]{1,0:T(8,128)(2,1)S(1)}, u32[]{:S(2)}, u32[]{:S(2)}) collective-permute-start(bf16[256,1024]{1,0:T(8,128)(2,1)} %bitcast.7), channel_id=1, source_target_pairs={{16,32},{32,16},{48,0},{0,48},{17,33},{33,17},{49,1},{1,49},{18,34... | collective-permute-start | bytes 1572872 | tf_op jit(solution)/shard_map/ppermute | solution.py:25
  6.8 3.8 %collective-permute-start.1 = (bf16[256,1024]{1,0:T(8,128)(2,1)}, bf16[256,1024]{1,0:T(8,128)(2,1)S(1)}, u32[]{:S(2)}, u32[]{:S(2)}) collective-permute-start(bf16[256,1024]{1,0:T(8,128)(2,1)} %bitcast.8), channel_id=1, source_target_pairs={{0,16},{16,0},{32,48},{48,32},{1,17},{17,1},{33,49},{49,33},{2,18}... | collective-permute-start | bytes 1572872 | tf_op jit(solution)/shard_map/ppermute | solution.py:25
  10.6 0.9 fusion
  11.6 1.1 %broadcast_in_dim.13 = bf16[8,64,1024]{2,1,0:T(8,128)(2,1)} broadcast(bf16[64,1024]{1,0:T(8,128)(2,1)S(1)} %fusion), dimensions={1,2} | broadcast | bytes 1179648 | tf_op jit(solution)/shard_map/broadcast_in_dim | solution.py:194
  12.6 10.0 %all-to-all-start = ((bf16[8,64,1024]{2,1,0:T(8,128)(2,1)}), bf16[8,64,1024]{2,1,0:T(8,128)(2,1)S(1)}, u32[]{:S(2)}, u32[]{:S(2)}) async-start(bf16[8,64,1024]{2,1,0:T(8,128)(2,1)} %broadcast_in_dim.13), calls=%async_computation | async-start | bytes 2097152 | tf_op jit(solution)/shard_map/all_to_all | solution.py:195
  22.7 0.0 copy-done.1
  22.7 0.0 copy-start
  22.7 7.2 %collective-permute-done.refs_3_ = bf16[256,1024]{1,0:T(8,128)(2,1)S(1)} collective-permute-done((bf16[256,1024]{1,0:T(8,128)(2,1)}, bf16[256,1024]{1,0:T(8,128)(2,1)S(1)}, u32[]{:S(2)}, u32[]{:S(2)}) %collective-permute-start) | collective-permute-done | bytes 524320 | tf_op jit(solution)/shard_map/ppermute | solution.py:25
  30.0 3.5 %collective-permute-start.4 = (bf16[160,1024]{1,0:T(8,128)(2,1)S(1)}, bf16[160,1024]{1,0:T(8,128)(2,1)S(1)}, u32[]{:S(2)}, u32[]{:S(2)}) collective-permute-start(bf16[160,1024]{1,0:T(8,128)(2,1)S(1)} %slice.19), channel_id=1, source_target_pairs={{0,16},{16,0},{32,48},{48,32},{1,17},{17,1},{33,49},{49,33},{2,18}... | collective-permute-start | bytes 983048 | tf_op jit(solution)/shard_map/ppermute | solution.py:25
  33.5 0.0 collective-permute-done.1.refs_2_
  33.5 0.7 slice.18
  34.2 4.5 %collective-permute-start.3 = (bf16[96,1024]{1,0:T(8,128)(2,1)}, bf16[96,1024]{1,0:T(8,128)(2,1)S(1)}, u32[]{:S(2)}, u32[]{:S(2)}) collective-permute-start(bf16[96,1024]{1,0:T(8,128)(2,1)} %slice.18), channel_id=1, source_target_pairs={{16,32},{32,16},{48,0},{0,48},{17,33},{33,17},{49,1},{1,49},{18,34... | collective-permute-start | bytes 589832 | tf_op jit(solution)/shard_map/ppermute | solution.py:25
  38.7 13.1 %all-to-all-done.refs_0_ = bf16[8,64,1024]{2,1,0:T(8,128)(2,1)S(1)} async-done(((bf16[8,64,1024]{2,1,0:T(8,128)(2,1)}), bf16[8,64,1024]{2,1,0:T(8,128)(2,1)S(1)}, u32[]{:S(2)}, u32[]{:S(2)}) %all-to-all-start) | async-done | bytes 1048608 | tf_op jit(solution)/shard_map/all_to_all | solution.py:195
  51.9 2.4 %collective-permute-start.2 = (bf16[8,64,1024]{2,1,0:T(8,128)(2,1)S(1)}, bf16[8,64,1024]{2,1,0:T(8,128)(2,1)S(1)}, u32[]{:S(2)}, u32[]{:S(2)}) collective-permute-start(bf16[8,64,1024]{2,1,0:T(8,128)(2,1)S(1)} %all-to-all-done.refs_0_), channel_id=1, source_target_pairs={{0,1},{1,0},{2,3},{3,2},{4,5},{5,4},{6,7},{7,6},{8,9},{9,8},{10,11... | collective-permute-start | bytes 3145736 | tf_op jit(solution)/shard_map/ppermute | solution.py:197
  54.3 2.4 %shard_map.38.refs_4_ = bf16[8,8,2,64,128]{4,3,2,1,0:T(8,128)(2,1)S(1)} custom-call(bf16[8,64,1024]{2,1,0:T(8,128)(2,1)S(1)} %all-to-all-done.refs_0_, bf16[256,1024]{1,0:T(8,128)(2,1)S(1)} %bitcast.9, bf16[256,1024]{1,0:T(8,128)(2,1)S(1)} %collective-permute-done.1.refs_2_, bf16[256,1024]{1,0:T(8,128)(2,1)S(1)} %collective-permute-done.refs_3_, ...), custom_call_target="tpu_custom_call" | custom-call | flops 99999997952 | bytes 5242880 | tf_op jit(solution)/shard_map/pallas_call | solution.py:110
  56.7 0.0 collective-permute-done.2.refs_0_.refs_1_
  56.7 2.4 %shard_map.39.refs_4_ = bf16[8,8,2,64,128]{4,3,2,1,0:T(8,128)(2,1)S(1)} custom-call(bf16[8,64,1024]{2,1,0:T(8,128)(2,1)S(1)} %collective-permute-done.2.refs_0_.refs_1_, bf16[256,1024]{1,0:T(8,128)(2,1)S(1)} %bitcast.10, bf16[256,1024]{1,0:T(8,128)(2,1)S(1)} %collective-permute-done.1.refs_2_, ...), custom_call_target="tpu_custom_call", output_to_operand_aliasing={{}: (4, {})} | custom-call | flops 805306368 | bytes 5242880 | tf_op jit(solution)/shard_map/pallas_call | solution.py:110
  59.1 0.0 collective-permute-done.3.refs_2_
  59.1 0.0 collective-permute-done.4.refs_3_
  59.1 1.5 %shard_map.40 = bf16[8,8,2,64,128]{4,3,2,1,0:T(8,128)(2,1)S(1)} custom-call(bf16[8,64,1024]{2,1,0:T(8,128)(2,1)S(1)} %all-to-all-done.refs_0_, bf16[8,64,1024]{2,1,0:T(8,128)(2,1)S(1)} %collective-permute-done.2.refs_0_.refs_1_, bf16[96,1024]{1,0:T(8,128)(2,1)S(1)} %collective-permute-done.3.refs_2_, ...), custom_call_target="tpu_custom_call", output_to_operand_aliasing={{}: (4, {})} | custom-call | flops 536870912 | bytes 5242880 | tf_op jit(solution)/shard_map/pallas_call | solution.py:110
  60.6 30.2 %all_to_all.15.refs_0_ = bf16[8,16,64,128]{3,2,1,0:T(8,128)(2,1)S(1)} all-to-all(bf16[8,16,64,128]{3,2,1,0:T(8,128)(2,1)S(1)} %bitcast.6), channel_id=1, replica_groups=mesh['x'=4,'yl'=2,'yh'=4,'z'=8,'core'=2] {'x','yl'}, dimensions={0} | all-to-all | bytes 4194304 | tf_op jit(solution)/shard_map/all_to_all | solution.py:208
  90.8 0.5 shard_map.41
  91.3 15.9 %all_to_all.16.terms_ref = bf16[16,64,128]{2,1,0:T(8,128)(2,1)S(1)} all-to-all(bf16[16,64,128]{2,1,0:T(8,128)(2,1)S(1)} %shard_map.41), channel_id=1, replica_groups=mesh['x'=4,'yl'=2,'yh'=4,'z'=8,'core'=2] {'z','core'}, dimensions={0} | all-to-all | bytes 524288 | tf_op jit(solution)/shard_map/all_to_all | solution.py:209
  107.2 0.8 shard_map.42
  (6 shorter events, 0.0 us)
Async XLA Ops:
  0.0 22.7 %copy-start.1 = (f32[1024]{0:T(1024)S(1)}, f32[1024]{0:T(1024)}, u32[]{:S(2)}) copy-start(f32[1024]{0:T(1024)} %param.5) | copy-start | bytes 12292
  0.0 29.9 %collective-permute-start = (bf16[256,1024]{1,0:T(8,128)(2,1)}, bf16[256,1024]{1,0:T(8,128)(2,1)S(1)}, u32[]{:S(2)}, u32[]{:S(2)}) collective-permute-start(bf16[256,1024]{1,0:T(8,128)(2,1)} %bitcast.7), channel_id=1, source_target_pairs={{16,32},{32,16},{48,0},{0,48},{17,33},{33,17},{49,1},{1,49},{18,34... | collective-permute-start | bytes 1572872 | tf_op jit(solution)/shard_map/ppermute | solution.py:25
  6.8 26.7 %collective-permute-start.1 = (bf16[256,1024]{1,0:T(8,128)(2,1)}, bf16[256,1024]{1,0:T(8,128)(2,1)S(1)}, u32[]{:S(2)}, u32[]{:S(2)}) collective-permute-start(bf16[256,1024]{1,0:T(8,128)(2,1)} %bitcast.8), channel_id=1, source_target_pairs={{0,16},{16,0},{32,48},{48,32},{1,17},{17,1},{33,49},{49,33},{2,18}... | collective-permute-start | bytes 1572872 | tf_op jit(solution)/shard_map/ppermute | solution.py:25
  12.6 39.2 %all-to-all-start = ((bf16[8,64,1024]{2,1,0:T(8,128)(2,1)}), bf16[8,64,1024]{2,1,0:T(8,128)(2,1)S(1)}, u32[]{:S(2)}, u32[]{:S(2)}) async-start(bf16[8,64,1024]{2,1,0:T(8,128)(2,1)} %broadcast_in_dim.13), calls=%async_computation | async-start | bytes 2097152 | tf_op jit(solution)/shard_map/all_to_all | solution.py:195
  22.7 31.6 %copy-start = (bf16[1,256,1024]{2,1,0:T(8,128)(2,1)S(1)}, bf16[1,256,1024]{2,1,0:T(8,128)(2,1)}, u32[]{:S(2)}) copy-start(bf16[1,256,1024]{2,1,0:T(8,128)(2,1)} %param.4) | copy-start | bytes 1572868
  30.0 29.1 %collective-permute-start.4 = (bf16[160,1024]{1,0:T(8,128)(2,1)S(1)}, bf16[160,1024]{1,0:T(8,128)(2,1)S(1)}, u32[]{:S(2)}, u32[]{:S(2)}) collective-permute-start(bf16[160,1024]{1,0:T(8,128)(2,1)S(1)} %slice.19), channel_id=1, source_target_pairs={{0,16},{16,0},{32,48},{48,32},{1,17},{17,1},{33,49},{49,33},{2,18}... | collective-permute-start | bytes 983048 | tf_op jit(solution)/shard_map/ppermute | solution.py:25
  34.2 24.8 %collective-permute-start.3 = (bf16[96,1024]{1,0:T(8,128)(2,1)}, bf16[96,1024]{1,0:T(8,128)(2,1)S(1)}, u32[]{:S(2)}, u32[]{:S(2)}) collective-permute-start(bf16[96,1024]{1,0:T(8,128)(2,1)} %slice.18), channel_id=1, source_target_pairs={{16,32},{32,16},{48,0},{0,48},{17,33},{33,17},{49,1},{1,49},{18,34... | collective-permute-start | bytes 589832 | tf_op jit(solution)/shard_map/ppermute | solution.py:25
  51.9 4.8 %collective-permute-start.2 = (bf16[8,64,1024]{2,1,0:T(8,128)(2,1)S(1)}, bf16[8,64,1024]{2,1,0:T(8,128)(2,1)S(1)}, u32[]{:S(2)}, u32[]{:S(2)}) collective-permute-start(bf16[8,64,1024]{2,1,0:T(8,128)(2,1)S(1)} %all-to-all-done.refs_0_), channel_id=1, source_target_pairs={{0,1},{1,0},{2,3},{3,2},{4,5},{5,4},{6,7},{7,6},{8,9},{9,8},{10,11... | collective-permute-start | bytes 3145736 | tf_op jit(solution)/shard_map/ppermute | solution.py:197

commit v11 on v9

--- a/solution.py
+++ b/solution.py
@@ -184,19 +184,21 @@
     columns = own.shape[0]
     cut = columns * 3 // 8
 
-    ahead, back = along(own, 1), along(own, NH - 1)
+    low, high = own[:cut], own[cut:]
+    back_high, ahead_low = along(high, NH - 1), along(low, 1)
+    back_low, ahead_high = along(low, NH - 1), along(high, 1)
 
     screened = (valence_pairs[0].astype(F32) * screening[None, :]).astype(BF16)
     sent = jnp.broadcast_to(screened[None], (NZ, second, plane_dev))
     mine = lax.all_to_all(sent, "z", 0, 0, tiled=True)
-    mine, *rows = lax.optimization_barrier((mine, back[:16], ahead[:16], mark(screening[None])))
+    mine, *rows = lax.optimization_barrier((mine, back_high[:16], ahead_low[:16], mark(screening[None])))
     other = lax.ppermute(mine, "core", [(0, 1), (1, 0)])
 
-    far = along(ahead[:cut], 1), along(back[cut:], NH - 1)
+    far = along(ahead_low, 1), along(back_high, NH - 1)
 
     height = NH * columns // LANES * (second // NQ)
     most = (NH - 1) * columns // LANES * (second // NQ)
-    near = ((own,), (ahead,), (back,))
+    near = ((own,), (ahead_low, ahead_high), (back_low, back_high))
     terms = product([mine], (0,), near, 0, height, rows, None, LONG)
     terms = product([other], (1,), near, 0, height, (), terms)
     terms = product([mine, other], (0, 1), (far,), most, height, (), terms)

time: 107 us -> 118 us (1.10)
  starting transfers between devices: 29.4 us -> 36 us
  local copies, waits for them, and re-layouts: 1.83 us -> 3.74 us
  waiting for transfers between devices: 20.2 us -> 21.6 us
  Pallas kernels: 7.58 us -> 8.91 us
    all_to_all x1, waiting for transfers between devices: 12.8 us -> 21.6 us  [body(): mine = lax.all_to_all(sent, 'z', 0, 0, tiled=True)]
    ppermute x4 -> x6, waiting for transfers between devices: 7.43 us -> 0.02 us  [along(): return lax.ppermute(block, 'yh', [(i, (i + step) % NH) for i in range(NH)])]
    ppermute x4 -> x6, starting transfers between devices: 16.9 us -> 23.5 us  [along(): return lax.ppermute(block, 'yh', [(i, (i + step) % NH) for i in range(NH)])]
    slice x4, local copies, waits for them, and re-layouts: 0.72 us -> 2.62 us  [the longest x2 2.61 us: body(): low, high = (own[:cut], own[cut:])]
    pallas_call x3, Pallas kernels: 6.28 us -> 7.61 us  [product(): pl.pallas_call(functools.partial(product_kernel, sides, cuts, ignored, at...]
  transfers between devices with their start and end apart: 6 -> 8, of which waited for: 2 -> 1; matrix products, arithmetic and copies ran while one was open for 3% -> 3% of each run, Pallas kernels for 4% -> 5%
where the time goes in v11:
time: 118 us; the launch traced here: 117 us
  blocking collectives  46.1 us (39%)
  starting transfers between devices  36 us (31%)
  waiting for transfers between devices  21.6 us (18%)
  Pallas kernels  8.91 us (8%)
  local copies, waits for them, and re-layouts  3.74 us (3%)
    all_to_all x1, blocking collectives, body(): terms = lax.all_to_all(terms, ('x', 'yl'), 0, 0, tiled=True)  30.7 us
    ppermute x6, starting transfers between devices, along(): return lax.ppermute(block, 'yh', [(i, (i + step) % NH) for i in range(NH)])  23.5 us
    all_to_all x1, waiting for transfers between devices, body(): mine = lax.all_to_all(sent, 'z', 0, 0, tiled=True)  21.6 us
    all_to_all x1, blocking collectives, body(): terms = lax.all_to_all(add(terms), ('z', 'core'), 0, 0, tiled=True)  15.4 us
    all_to_all x1, starting transfers between devices, body(): mine = lax.all_to_all(sent, 'z', 0, 0, tiled=True)  10 us
    pallas_call x3, Pallas kernels, product(): pl.pallas_call(functools.partial(product_kernel, sides, cuts, ignored, at...  7.61 us
    slice x2, local copies, waits for them, and re-layouts, body(): low, high = (own[:cut], own[cut:])  2.61 us
    ppermute x1, starting transfers between devices, body(): other = lax.ppermute(mine, 'core', [(0, 1), (1, 0)])  2.39 us
  transfers between devices with their start and end apart: 8, of which 1 were waited for; matrix products, arithmetic and copies ran while one was open for 3% of the time, Pallas kernels for 5%

profile of v11, /device:TPU:1, one launch (start us, length us, event | category | flops | bytes accessed | tf_op | source)
XLA Modules:
  0.0 117.4 jit_solution(10822311079495436098)
XLA Ops:
  0.0 1.0 slice_bitcast_fusion
  1.0 0.0 copy-start.1
  1.0 6.7 %collective-permute-start = (bf16[160,1024]{1,0:T(8,128)(2,1)S(1)}, bf16[160,1024]{1,0:T(8,128)(2,1)S(1)}, u32[]{:S(2)}, u32[]{:S(2)}) collective-permute-start(bf16[160,1024]{1,0:T(8,128)(2,1)S(1)} %slice_bitcast_fusion), channel_id=1, source_target_pairs={{0,48},{16,0},{32,16},{48,32},{1,49},{17,1},{33,17},{49,33},{2,50}... | collective-permute-start | bytes 983048 | tf_op jit(solution)/shard_map/ppermute | solution.py:22
  7.7 1.9 %collective-permute-start.5 = (bf16[160,1024]{1,0:T(8,128)(2,1)S(1)}, bf16[160,1024]{1,0:T(8,128)(2,1)S(1)}, u32[]{:S(2)}, u32[]{:S(2)}) collective-permute-start(bf16[160,1024]{1,0:T(8,128)(2,1)S(1)} %slice_bitcast_fusion), channel_id=1, source_target_pairs={{0,16},{16,32},{32,48},{48,0},{1,17},{17,33},{33,49},{49,1},{2,18}... | collective-permute-start | bytes 983048 | tf_op jit(solution)/shard_map/ppermute | solution.py:22
  9.7 1.6 %slice_bitcast_fusion.1 = bf16[96,1024]{1,0:T(8,128)(2,1)} fusion(bf16[1,256,1024]{2,1,0:T(8,128)(2,1)} %param.4), kind=kLoop, calls=%fused_computation.2 | loop fusion | bytes 393216 | tf_op jit(solution)/shard_map/slice | solution.py:187
  11.3 3.8 %collective-permute-start.1 = (bf16[96,1024]{1,0:T(8,128)(2,1)}, bf16[96,1024]{1,0:T(8,128)(2,1)S(1)}, u32[]{:S(2)}, u32[]{:S(2)}) collective-permute-start(bf16[96,1024]{1,0:T(8,128)(2,1)} %slice_bitcast_fusion.1), channel_id=1, source_target_pairs={{0,16},{16,32},{32,48},{48,0},{1,17},{17,33},{33,49},{49,1},{2,18}... | collective-permute-start | bytes 589832 | tf_op jit(solution)/shard_map/ppermute | solution.py:22
  15.1 3.6 %collective-permute-start.6 = (bf16[96,1024]{1,0:T(8,128)(2,1)}, bf16[96,1024]{1,0:T(8,128)(2,1)S(1)}, u32[]{:S(2)}, u32[]{:S(2)}) collective-permute-start(bf16[96,1024]{1,0:T(8,128)(2,1)} %slice_bitcast_fusion.1), channel_id=1, source_target_pairs={{0,48},{16,0},{32,16},{48,32},{1,49},{17,1},{33,17},{49,33},{2,50}... | collective-permute-start | bytes 589832 | tf_op jit(solution)/shard_map/ppermute | solution.py:22
  18.7 0.9 fusion
  19.6 1.1 broadcast_in_dim.13
  20.7 10.0 %all-to-all-start = ((bf16[8,64,1024]{2,1,0:T(8,128)(2,1)}), bf16[8,64,1024]{2,1,0:T(8,128)(2,1)S(1)}, u32[]{:S(2)}, u32[]{:S(2)}) async-start(bf16[8,64,1024]{2,1,0:T(8,128)(2,1)} %broadcast_in_dim.13), calls=%async_computation | async-start | bytes 2097152 | tf_op jit(solution)/shard_map/all_to_all | solution.py:193
  30.8 0.0 copy-start
  30.8 0.0 collective-permute-done.1.refs_2_
  30.8 2.7 %collective-permute-start.3 = (bf16[96,1024]{1,0:T(8,128)(2,1)S(1)}, bf16[96,1024]{1,0:T(8,128)(2,1)S(1)}, u32[]{:S(2)}, u32[]{:S(2)}) collective-permute-start(bf16[96,1024]{1,0:T(8,128)(2,1)S(1)} %collective-permute-done.1.refs_2_), channel_id=1, source_target_pairs={{0,16},{16,32},{32,48},{48,0},{1,17},{17,33},{33,49},{49,1},{2,18}... | collective-permute-start | bytes 589832 | tf_op jit(solution)/shard_map/ppermute | solution.py:22
  33.5 0.0 collective-permute-done.refs_5_
  33.6 4.8 %collective-permute-start.4 = (bf16[160,1024]{1,0:T(8,128)(2,1)S(1)}, bf16[160,1024]{1,0:T(8,128)(2,1)S(1)}, u32[]{:S(2)}, u32[]{:S(2)}) collective-permute-start(bf16[160,1024]{1,0:T(8,128)(2,1)S(1)} %collective-permute-done.refs_5_), channel_id=1, source_target_pairs={{0,48},{16,0},{32,16},{48,32},{1,49},{17,1},{33,17},{49,33},{2,50}... | collective-permute-start | bytes 983048 | tf_op jit(solution)/shard_map/ppermute | solution.py:22
  38.4 21.6 %all-to-all-done.refs_0_ = bf16[8,64,1024]{2,1,0:T(8,128)(2,1)S(1)} async-done(((bf16[8,64,1024]{2,1,0:T(8,128)(2,1)}), bf16[8,64,1024]{2,1,0:T(8,128)(2,1)S(1)}, u32[]{:S(2)}, u32[]{:S(2)}) %all-to-all-start) | async-done | bytes 1048608 | tf_op jit(solution)/shard_map/all_to_all | solution.py:193
  59.9 2.4 %collective-permute-start.2 = (bf16[8,64,1024]{2,1,0:T(8,128)(2,1)S(1)}, bf16[8,64,1024]{2,1,0:T(8,128)(2,1)S(1)}, u32[]{:S(2)}, u32[]{:S(2)}) collective-permute-start(bf16[8,64,1024]{2,1,0:T(8,128)(2,1)S(1)} %all-to-all-done.refs_0_), channel_id=1, source_target_pairs={{0,1},{1,0},{2,3},{3,2},{4,5},{5,4},{6,7},{7,6},{8,9},{9,8},{10,11... | collective-permute-start | bytes 3145736 | tf_op jit(solution)/shard_map/ppermute | solution.py:195
  62.4 3.0 %shard_map.38.refs_6_ = bf16[8,8,2,64,128]{4,3,2,1,0:T(8,128)(2,1)S(1)} custom-call(bf16[8,64,1024]{2,1,0:T(8,128)(2,1)S(1)} %all-to-all-done.refs_0_, bf16[256,1024]{1,0:T(8,128)(2,1)S(1)} %bitcast.11, bf16[96,1024]{1,0:T(8,128)(2,1)S(1)} %collective-permute-done.1.refs_2_, bf16[160,1024]{1,0:T(8,128)(2,1)S(1)} %collective-permute-done.5.refs_3_, ...), custom_call_target="tpu_custom_call" | custom-call | flops 99999997952 | bytes 5242880 | tf_op jit(solution)/shard_map/pallas_call | solution.py:107
  65.4 3.0 %shard_map.39.refs_4_ = bf16[8,8,2,64,128]{4,3,2,1,0:T(8,128)(2,1)S(1)} custom-call(bf16[8,64,1024]{2,1,0:T(8,128)(2,1)S(1)} %collective-permute-done.2.refs_0_.refs_1_, bf16[256,1024]{1,0:T(8,128)(2,1)S(1)} %bitcast.12, bf16[96,1024]{1,0:T(8,128)(2,1)S(1)} %collective-permute-done.1.refs_2_, ...), custom_call_target="tpu_custom_call", output_to_operand_aliasing={{}: (6, {})} | custom-call | flops 805306368 | bytes 5242880 | tf_op jit(solution)/shard_map/pallas_call | solution.py:107
  68.5 1.5 %shard_map.40 = bf16[8,8,2,64,128]{4,3,2,1,0:T(8,128)(2,1)S(1)} custom-call(bf16[8,64,1024]{2,1,0:T(8,128)(2,1)S(1)} %all-to-all-done.refs_0_, bf16[8,64,1024]{2,1,0:T(8,128)(2,1)S(1)} %collective-permute-done.2.refs_0_.refs_1_, bf16[96,1024]{1,0:T(8,128)(2,1)S(1)} %collective-permute-done.3.refs_2_, ...), custom_call_target="tpu_custom_call", output_to_operand_aliasing={{}: (4, {})} | custom-call | flops 536870912 | bytes 5242880 | tf_op jit(solution)/shard_map/pallas_call | solution.py:107
  70.0 30.7 %all_to_all.15.refs_0_ = bf16[8,16,64,128]{3,2,1,0:T(8,128)(2,1)S(1)} all-to-all(bf16[8,16,64,128]{3,2,1,0:T(8,128)(2,1)S(1)} %bitcast.10), channel_id=1, replica_groups=mesh['x'=4,'yl'=2,'yh'=4,'z'=8,'core'=2] {'x','yl'}, dimensions={0} | all-to-all | bytes 4194304 | tf_op jit(solution)/shard_map/all_to_all | solution.py:206
  100.7 0.5 shard_map.41
  101.2 15.4 %all_to_all.16.terms_ref = bf16[16,64,128]{2,1,0:T(8,128)(2,1)S(1)} all-to-all(bf16[16,64,128]{2,1,0:T(8,128)(2,1)S(1)} %shard_map.41), channel_id=1, replica_groups=mesh['x'=4,'yl'=2,'yh'=4,'z'=8,'core'=2] {'z','core'}, dimensions={0} | all-to-all | bytes 524288 | tf_op jit(solution)/shard_map/all_to_all | solution.py:207
  116.6 0.8 shard_map.42
  (10 shorter events, 0.0 us)
Async XLA Ops:
  1.0 29.8 %copy-start.1 = (f32[1024]{0:T(1024)S(1)}, f32[1024]{0:T(1024)}, u32[]{:S(2)}) copy-start(f32[1024]{0:T(1024)} %param.5) | copy-start | bytes 12292
  1.0 32.5 %collective-permute-start = (bf16[160,1024]{1,0:T(8,128)(2,1)S(1)}, bf16[160,1024]{1,0:T(8,128)(2,1)S(1)}, u32[]{:S(2)}, u32[]{:S(2)}) collective-permute-start(bf16[160,1024]{1,0:T(8,128)(2,1)S(1)} %slice_bitcast_fusion), channel_id=1, source_target_pairs={{0,48},{16,0},{32,16},{48,32},{1,49},{17,1},{33,17},{49,33},{2,50}... | collective-permute-start | bytes 983048 | tf_op jit(solution)/shard_map/ppermute | solution.py:22
  7.7 54.6 %collective-permute-start.5 = (bf16[160,1024]{1,0:T(8,128)(2,1)S(1)}, bf16[160,1024]{1,0:T(8,128)(2,1)S(1)}, u32[]{:S(2)}, u32[]{:S(2)}) collective-permute-start(bf16[160,1024]{1,0:T(8,128)(2,1)S(1)} %slice_bitcast_fusion), channel_id=1, source_target_pairs={{0,16},{16,32},{32,48},{48,0},{1,17},{17,33},{33,49},{49,1},{2,18}... | collective-permute-start | bytes 983048 | tf_op jit(solution)/shard_map/ppermute | solution.py:22
  11.3 19.5 %collective-permute-start.1 = (bf16[96,1024]{1,0:T(8,128)(2,1)}, bf16[96,1024]{1,0:T(8,128)(2,1)S(1)}, u32[]{:S(2)}, u32[]{:S(2)}) collective-permute-start(bf16[96,1024]{1,0:T(8,128)(2,1)} %slice_bitcast_fusion.1), channel_id=1, source_target_pairs={{0,16},{16,32},{32,48},{48,0},{1,17},{17,33},{33,49},{49,1},{2,18}... | collective-permute-start | bytes 589832 | tf_op jit(solution)/shard_map/ppermute | solution.py:22
  15.1 47.3 %collective-permute-start.6 = (bf16[96,1024]{1,0:T(8,128)(2,1)}, bf16[96,1024]{1,0:T(8,128)(2,1)S(1)}, u32[]{:S(2)}, u32[]{:S(2)}) collective-permute-start(bf16[96,1024]{1,0:T(8,128)(2,1)} %slice_bitcast_fusion.1), channel_id=1, source_target_pairs={{0,48},{16,0},{32,16},{48,32},{1,49},{17,1},{33,17},{49,33},{2,50}... | collective-permute-start | bytes 589832 | tf_op jit(solution)/shard_map/ppermute | solution.py:22
  20.7 39.2 %all-to-all-start = ((bf16[8,64,1024]{2,1,0:T(8,128)(2,1)}), bf16[8,64,1024]{2,1,0:T(8,128)(2,1)S(1)}, u32[]{:S(2)}, u32[]{:S(2)}) async-start(bf16[8,64,1024]{2,1,0:T(8,128)(2,1)} %broadcast_in_dim.13), calls=%async_computation | async-start | bytes 2097152 | tf_op jit(solution)/shard_map/all_to_all | solution.py:193
  30.8 31.6 %copy-start = (bf16[1,256,1024]{2,1,0:T(8,128)(2,1)S(1)}, bf16[1,256,1024]{2,1,0:T(8,128)(2,1)}, u32[]{:S(2)}) copy-start(bf16[1,256,1024]{2,1,0:T(8,128)(2,1)} %param.4) | copy-start | bytes 1572868
  30.8 37.7 %collective-permute-start.3 = (bf16[96,1024]{1,0:T(8,128)(2,1)S(1)}, bf16[96,1024]{1,0:T(8,128)(2,1)S(1)}, u32[]{:S(2)}, u32[]{:S(2)}) collective-permute-start(bf16[96,1024]{1,0:T(8,128)(2,1)S(1)} %collective-permute-done.1.refs_2_), channel_id=1, source_target_pairs={{0,16},{16,32},{32,48},{48,0},{1,17},{17,33},{33,49},{49,1},{2,18}... | collective-permute-start | bytes 589832 | tf_op jit(solution)/shard_map/ppermute | solution.py:22
  33.6 34.9 %collective-permute-start.4 = (bf16[160,1024]{1,0:T(8,128)(2,1)S(1)}, bf16[160,1024]{1,0:T(8,128)(2,1)S(1)}, u32[]{:S(2)}, u32[]{:S(2)}) collective-permute-start(bf16[160,1024]{1,0:T(8,128)(2,1)S(1)} %collective-permute-done.refs_5_), channel_id=1, source_target_pairs={{0,48},{16,0},{32,16},{48,32},{1,49},{17,1},{33,17},{49,33},{2,50}... | collective-permute-start | bytes 983048 | tf_op jit(solution)/shard_map/ppermute | solution.py:22
  59.9 5.5 %collective-permute-start.2 = (bf16[8,64,1024]{2,1,0:T(8,128)(2,1)S(1)}, bf16[8,64,1024]{2,1,0:T(8,128)(2,1)S(1)}, u32[]{:S(2)}, u32[]{:S(2)}) collective-permute-start(bf16[8,64,1024]{2,1,0:T(8,128)(2,1)S(1)} %all-to-all-done.refs_0_), channel_id=1, source_target_pairs={{0,1},{1,0},{2,3},{3,2},{4,5},{5,4},{6,7},{7,6},{8,9},{9,8},{10,11... | collective-permute-start | bytes 3145736 | tf_op jit(solution)/shard_map/ppermute | solution.py:195

commit v12 on v11

--- a/solution.py
+++ b/solution.py
@@ -24,19 +24,6 @@
 
 def dot(left, right):
     return lax.dot_general(left, right, (((1,), (1,)), ((), ())), preferred_element_type=F32)
-
-
-def mark_kernel(seen_ref, out_ref):
-    out_ref[...] = seen_ref[...]
-
-
-def mark(seen):
-    return pl.pallas_call(
-        mark_kernel,
-        out_shape=jax.ShapeDtypeStruct(seen.shape, seen.dtype),
-        compiler_params=pltpu.CompilerParams(vmem_limit_bytes=MIB),
-        cost_estimate=pl.CostEstimate(flops=LONG, bytes_accessed=10**8, transcendentals=0),
-    )(seen)
 
 
 def product_kernel(sides, cuts, ignored, at_row, *refs):
@@ -191,7 +178,7 @@
     screened = (valence_pairs[0].astype(F32) * screening[None, :]).astype(BF16)
     sent = jnp.broadcast_to(screened[None], (NZ, second, plane_dev))
     mine = lax.all_to_all(sent, "z", 0, 0, tiled=True)
-    mine, *rows = lax.optimization_barrier((mine, back_high[:16], ahead_low[:16], mark(screening[None])))
+    mine, *rows = lax.optimization_barrier((mine, back_high[:16], ahead_low[:16]))
     other = lax.ppermute(mine, "core", [(0, 1), (1, 0)])
 
     far = along(ahead_low, 1), along(back_high, NH - 1)

time: 118 us -> 120 us (1.017)
  blocking collectives: 46.1 us -> 57.5 us
  waiting for transfers between devices: 21.6 us -> 10.4 us
  starting transfers between devices: 36 us -> 39 us
  local copies, waits for them, and re-layouts: 3.74 us -> 1.82 us
    all_to_all x1, waiting for transfers between devices: 21.6 us -> 0.01 us  [body(): mine = lax.all_to_all(sent, 'z', 0, 0, tiled=True)]
    ppermute x6, waiting for transfers between devices: 0.02 us -> 10.4 us  [along(): return lax.ppermute(block, 'yh', [(i, (i + step) % NH) for i in range(NH)])]
    all_to_all x1, blocking collectives: 15.4 us -> 21.2 us  [body(): terms = lax.all_to_all(add(terms), ('z', 'core'), 0, 0, tiled=True)]
    all_to_all x1, blocking collectives: 30.7 us -> 36.3 us  [body(): terms = lax.all_to_all(terms, ('x', 'yl'), 0, 0, tiled=True)]
    ppermute x1, starting transfers between devices: 2.39 us -> 5.61 us  [body(): other = lax.ppermute(mine, 'core', [(0, 1), (1, 0)])]
    slice x2, local copies, waits for them, and re-layouts: 2.61 us -> 0.71 us  [body(): low, high = (own[:cut], own[cut:])]
  transfers between devices with their start and end apart: 8 -> 8, of which waited for: 1 -> 1; matrix products, arithmetic and copies ran while one was open for 3% -> 1% of each run, Pallas kernels for 5% -> 5%
where the time goes in v12:
time: 120 us; the launch traced here: 119 us
  blocking collectives  57.5 us (48%)
  starting transfers between devices  39 us (32%)
  waiting for transfers between devices  10.4 us (9%)
  Pallas kernels  8.9 us (7%)
  local copies, waits for them, and re-layouts  1.82 us (2%)
    all_to_all x1, blocking collectives, body(): terms = lax.all_to_all(terms, ('x', 'yl'), 0, 0, tiled=True)  36.3 us
    ppermute x6, starting transfers between devices, along(): return lax.ppermute(block, 'yh', [(i, (i + step) % NH) for i in range(NH)])  22.6 us
    all_to_all x1, blocking collectives, body(): terms = lax.all_to_all(add(terms), ('z', 'core'), 0, 0, tiled=True)  21.2 us
    all_to_all x1, starting transfers between devices, body(): mine = lax.all_to_all(sent, 'z', 0, 0, tiled=True)  10.9 us
    ppermute x6, waiting for transfers between devices, along(): return lax.ppermute(block, 'yh', [(i, (i + step) % NH) for i in range(NH)])  10.4 us
    pallas_call x3, Pallas kernels, product(): pl.pallas_call(functools.partial(product_kernel, sides, cuts, ignored, at...  7.6 us
    ppermute x1, starting transfers between devices, body(): other = lax.ppermute(mine, 'core', [(0, 1), (1, 0)])  5.61 us
  transfers between devices with their start and end apart: 8, of which 1 were waited for; matrix products, arithmetic and copies ran while one was open for 1% of the time, Pallas kernels for 5%

profile of v12, /device:TPU:1, one launch (start us, length us, event | category | flops | bytes accessed | tf_op | source)
XLA Modules:
  0.0 118.9 jit_solution(2536488911105406535)
XLA Ops:
  0.0 1.0 fusion
  1.0 1.1 broadcast_in_dim.10
  2.1 10.9 %all-to-all-start = ((bf16[8,64,1024]{2,1,0:T(8,128)(2,1)}), bf16[8,64,1024]{2,1,0:T(8,128)(2,1)S(1)}, u32[]{:S(2)}, u32[]{:S(2)}) async-start(bf16[8,64,1024]{2,1,0:T(8,128)(2,1)} %broadcast_in_dim.10), calls=%async_computation | async-start | bytes 2097152 | tf_op jit(solution)/shard_map/all_to_all | solution.py:180
  13.0 5.9 %collective-permute-start = (bf16[160,1024]{1,0:T(8,128)(2,1)S(1)}, bf16[160,1024]{1,0:T(8,128)(2,1)S(1)}, u32[]{:S(2)}, u32[]{:S(2)}) collective-permute-start(bf16[160,1024]{1,0:T(8,128)(2,1)S(1)} %slice_bitcast_fusion), channel_id=1, source_target_pairs={{0,48},{16,0},{32,16},{48,32},{1,49},{17,1},{33,17},{49,33},{2,50}... | collective-permute-start | bytes 983048 | tf_op jit(solution)/shard_map/ppermute | solution.py:22
  18.9 1.9 %collective-permute-start.5 = (bf16[160,1024]{1,0:T(8,128)(2,1)S(1)}, bf16[160,1024]{1,0:T(8,128)(2,1)S(1)}, u32[]{:S(2)}, u32[]{:S(2)}) collective-permute-start(bf16[160,1024]{1,0:T(8,128)(2,1)S(1)} %slice_bitcast_fusion), channel_id=1, source_target_pairs={{0,16},{16,32},{32,48},{48,0},{1,17},{17,33},{33,49},{49,1},{2,18}... | collective-permute-start | bytes 983048 | tf_op jit(solution)/shard_map/ppermute | solution.py:22
  20.8 0.7 slice_bitcast_fusion.1
  21.5 3.8 %collective-permute-start.1 = (bf16[96,1024]{1,0:T(8,128)(2,1)}, bf16[96,1024]{1,0:T(8,128)(2,1)S(1)}, u32[]{:S(2)}, u32[]{:S(2)}) collective-permute-start(bf16[96,1024]{1,0:T(8,128)(2,1)} %slice_bitcast_fusion.1), channel_id=1, source_target_pairs={{0,16},{16,32},{32,48},{48,0},{1,17},{17,33},{33,49},{49,1},{2,18}... | collective-permute-start | bytes 589832 | tf_op jit(solution)/shard_map/ppermute | solution.py:22
  25.3 3.6 %collective-permute-start.6 = (bf16[96,1024]{1,0:T(8,128)(2,1)}, bf16[96,1024]{1,0:T(8,128)(2,1)S(1)}, u32[]{:S(2)}, u32[]{:S(2)}) collective-permute-start(bf16[96,1024]{1,0:T(8,128)(2,1)} %slice_bitcast_fusion.1), channel_id=1, source_target_pairs={{0,48},{16,0},{32,16},{48,32},{1,49},{17,1},{33,17},{49,33},{2,50}... | collective-permute-start | bytes 589832 | tf_op jit(solution)/shard_map/ppermute | solution.py:22
  28.9 10.4 %collective-permute-done.1.refs_2_ = bf16[96,1024]{1,0:T(8,128)(2,1)S(1)} collective-permute-done((bf16[96,1024]{1,0:T(8,128)(2,1)}, bf16[96,1024]{1,0:T(8,128)(2,1)S(1)}, u32[]{:S(2)}, u32[]{:S(2)}) %collective-permute-start.1) | collective-permute-done | bytes 196640 | tf_op jit(solution)/shard_map/ppermute | solution.py:22
  39.3 1.9 %collective-permute-start.3 = (bf16[96,1024]{1,0:T(8,128)(2,1)S(1)}, bf16[96,1024]{1,0:T(8,128)(2,1)S(1)}, u32[]{:S(2)}, u32[]{:S(2)}) collective-permute-start(bf16[96,1024]{1,0:T(8,128)(2,1)S(1)} %collective-permute-done.1.refs_2_), channel_id=1, source_target_pairs={{0,16},{16,32},{32,48},{48,0},{1,17},{17,33},{33,49},{49,1},{2,18}... | collective-permute-start | bytes 589832 | tf_op jit(solution)/shard_map/ppermute | solution.py:22
  41.2 0.0 collective-permute-done.refs_5_
  41.3 5.5 %collective-permute-start.4 = (bf16[160,1024]{1,0:T(8,128)(2,1)S(1)}, bf16[160,1024]{1,0:T(8,128)(2,1)S(1)}, u32[]{:S(2)}, u32[]{:S(2)}) collective-permute-start(bf16[160,1024]{1,0:T(8,128)(2,1)S(1)} %collective-permute-done.refs_5_), channel_id=1, source_target_pairs={{0,48},{16,0},{32,16},{48,32},{1,49},{17,1},{33,17},{49,33},{2,50}... | collective-permute-start | bytes 983048 | tf_op jit(solution)/shard_map/ppermute | solution.py:22
  46.7 0.0 all-to-all-done.refs_0_
  46.7 5.6 %collective-permute-start.2 = (bf16[8,64,1024]{2,1,0:T(8,128)(2,1)S(1)}, bf16[8,64,1024]{2,1,0:T(8,128)(2,1)S(1)}, u32[]{:S(2)}, u32[]{:S(2)}) collective-permute-start(bf16[8,64,1024]{2,1,0:T(8,128)(2,1)S(1)} %all-to-all-done.refs_0_), channel_id=1, source_target_pairs={{0,1},{1,0},{2,3},{3,2},{4,5},{5,4},{6,7},{7,6},{8,9},{9,8},{10,11... | collective-permute-start | bytes 3145736 | tf_op jit(solution)/shard_map/ppermute | solution.py:182
  52.4 0.0 collective-permute-done.6.refs_4_
  52.4 3.0 %shard_map.37.refs_6_ = bf16[8,8,2,64,128]{4,3,2,1,0:T(8,128)(2,1)S(1)} custom-call(bf16[8,64,1024]{2,1,0:T(8,128)(2,1)S(1)} %all-to-all-done.refs_0_, bf16[256,1024]{1,0:T(8,128)(2,1)S(1)} %bitcast.10, bf16[96,1024]{1,0:T(8,128)(2,1)S(1)} %collective-permute-done.1.refs_2_, bf16[160,1024]{1,0:T(8,128)(2,1)S(1)} %collective-permute-done.5.refs_3_, ...), custom_call_target="tpu_custom_call" | custom-call | flops 99999997952 | bytes 5242880 | tf_op jit(solution)/shard_map/pallas_call | solution.py:94
  55.4 0.0 collective-permute-done.2.refs_0_.refs_1_
  55.4 3.0 %shard_map.38.refs_4_ = bf16[8,8,2,64,128]{4,3,2,1,0:T(8,128)(2,1)S(1)} custom-call(bf16[8,64,1024]{2,1,0:T(8,128)(2,1)S(1)} %collective-permute-done.2.refs_0_.refs_1_, bf16[256,1024]{1,0:T(8,128)(2,1)S(1)} %bitcast.11, bf16[96,1024]{1,0:T(8,128)(2,1)S(1)} %collective-permute-done.1.refs_2_, ...), custom_call_target="tpu_custom_call", output_to_operand_aliasing={{}: (6, {})} | custom-call | flops 805306368 | bytes 5242880 | tf_op jit(solution)/shard_map/pallas_call | solution.py:94
  58.5 0.0 collective-permute-done.4.refs_3_
  58.5 1.5 %shard_map.39 = bf16[8,8,2,64,128]{4,3,2,1,0:T(8,128)(2,1)S(1)} custom-call(bf16[8,64,1024]{2,1,0:T(8,128)(2,1)S(1)} %all-to-all-done.refs_0_, bf16[8,64,1024]{2,1,0:T(8,128)(2,1)S(1)} %collective-permute-done.2.refs_0_.refs_1_, bf16[96,1024]{1,0:T(8,128)(2,1)S(1)} %collective-permute-done.3.refs_2_, ...), custom_call_target="tpu_custom_call", output_to_operand_aliasing={{}: (4, {})} | custom-call | flops 536870912 | bytes 5242880 | tf_op jit(solution)/shard_map/pallas_call | solution.py:94
  60.0 36.3 %all_to_all.15.refs_0_ = bf16[8,16,64,128]{3,2,1,0:T(8,128)(2,1)S(1)} all-to-all(bf16[8,16,64,128]{3,2,1,0:T(8,128)(2,1)S(1)} %bitcast.9), channel_id=1, replica_groups=mesh['x'=4,'yl'=2,'yh'=4,'z'=8,'core'=2] {'x','yl'}, dimensions={0} | all-to-all | bytes 4194304 | tf_op jit(solution)/shard_map/all_to_all | solution.py:193
  96.4 0.5 shard_map.40
  96.9 21.2 %all_to_all.16.terms_ref = bf16[16,64,128]{2,1,0:T(8,128)(2,1)S(1)} all-to-all(bf16[16,64,128]{2,1,0:T(8,128)(2,1)S(1)} %shard_map.40), channel_id=1, replica_groups=mesh['x'=4,'yl'=2,'yh'=4,'z'=8,'core'=2] {'z','core'}, dimensions={0} | all-to-all | bytes 524288 | tf_op jit(solution)/shard_map/all_to_all | solution.py:194
  118.1 0.8 shard_map.41
  (7 shorter events, 0.0 us)
Async XLA Ops:
  0.0 13.0 %copy-start = (bf16[1,256,1024]{2,1,0:T(8,128)(2,1)S(1)}, bf16[1,256,1024]{2,1,0:T(8,128)(2,1)}, u32[]{:S(2)}) copy-start(bf16[1,256,1024]{2,1,0:T(8,128)(2,1)} %param.4) | copy-start | bytes 1572868
  2.1 44.6 %all-to-all-start = ((bf16[8,64,1024]{2,1,0:T(8,128)(2,1)}), bf16[8,64,1024]{2,1,0:T(8,128)(2,1)S(1)}, u32[]{:S(2)}, u32[]{:S(2)}) async-start(bf16[8,64,1024]{2,1,0:T(8,128)(2,1)} %broadcast_in_dim.10), calls=%async_computation | async-start | bytes 2097152 | tf_op jit(solution)/shard_map/all_to_all | solution.py:180
  13.0 28.2 %collective-permute-start = (bf16[160,1024]{1,0:T(8,128)(2,1)S(1)}, bf16[160,1024]{1,0:T(8,128)(2,1)S(1)}, u32[]{:S(2)}, u32[]{:S(2)}) collective-permute-start(bf16[160,1024]{1,0:T(8,128)(2,1)S(1)} %slice_bitcast_fusion), channel_id=1, source_target_pairs={{0,48},{16,0},{32,16},{48,32},{1,49},{17,1},{33,17},{49,33},{2,50}... | collective-permute-start | bytes 983048 | tf_op jit(solution)/shard_map/ppermute | solution.py:22
  18.9 33.5 %collective-permute-start.5 = (bf16[160,1024]{1,0:T(8,128)(2,1)S(1)}, bf16[160,1024]{1,0:T(8,128)(2,1)S(1)}, u32[]{:S(2)}, u32[]{:S(2)}) collective-permute-start(bf16[160,1024]{1,0:T(8,128)(2,1)S(1)} %slice_bitcast_fusion), channel_id=1, source_target_pairs={{0,16},{16,32},{32,48},{48,0},{1,17},{17,33},{33,49},{49,1},{2,18}... | collective-permute-start | bytes 983048 | tf_op jit(solution)/shard_map/ppermute | solution.py:22
  21.5 17.8 %collective-permute-start.1 = (bf16[96,1024]{1,0:T(8,128)(2,1)}, bf16[96,1024]{1,0:T(8,128)(2,1)S(1)}, u32[]{:S(2)}, u32[]{:S(2)}) collective-permute-start(bf16[96,1024]{1,0:T(8,128)(2,1)} %slice_bitcast_fusion.1), channel_id=1, source_target_pairs={{0,16},{16,32},{32,48},{48,0},{1,17},{17,33},{33,49},{49,1},{2,18}... | collective-permute-start | bytes 589832 | tf_op jit(solution)/shard_map/ppermute | solution.py:22
  25.3 27.1 %collective-permute-start.6 = (bf16[96,1024]{1,0:T(8,128)(2,1)}, bf16[96,1024]{1,0:T(8,128)(2,1)S(1)}, u32[]{:S(2)}, u32[]{:S(2)}) collective-permute-start(bf16[96,1024]{1,0:T(8,128)(2,1)} %slice_bitcast_fusion.1), channel_id=1, source_target_pairs={{0,48},{16,0},{32,16},{48,32},{1,49},{17,1},{33,17},{49,33},{2,50}... | collective-permute-start | bytes 589832 | tf_op jit(solution)/shard_map/ppermute | solution.py:22
  39.3 19.2 %collective-permute-start.3 = (bf16[96,1024]{1,0:T(8,128)(2,1)S(1)}, bf16[96,1024]{1,0:T(8,128)(2,1)S(1)}, u32[]{:S(2)}, u32[]{:S(2)}) collective-permute-start(bf16[96,1024]{1,0:T(8,128)(2,1)S(1)} %collective-permute-done.1.refs_2_), channel_id=1, source_target_pairs={{0,16},{16,32},{32,48},{48,0},{1,17},{17,33},{33,49},{49,1},{2,18}... | collective-permute-start | bytes 589832 | tf_op jit(solution)/shard_map/ppermute | solution.py:22
  41.3 17.2 %collective-permute-start.4 = (bf16[160,1024]{1,0:T(8,128)(2,1)S(1)}, bf16[160,1024]{1,0:T(8,128)(2,1)S(1)}, u32[]{:S(2)}, u32[]{:S(2)}) collective-permute-start(bf16[160,1024]{1,0:T(8,128)(2,1)S(1)} %collective-permute-done.refs_5_), channel_id=1, source_target_pairs={{0,48},{16,0},{32,16},{48,32},{1,49},{17,1},{33,17},{49,33},{2,50}... | collective-permute-start | bytes 983048 | tf_op jit(solution)/shard_map/ppermute | solution.py:22
  46.7 8.7 %collective-permute-start.2 = (bf16[8,64,1024]{2,1,0:T(8,128)(2,1)S(1)}, bf16[8,64,1024]{2,1,0:T(8,128)(2,1)S(1)}, u32[]{:S(2)}, u32[]{:S(2)}) collective-permute-start(bf16[8,64,1024]{2,1,0:T(8,128)(2,1)S(1)} %all-to-all-done.refs_0_), channel_id=1, source_target_pairs={{0,1},{1,0},{2,3},{3,2},{4,5},{5,4},{6,7},{7,6},{8,9},{9,8},{10,11... | collective-permute-start | bytes 3145736 | tf_op jit(solution)/shard_map/ppermute | solution.py:182

commit v13 on v9

--- a/solution.py
+++ b/solution.py
@@ -182,7 +182,7 @@
     _, second, plane_dev = valence_pairs.shape
     own = conduction_pairs[0]
     columns = own.shape[0]
-    cut = columns * 3 // 8
+    cut = columns // 4
 
     ahead, back = along(own, 1), along(own, NH - 1)
 

time: 107 us -> 108 us (level)
  no operation moved by 1% of the time
where the time goes in v13:
time: 108 us; the launch traced here: 107 us
  blocking collectives  47.3 us (44%)
  starting transfers between devices  29.2 us (27%)
  waiting for transfers between devices  20.3 us (19%)
  Pallas kernels  7.58 us (7%)
  local copies, waits for them, and re-layouts  1.9 us (2%)
    all_to_all x1, blocking collectives, body(): terms = lax.all_to_all(terms, ('x', 'yl'), 0, 0, tiled=True)  30.2 us
    all_to_all x1, blocking collectives, body(): terms = lax.all_to_all(add(terms), ('z', 'core'), 0, 0, tiled=True)  17.1 us
    ppermute x4, starting transfers between devices, along(): return lax.ppermute(block, 'yh', [(i, (i + step) % NH) for i in range(NH)])  16.8 us
    all_to_all x1, waiting for transfers between devices, body(): mine = lax.all_to_all(sent, 'z', 0, 0, tiled=True)  12.8 us
    all_to_all x1, starting transfers between devices, body(): mine = lax.all_to_all(sent, 'z', 0, 0, tiled=True)  10 us
    ppermute x4, waiting for transfers between devices, along(): return lax.ppermute(block, 'yh', [(i, (i + step) % NH) for i in range(NH)])  7.53 us
    pallas_call x3, Pallas kernels, product(): pl.pallas_call(functools.partial(product_kernel, sides, cuts, ignored, at...  6.28 us
    ppermute x1, starting transfers between devices, body(): other = lax.ppermute(mine, 'core', [(0, 1), (1, 0)])  2.39 us
  transfers between devices with their start and end apart: 6, of which 2 were waited for; matrix products, arithmetic and copies ran while one was open for 3% of the time, Pallas kernels for 4%

profile of v13, /device:TPU:1, one launch (start us, length us, event | category | flops | bytes accessed | tf_op | source)
XLA Modules:
  0.0 107.4 jit_solution(11757038376230450481)
XLA Ops:
  0.0 6.8 %collective-permute-start = (bf16[256,1024]{1,0:T(8,128)(2,1)}, bf16[256,1024]{1,0:T(8,128)(2,1)S(1)}, u32[]{:S(2)}, u32[]{:S(2)}) collective-permute-start(bf16[256,1024]{1,0:T(8,128)(2,1)} %bitcast.7), channel_id=1, source_target_pairs={{0,48},{16,0},{32,16},{48,32},{1,49},{17,1},{33,17},{49,33},{2,50}... | collective-permute-start | bytes 1572872 | tf_op jit(solution)/shard_map/ppermute | solution.py:22
  6.8 1.9 %collective-permute-start.1 = (bf16[256,1024]{1,0:T(8,128)(2,1)}, bf16[256,1024]{1,0:T(8,128)(2,1)S(1)}, u32[]{:S(2)}, u32[]{:S(2)}) collective-permute-start(bf16[256,1024]{1,0:T(8,128)(2,1)} %bitcast.8), channel_id=1, source_target_pairs={{0,16},{16,32},{32,48},{48,0},{1,17},{17,33},{33,49},{49,1},{2,18}... | collective-permute-start | bytes 1572872 | tf_op jit(solution)/shard_map/ppermute | solution.py:22
  8.8 0.9 fusion
  9.7 1.1 %broadcast_in_dim.13 = bf16[8,64,1024]{2,1,0:T(8,128)(2,1)} broadcast(bf16[64,1024]{1,0:T(8,128)(2,1)S(1)} %fusion), dimensions={1,2} | broadcast | bytes 1179648 | tf_op jit(solution)/shard_map/broadcast_in_dim | solution.py:190
  10.8 10.0 %all-to-all-start = ((bf16[8,64,1024]{2,1,0:T(8,128)(2,1)}), bf16[8,64,1024]{2,1,0:T(8,128)(2,1)S(1)}, u32[]{:S(2)}, u32[]{:S(2)}) async-start(bf16[8,64,1024]{2,1,0:T(8,128)(2,1)} %broadcast_in_dim.13), calls=%async_computation | async-start | bytes 2097152 | tf_op jit(solution)/shard_map/all_to_all | solution.py:191
  20.8 0.0 copy-done.1
  20.8 0.0 copy-start
  20.9 7.5 %collective-permute-done.refs_3_ = bf16[256,1024]{1,0:T(8,128)(2,1)S(1)} collective-permute-done((bf16[256,1024]{1,0:T(8,128)(2,1)}, bf16[256,1024]{1,0:T(8,128)(2,1)S(1)}, u32[]{:S(2)}, u32[]{:S(2)}) %collective-permute-start) | collective-permute-done | bytes 524320 | tf_op jit(solution)/shard_map/ppermute | solution.py:22
  28.4 0.8 slice.19
  29.2 6.1 %collective-permute-start.4 = (bf16[192,1024]{1,0:T(8,128)(2,1)}, bf16[192,1024]{1,0:T(8,128)(2,1)S(1)}, u32[]{:S(2)}, u32[]{:S(2)}) collective-permute-start(bf16[192,1024]{1,0:T(8,128)(2,1)} %slice.19), channel_id=1, source_target_pairs={{0,48},{16,0},{32,16},{48,32},{1,49},{17,1},{33,17},{49,33},{2,50}... | collective-permute-start | bytes 1179656 | tf_op jit(solution)/shard_map/ppermute | solution.py:22
  35.3 0.0 collective-permute-done.1.refs_2_
  35.3 1.9 %collective-permute-start.3 = (bf16[64,1024]{1,0:T(8,128)(2,1)S(1)}, bf16[64,1024]{1,0:T(8,128)(2,1)S(1)}, u32[]{:S(2)}, u32[]{:S(2)}) collective-permute-start(bf16[64,1024]{1,0:T(8,128)(2,1)S(1)} %slice.18), channel_id=1, source_target_pairs={{0,16},{16,32},{32,48},{48,0},{1,17},{17,33},{33,49},{49,1},{2,18}... | collective-permute-start | bytes 393224 | tf_op jit(solution)/shard_map/ppermute | solution.py:22
  37.3 12.8 %all-to-all-done.refs_0_ = bf16[8,64,1024]{2,1,0:T(8,128)(2,1)S(1)} async-done(((bf16[8,64,1024]{2,1,0:T(8,128)(2,1)}), bf16[8,64,1024]{2,1,0:T(8,128)(2,1)S(1)}, u32[]{:S(2)}, u32[]{:S(2)}) %all-to-all-start) | async-done | bytes 1048608 | tf_op jit(solution)/shard_map/all_to_all | solution.py:191
  50.0 2.4 %collective-permute-start.2 = (bf16[8,64,1024]{2,1,0:T(8,128)(2,1)S(1)}, bf16[8,64,1024]{2,1,0:T(8,128)(2,1)S(1)}, u32[]{:S(2)}, u32[]{:S(2)}) collective-permute-start(bf16[8,64,1024]{2,1,0:T(8,128)(2,1)S(1)} %all-to-all-done.refs_0_), channel_id=1, source_target_pairs={{0,1},{1,0},{2,3},{3,2},{4,5},{5,4},{6,7},{7,6},{8,9},{9,8},{10,11... | collective-permute-start | bytes 3145736 | tf_op jit(solution)/shard_map/ppermute | solution.py:193
  52.4 2.4 %shard_map.38.refs_4_ = bf16[8,8,2,64,128]{4,3,2,1,0:T(8,128)(2,1)S(1)} custom-call(bf16[8,64,1024]{2,1,0:T(8,128)(2,1)S(1)} %all-to-all-done.refs_0_, bf16[256,1024]{1,0:T(8,128)(2,1)S(1)} %bitcast.9, bf16[256,1024]{1,0:T(8,128)(2,1)S(1)} %collective-permute-done.1.refs_2_, bf16[256,1024]{1,0:T(8,128)(2,1)S(1)} %collective-permute-done.refs_3_, ...), custom_call_target="tpu_custom_call" | custom-call | flops 99999997952 | bytes 5242880 | tf_op jit(solution)/shard_map/pallas_call | solution.py:107
  54.8 0.0 collective-permute-done.2.refs_0_.refs_1_
  54.8 2.4 %shard_map.39.refs_4_ = bf16[8,8,2,64,128]{4,3,2,1,0:T(8,128)(2,1)S(1)} custom-call(bf16[8,64,1024]{2,1,0:T(8,128)(2,1)S(1)} %collective-permute-done.2.refs_0_.refs_1_, bf16[256,1024]{1,0:T(8,128)(2,1)S(1)} %bitcast.10, bf16[256,1024]{1,0:T(8,128)(2,1)S(1)} %collective-permute-done.1.refs_2_, ...), custom_call_target="tpu_custom_call", output_to_operand_aliasing={{}: (4, {})} | custom-call | flops 805306368 | bytes 5242880 | tf_op jit(solution)/shard_map/pallas_call | solution.py:107
  57.2 0.0 collective-permute-done.3.refs_2_
  57.2 0.0 collective-permute-done.4.refs_3_
  57.2 1.5 %shard_map.40 = bf16[8,8,2,64,128]{4,3,2,1,0:T(8,128)(2,1)S(1)} custom-call(bf16[8,64,1024]{2,1,0:T(8,128)(2,1)S(1)} %all-to-all-done.refs_0_, bf16[8,64,1024]{2,1,0:T(8,128)(2,1)S(1)} %collective-permute-done.2.refs_0_.refs_1_, bf16[64,1024]{1,0:T(8,128)(2,1)S(1)} %collective-permute-done.3.refs_2_, ...), custom_call_target="tpu_custom_call", output_to_operand_aliasing={{}: (4, {})} | custom-call | flops 536870912 | bytes 5242880 | tf_op jit(solution)/shard_map/pallas_call | solution.py:107
  58.8 30.2 %all_to_all.15.refs_0_ = bf16[8,16,64,128]{3,2,1,0:T(8,128)(2,1)S(1)} all-to-all(bf16[8,16,64,128]{3,2,1,0:T(8,128)(2,1)S(1)} %bitcast.6), channel_id=1, replica_groups=mesh['x'=4,'yl'=2,'yh'=4,'z'=8,'core'=2] {'x','yl'}, dimensions={0} | all-to-all | bytes 4194304 | tf_op jit(solution)/shard_map/all_to_all | solution.py:204
  88.9 0.5 shard_map.41
  89.4 17.1 %all_to_all.16.terms_ref = bf16[16,64,128]{2,1,0:T(8,128)(2,1)S(1)} all-to-all(bf16[16,64,128]{2,1,0:T(8,128)(2,1)S(1)} %shard_map.41), channel_id=1, replica_groups=mesh['x'=4,'yl'=2,'yh'=4,'z'=8,'core'=2] {'z','core'}, dimensions={0} | all-to-all | bytes 524288 | tf_op jit(solution)/shard_map/all_to_all | solution.py:205
  106.5 0.8 shard_map.42
  (6 shorter events, 0.0 us)
Async XLA Ops:
  0.0 20.8 %copy-start.1 = (f32[1024]{0:T(1024)S(1)}, f32[1024]{0:T(1024)}, u32[]{:S(2)}) copy-start(f32[1024]{0:T(1024)} %param.5) | copy-start | bytes 12292
  0.0 28.4 %collective-permute-start = (bf16[256,1024]{1,0:T(8,128)(2,1)}, bf16[256,1024]{1,0:T(8,128)(2,1)S(1)}, u32[]{:S(2)}, u32[]{:S(2)}) collective-permute-start(bf16[256,1024]{1,0:T(8,128)(2,1)} %bitcast.7), channel_id=1, source_target_pairs={{0,48},{16,0},{32,16},{48,32},{1,49},{17,1},{33,17},{49,33},{2,50}... | collective-permute-start | bytes 1572872 | tf_op jit(solution)/shard_map/ppermute | solution.py:22
  6.8 28.4 %collective-permute-start.1 = (bf16[256,1024]{1,0:T(8,128)(2,1)}, bf16[256,1024]{1,0:T(8,128)(2,1)S(1)}, u32[]{:S(2)}, u32[]{:S(2)}) collective-permute-start(bf16[256,1024]{1,0:T(8,128)(2,1)} %bitcast.8), channel_id=1, source_target_pairs={{0,16},{16,32},{32,48},{48,0},{1,17},{17,33},{33,49},{49,1},{2,18}... | collective-permute-start | bytes 1572872 | tf_op jit(solution)/shard_map/ppermute | solution.py:22
  10.8 39.2 %all-to-all-start = ((bf16[8,64,1024]{2,1,0:T(8,128)(2,1)}), bf16[8,64,1024]{2,1,0:T(8,128)(2,1)S(1)}, u32[]{:S(2)}, u32[]{:S(2)}) async-start(bf16[8,64,1024]{2,1,0:T(8,128)(2,1)} %broadcast_in_dim.13), calls=%async_computation | async-start | bytes 2097152 | tf_op jit(solution)/shard_map/all_to_all | solution.py:191
  20.8 31.6 %copy-start = (bf16[1,256,1024]{2,1,0:T(8,128)(2,1)S(1)}, bf16[1,256,1024]{2,1,0:T(8,128)(2,1)}, u32[]{:S(2)}) copy-start(bf16[1,256,1024]{2,1,0:T(8,128)(2,1)} %param.4) | copy-start | bytes 1572868
  29.2 28.1 %collective-permute-start.4 = (bf16[192,1024]{1,0:T(8,128)(2,1)}, bf16[192,1024]{1,0:T(8,128)(2,1)S(1)}, u32[]{:S(2)}, u32[]{:S(2)}) collective-permute-start(bf16[192,1024]{1,0:T(8,128)(2,1)} %slice.19), channel_id=1, source_target_pairs={{0,48},{16,0},{32,16},{48,32},{1,49},{17,1},{33,17},{49,33},{2,50}... | collective-permute-start | bytes 1179656 | tf_op jit(solution)/shard_map/ppermute | solution.py:22
  35.3 21.9 %collective-permute-start.3 = (bf16[64,1024]{1,0:T(8,128)(2,1)S(1)}, bf16[64,1024]{1,0:T(8,128)(2,1)S(1)}, u32[]{:S(2)}, u32[]{:S(2)}) collective-permute-start(bf16[64,1024]{1,0:T(8,128)(2,1)S(1)} %slice.18), channel_id=1, source_target_pairs={{0,16},{16,32},{32,48},{48,0},{1,17},{17,33},{33,49},{49,1},{2,18}... | collective-permute-start | bytes 393224 | tf_op jit(solution)/shard_map/ppermute | solution.py:22
  50.0 4.8 %collective-permute-start.2 = (bf16[8,64,1024]{2,1,0:T(8,128)(2,1)S(1)}, bf16[8,64,1024]{2,1,0:T(8,128)(2,1)S(1)}, u32[]{:S(2)}, u32[]{:S(2)}) collective-permute-start(bf16[8,64,1024]{2,1,0:T(8,128)(2,1)S(1)} %all-to-all-done.refs_0_), channel_id=1, source_target_pairs={{0,1},{1,0},{2,3},{3,2},{4,5},{5,4},{6,7},{7,6},{8,9},{9,8},{10,11... | collective-permute-start | bytes 3145736 | tf_op jit(solution)/shard_map/ppermute | solution.py:193

commit v14 on v9

--- a/solution.py
+++ b/solution.py
@@ -40,37 +40,19 @@
 
 
 def product_kernel(sides, cuts, ignored, at_row, *refs):
-    count, pieces, width = len(cuts), sum(cuts), len(sides)
-    rows_refs, piece_refs = refs[:width], refs[width : width + pieces]
-    out_ref, left, right, held, left_sem, right_sem, out_sem = refs[width + pieces + ignored :]
+    pieces, width = sum(cuts), len(sides)
+    rows_refs, piece_refs = refs[:width], list(refs[width : width + pieces])
+    out_ref, held, out_sem = refs[width + pieces + ignored :]
     core = lax.axis_index("core")
     nz, rows, planes = rows_refs[0].shape
     wide = rows // NQ
-    lefts = [
-        pltpu.make_async_copy(rows_refs[i], left.at[i], left_sem.at[i]) for i in range(width)
-    ]
-    rights, at = [], 0
-    for i, cut in enumerate(cuts):
-        group, top = [], 0
-        for _ in range(cut):
-            part = piece_refs[at].shape[0]
-            group.append(
-                pltpu.make_async_copy(
-                    piece_refs[at], right.at[i, pl.ds(top, part)], right_sem.at[at]
-                )
-            )
-            at, top = at + 1, top + part
-        rights.append(group)
-    for copy in [*lefts, *[copy for group in rights for copy in group]]:
-        copy.start()
-    for copy in lefts:
-        copy.wait()
-    whole = left[...].reshape(width * nz * rows, planes)
+    parts = [ref[...].reshape(nz * rows, planes) for ref in rows_refs]
+    whole = parts[0] if width == 1 else jnp.concatenate(parts, axis=0)
     done = []
-    for i in range(count):
-        for copy in rights[i]:
-            copy.wait()
-        term = dot(whole, right[i])
+    for cut in cuts:
+        group = [piece_refs.pop(0)[...] for _ in range(cut)]
+        block = group[0] if cut == 1 else jnp.concatenate(group, axis=0)
+        term = dot(whole, block)
         done += [term[:, c : c + LANES] for c in range(0, term.shape[1], LANES)]
     tall = held.shape[3]
     copies = []
@@ -97,7 +79,8 @@
     tall = count * columns // LANES * wide
     if flops is None:
         flops = 2 * len(lefts) * nz * rows * width * columns * count
-    anywhere = pl.BlockSpec(memory_space=pltpu.HBM)
+    near = pl.BlockSpec(memory_space=pltpu.VMEM)
+    anywhere = pl.BlockSpec(memory_space=pl.ANY)
     operands = [*lefts, *[piece for block in blocks for piece in block], *unread]
     ignored, aliases = len(unread), {}
     if begun is not None:
@@ -107,14 +90,10 @@
     return pl.pallas_call(
         functools.partial(product_kernel, sides, cuts, ignored, at_row),
         out_shape=jax.ShapeDtypeStruct((NQ, nz, NC, height, LANES), BF16),
-        in_specs=[anywhere] * len(operands),
+        in_specs=[near] * (len(lefts) + sum(cuts)) + [anywhere] * ignored,
         out_specs=pl.BlockSpec(memory_space=pl.ANY),
         scratch_shapes=[
-            pltpu.VMEM((len(lefts), nz, rows, width), BF16),
-            pltpu.VMEM((count, columns, width), BF16),
             pltpu.VMEM((len(lefts), NQ, nz, tall, LANES), BF16),
-            pltpu.SemaphoreType.DMA((len(lefts),)),
-            pltpu.SemaphoreType.DMA((sum(cuts),)),
             pltpu.SemaphoreType.DMA((len(lefts),)),
         ],
         input_output_aliases=aliases,

time: 107 us -> 106 us (level)
  Pallas kernels: 7.58 us -> 4.44 us
  blocking collectives: 46.5 us -> 47.9 us
  waiting for transfers between devices: 20.2 us -> 21.3 us
    pallas_call x3, Pallas kernels: 6.28 us -> 3.14 us  [product(): pl.pallas_call(functools.partial(product_kernel, sides, cuts, ignored, at...]
    all_to_all x1, blocking collectives: 16.4 us -> 17.9 us  [body(): terms = lax.all_to_all(add(terms), ('z', 'core'), 0, 0, tiled=True)]
    ppermute x1, waiting for transfers between devices: 0.01 us -> 1.11 us  [body(): other = lax.ppermute(mine, 'core', [(0, 1), (1, 0)])]
  transfers between devices with their start and end apart: 6 -> 6, of which waited for: 2 -> 3; matrix products, arithmetic and copies ran while one was open for 3% -> 3% of each run, Pallas kernels for 4% -> 2%
where the time goes in v14:
time: 106 us
  blocking collectives  47.9 us (45%)
  starting transfers between devices  29.4 us (28%)
  waiting for transfers between devices  21.3 us (20%)
  Pallas kernels  4.44 us (4%)
  local copies, waits for them, and re-layouts  1.83 us (2%)
    all_to_all x1, blocking collectives, body(): terms = lax.all_to_all(terms, ('x', 'yl'), 0, 0, tiled=True)  30 us
    all_to_all x1, blocking collectives, body(): terms = lax.all_to_all(add(terms), ('z', 'core'), 0, 0, tiled=True)  17.9 us
    ppermute x4, starting transfers between devices, along(): return lax.ppermute(block, 'yh', [(i, (i + step) % NH) for i in range(NH)])  16.9 us
    all_to_all x1, waiting for transfers between devices, body(): mine = lax.all_to_all(sent, 'z', 0, 0, tiled=True)  12.8 us
    all_to_all x1, starting transfers between devices, body(): mine = lax.all_to_all(sent, 'z', 0, 0, tiled=True)  10 us
    ppermute x4, waiting for transfers between devices, along(): return lax.ppermute(block, 'yh', [(i, (i + step) % NH) for i in range(NH)])  7.43 us
    pallas_call x3, Pallas kernels, product(): pl.pallas_call(functools.partial(product_kernel, sides, cuts, ignored, at...  3.14 us
    ppermute x1, starting transfers between devices, body(): other = lax.ppermute(mine, 'core', [(0, 1), (1, 0)])  2.39 us
  transfers between devices with their start and end apart: 6, of which 3 were waited for; matrix products, arithmetic and copies ran while one was open for 3% of the time, Pallas kernels for 2%

profile of v14, /device:TPU:1, one launch (start us, length us, event | category | flops | bytes accessed | tf_op | source)
XLA Modules:
  0.0 106.0 jit_solution(15881196435788318350)
XLA Ops:
  0.0 6.8 %collective-permute-start = (bf16[256,1024]{1,0:T(8,128)(2,1)}, bf16[256,1024]{1,0:T(8,128)(2,1)S(1)}, u32[]{:S(2)}, u32[]{:S(2)}) collective-permute-start(bf16[256,1024]{1,0:T(8,128)(2,1)} %bitcast.7), channel_id=1, source_target_pairs={{0,48},{16,0},{32,16},{48,32},{1,49},{17,1},{33,17},{49,33},{2,50}... | collective-permute-start | bytes 1572872 | tf_op jit(solution)/shard_map/ppermute | solution.py:22
  6.8 1.9 %collective-permute-start.1 = (bf16[256,1024]{1,0:T(8,128)(2,1)}, bf16[256,1024]{1,0:T(8,128)(2,1)S(1)}, u32[]{:S(2)}, u32[]{:S(2)}) collective-permute-start(bf16[256,1024]{1,0:T(8,128)(2,1)} %bitcast.8), channel_id=1, source_target_pairs={{0,16},{16,32},{32,48},{48,0},{1,17},{17,33},{33,49},{49,1},{2,18}... | collective-permute-start | bytes 1572872 | tf_op jit(solution)/shard_map/ppermute | solution.py:22
  8.8 0.9 fusion
  9.7 1.1 %broadcast_in_dim.13 = bf16[8,64,1024]{2,1,0:T(8,128)(2,1)} broadcast(bf16[64,1024]{1,0:T(8,128)(2,1)S(1)} %fusion), dimensions={1,2} | broadcast | bytes 1179648 | tf_op jit(solution)/shard_map/broadcast_in_dim | solution.py:169
  10.8 10.0 %all-to-all-start = ((bf16[8,64,1024]{2,1,0:T(8,128)(2,1)}), bf16[8,64,1024]{2,1,0:T(8,128)(2,1)S(1)}, u32[]{:S(2)}, u32[]{:S(2)}) async-start(bf16[8,64,1024]{2,1,0:T(8,128)(2,1)} %broadcast_in_dim.13), calls=%async_computation | async-start | bytes 2097152 | tf_op jit(solution)/shard_map/all_to_all | solution.py:170
  20.8 0.0 copy-done.1
  20.8 0.0 copy-start
  20.9 7.4 %collective-permute-done.refs_3_ = bf16[256,1024]{1,0:T(8,128)(2,1)S(1)} collective-permute-done((bf16[256,1024]{1,0:T(8,128)(2,1)}, bf16[256,1024]{1,0:T(8,128)(2,1)S(1)}, u32[]{:S(2)}, u32[]{:S(2)}) %collective-permute-start) | collective-permute-done | bytes 524320 | tf_op jit(solution)/shard_map/ppermute | solution.py:22
  28.3 6.3 %collective-permute-start.4 = (bf16[160,1024]{1,0:T(8,128)(2,1)S(1)}, bf16[160,1024]{1,0:T(8,128)(2,1)S(1)}, u32[]{:S(2)}, u32[]{:S(2)}) collective-permute-start(bf16[160,1024]{1,0:T(8,128)(2,1)S(1)} %slice.19), channel_id=1, source_target_pairs={{0,48},{16,0},{32,16},{48,32},{1,49},{17,1},{33,17},{49,33},{2,50}... | collective-permute-start | bytes 983048 | tf_op jit(solution)/shard_map/ppermute | solution.py:22
  34.6 0.0 collective-permute-done.1.refs_2_
  34.6 0.7 slice.18
  35.3 1.9 %collective-permute-start.3 = (bf16[96,1024]{1,0:T(8,128)(2,1)}, bf16[96,1024]{1,0:T(8,128)(2,1)S(1)}, u32[]{:S(2)}, u32[]{:S(2)}) collective-permute-start(bf16[96,1024]{1,0:T(8,128)(2,1)} %slice.18), channel_id=1, source_target_pairs={{0,16},{16,32},{32,48},{48,0},{1,17},{17,33},{33,49},{49,1},{2,18}... | collective-permute-start | bytes 589832 | tf_op jit(solution)/shard_map/ppermute | solution.py:22
  37.2 12.8 %all-to-all-done.refs_0_ = bf16[8,64,1024]{2,1,0:T(8,128)(2,1)S(1)} async-done(((bf16[8,64,1024]{2,1,0:T(8,128)(2,1)}), bf16[8,64,1024]{2,1,0:T(8,128)(2,1)S(1)}, u32[]{:S(2)}, u32[]{:S(2)}) %all-to-all-start) | async-done | bytes 1048608 | tf_op jit(solution)/shard_map/all_to_all | solution.py:170
  50.0 2.4 %collective-permute-start.2 = (bf16[8,64,1024]{2,1,0:T(8,128)(2,1)S(1)}, bf16[8,64,1024]{2,1,0:T(8,128)(2,1)S(1)}, u32[]{:S(2)}, u32[]{:S(2)}) collective-permute-start(bf16[8,64,1024]{2,1,0:T(8,128)(2,1)S(1)} %all-to-all-done.refs_0_), channel_id=1, source_target_pairs={{0,1},{1,0},{2,3},{3,2},{4,5},{5,4},{6,7},{7,6},{8,9},{9,8},{10,11... | collective-permute-start | bytes 3145736 | tf_op jit(solution)/shard_map/ppermute | solution.py:172
  52.4 1.1 %shard_map.38.refs_4_ = bf16[8,8,2,64,128]{4,3,2,1,0:T(8,128)(2,1)S(1)} custom-call(bf16[8,64,1024]{2,1,0:T(8,128)(2,1)S(1)} %all-to-all-done.refs_0_, bf16[256,1024]{1,0:T(8,128)(2,1)S(1)} %bitcast.9, bf16[256,1024]{1,0:T(8,128)(2,1)S(1)} %collective-permute-done.1.refs_2_, bf16[256,1024]{1,0:T(8,128)(2,1)S(1)} %collective-permute-done.refs_3_, ...), custom_call_target="tpu_custom_call" | custom-call | flops 99999997952 | bytes 5242880 | tf_op jit(solution)/shard_map/pallas_call | solution.py:90
  53.6 1.1 %collective-permute-done.2.refs_0_.refs_1_ = bf16[8,64,1024]{2,1,0:T(8,128)(2,1)S(1)} collective-permute-done((bf16[8,64,1024]{2,1,0:T(8,128)(2,1)S(1)}, bf16[8,64,1024]{2,1,0:T(8,128)(2,1)S(1)}, u32[]{:S(2)}, u32[]{:S(2)}) %collective-permute-start.2) | collective-permute-done | bytes 1048608 | tf_op jit(solution)/shard_map/ppermute | solution.py:172
  54.7 1.1 %shard_map.39.refs_4_ = bf16[8,8,2,64,128]{4,3,2,1,0:T(8,128)(2,1)S(1)} custom-call(bf16[8,64,1024]{2,1,0:T(8,128)(2,1)S(1)} %collective-permute-done.2.refs_0_.refs_1_, bf16[256,1024]{1,0:T(8,128)(2,1)S(1)} %bitcast.10, bf16[256,1024]{1,0:T(8,128)(2,1)S(1)} %collective-permute-done.1.refs_2_, ...), custom_call_target="tpu_custom_call", output_to_operand_aliasing={{}: (4, {})} | custom-call | flops 805306368 | bytes 5242880 | tf_op jit(solution)/shard_map/pallas_call | solution.py:90
  55.8 0.0 collective-permute-done.3.refs_2_
  55.9 0.0 collective-permute-done.4.refs_3_
  55.9 0.9 shard_map.40
  56.7 30.0 %all_to_all.15.refs_0_ = bf16[8,16,64,128]{3,2,1,0:T(8,128)(2,1)S(1)} all-to-all(bf16[8,16,64,128]{3,2,1,0:T(8,128)(2,1)S(1)} %bitcast.6), channel_id=1, replica_groups=mesh['x'=4,'yl'=2,'yh'=4,'z'=8,'core'=2] {'x','yl'}, dimensions={0} | all-to-all | bytes 4194304 | tf_op jit(solution)/shard_map/all_to_all | solution.py:183
  86.7 0.5 shard_map.41
  87.2 17.9 %all_to_all.16.terms_ref = bf16[16,64,128]{2,1,0:T(8,128)(2,1)S(1)} all-to-all(bf16[16,64,128]{2,1,0:T(8,128)(2,1)S(1)} %shard_map.41), channel_id=1, replica_groups=mesh['x'=4,'yl'=2,'yh'=4,'z'=8,'core'=2] {'z','core'}, dimensions={0} | all-to-all | bytes 524288 | tf_op jit(solution)/shard_map/all_to_all | solution.py:184
  105.2 0.8 shard_map.42
  (6 shorter events, 0.0 us)
Async XLA Ops:
  0.0 20.8 %copy-start.1 = (f32[1024]{0:T(1024)S(1)}, f32[1024]{0:T(1024)}, u32[]{:S(2)}) copy-start(f32[1024]{0:T(1024)} %param.5) | copy-start | bytes 12292
  0.0 28.3 %collective-permute-start = (bf16[256,1024]{1,0:T(8,128)(2,1)}, bf16[256,1024]{1,0:T(8,128)(2,1)S(1)}, u32[]{:S(2)}, u32[]{:S(2)}) collective-permute-start(bf16[256,1024]{1,0:T(8,128)(2,1)} %bitcast.7), channel_id=1, source_target_pairs={{0,48},{16,0},{32,16},{48,32},{1,49},{17,1},{33,17},{49,33},{2,50}... | collective-permute-start | bytes 1572872 | tf_op jit(solution)/shard_map/ppermute | solution.py:22
  6.8 27.7 %collective-permute-start.1 = (bf16[256,1024]{1,0:T(8,128)(2,1)}, bf16[256,1024]{1,0:T(8,128)(2,1)S(1)}, u32[]{:S(2)}, u32[]{:S(2)}) collective-permute-start(bf16[256,1024]{1,0:T(8,128)(2,1)} %bitcast.8), channel_id=1, source_target_pairs={{0,16},{16,32},{32,48},{48,0},{1,17},{17,33},{33,49},{49,1},{2,18}... | collective-permute-start | bytes 1572872 | tf_op jit(solution)/shard_map/ppermute | solution.py:22
  10.8 39.2 %all-to-all-start = ((bf16[8,64,1024]{2,1,0:T(8,128)(2,1)}), bf16[8,64,1024]{2,1,0:T(8,128)(2,1)S(1)}, u32[]{:S(2)}, u32[]{:S(2)}) async-start(bf16[8,64,1024]{2,1,0:T(8,128)(2,1)} %broadcast_in_dim.13), calls=%async_computation | async-start | bytes 2097152 | tf_op jit(solution)/shard_map/all_to_all | solution.py:170
  20.8 31.6 %copy-start = (bf16[1,256,1024]{2,1,0:T(8,128)(2,1)S(1)}, bf16[1,256,1024]{2,1,0:T(8,128)(2,1)}, u32[]{:S(2)}) copy-start(bf16[1,256,1024]{2,1,0:T(8,128)(2,1)} %param.4) | copy-start | bytes 1572868
  28.3 27.5 %collective-permute-start.4 = (bf16[160,1024]{1,0:T(8,128)(2,1)S(1)}, bf16[160,1024]{1,0:T(8,128)(2,1)S(1)}, u32[]{:S(2)}, u32[]{:S(2)}) collective-permute-start(bf16[160,1024]{1,0:T(8,128)(2,1)S(1)} %slice.19), channel_id=1, source_target_pairs={{0,48},{16,0},{32,16},{48,32},{1,49},{17,1},{33,17},{49,33},{2,50}... | collective-permute-start | bytes 983048 | tf_op jit(solution)/shard_map/ppermute | solution.py:22
  35.3 20.6 %collective-permute-start.3 = (bf16[96,1024]{1,0:T(8,128)(2,1)}, bf16[96,1024]{1,0:T(8,128)(2,1)S(1)}, u32[]{:S(2)}, u32[]{:S(2)}) collective-permute-start(bf16[96,1024]{1,0:T(8,128)(2,1)} %slice.18), channel_id=1, source_target_pairs={{0,16},{16,32},{32,48},{48,0},{1,17},{17,33},{33,49},{49,1},{2,18}... | collective-permute-start | bytes 589832 | tf_op jit(solution)/shard_map/ppermute | solution.py:22
  50.0 4.7 %collective-permute-start.2 = (bf16[8,64,1024]{2,1,0:T(8,128)(2,1)S(1)}, bf16[8,64,1024]{2,1,0:T(8,128)(2,1)S(1)}, u32[]{:S(2)}, u32[]{:S(2)}) collective-permute-start(bf16[8,64,1024]{2,1,0:T(8,128)(2,1)S(1)} %all-to-all-done.refs_0_), channel_id=1, source_target_pairs={{0,1},{1,0},{2,3},{3,2},{4,5},{5,4},{6,7},{7,6},{8,9},{9,8},{10,11... | collective-permute-start | bytes 3145736 | tf_op jit(solution)/shard_map/ppermute | solution.py:172

commit v15 on v14

--- a/solution.py
+++ b/solution.py
@@ -161,7 +161,7 @@
     _, second, plane_dev = valence_pairs.shape
     own = conduction_pairs[0]
     columns = own.shape[0]
-    cut = columns * 3 // 8
+    cut = columns // 4
 
     ahead, back = along(own, 1), along(own, NH - 1)
 

time: 106 us -> 107 us (level)
  no operation moved by 1% of the time
where the time goes in v15:
time: 107 us
  blocking collectives  48.6 us (45%)
  starting transfers between devices  29.2 us (27%)
  waiting for transfers between devices  21.4 us (20%)
  Pallas kernels  4.44 us (4%)
  local copies, waits for them, and re-layouts  1.9 us (2%)
    all_to_all x1, blocking collectives, body(): terms = lax.all_to_all(terms, ('x', 'yl'), 0, 0, tiled=True)  30 us
    all_to_all x1, blocking collectives, body(): terms = lax.all_to_all(add(terms), ('z', 'core'), 0, 0, tiled=True)  18.6 us
    ppermute x4, starting transfers between devices, along(): return lax.ppermute(block, 'yh', [(i, (i + step) % NH) for i in range(NH)])  16.8 us
    all_to_all x1, waiting for transfers between devices, body(): mine = lax.all_to_all(sent, 'z', 0, 0, tiled=True)  12.8 us
    all_to_all x1, starting transfers between devices, body(): mine = lax.all_to_all(sent, 'z', 0, 0, tiled=True)  10 us
    ppermute x4, waiting for transfers between devices, along(): return lax.ppermute(block, 'yh', [(i, (i + step) % NH) for i in range(NH)])  7.53 us
    pallas_call x3, Pallas kernels, product(): pl.pallas_call(functools.partial(product_kernel, sides, cuts, ignored, at...  3.14 us
    ppermute x1, starting transfers between devices, body(): other = lax.ppermute(mine, 'core', [(0, 1), (1, 0)])  2.39 us
  transfers between devices with their start and end apart: 6, of which 3 were waited for; matrix products, arithmetic and copies ran while one was open for 3% of the time, Pallas kernels for 2%

profile of v15, /device:TPU:1, one launch (start us, length us, event | category | flops | bytes accessed | tf_op | source)
XLA Modules:
  0.0 106.7 jit_solution(14492088569661306868)
XLA Ops:
  0.0 6.8 %collective-permute-start = (bf16[256,1024]{1,0:T(8,128)(2,1)}, bf16[256,1024]{1,0:T(8,128)(2,1)S(1)}, u32[]{:S(2)}, u32[]{:S(2)}) collective-permute-start(bf16[256,1024]{1,0:T(8,128)(2,1)} %bitcast.7), channel_id=1, source_target_pairs={{0,48},{16,0},{32,16},{48,32},{1,49},{17,1},{33,17},{49,33},{2,50}... | collective-permute-start | bytes 1572872 | tf_op jit(solution)/shard_map/ppermute | solution.py:22
  6.8 1.9 %collective-permute-start.1 = (bf16[256,1024]{1,0:T(8,128)(2,1)}, bf16[256,1024]{1,0:T(8,128)(2,1)S(1)}, u32[]{:S(2)}, u32[]{:S(2)}) collective-permute-start(bf16[256,1024]{1,0:T(8,128)(2,1)} %bitcast.8), channel_id=1, source_target_pairs={{0,16},{16,32},{32,48},{48,0},{1,17},{17,33},{33,49},{49,1},{2,18}... | collective-permute-start | bytes 1572872 | tf_op jit(solution)/shard_map/ppermute | solution.py:22
  8.8 0.9 fusion
  9.7 1.1 %broadcast_in_dim.13 = bf16[8,64,1024]{2,1,0:T(8,128)(2,1)} broadcast(bf16[64,1024]{1,0:T(8,128)(2,1)S(1)} %fusion), dimensions={1,2} | broadcast | bytes 1179648 | tf_op jit(solution)/shard_map/broadcast_in_dim | solution.py:169
  10.8 10.0 %all-to-all-start = ((bf16[8,64,1024]{2,1,0:T(8,128)(2,1)}), bf16[8,64,1024]{2,1,0:T(8,128)(2,1)S(1)}, u32[]{:S(2)}, u32[]{:S(2)}) async-start(bf16[8,64,1024]{2,1,0:T(8,128)(2,1)} %broadcast_in_dim.13), calls=%async_computation | async-start | bytes 2097152 | tf_op jit(solution)/shard_map/all_to_all | solution.py:170
  20.8 0.0 copy-done.1
  20.8 0.0 copy-start
  20.9 7.5 %collective-permute-done.refs_3_ = bf16[256,1024]{1,0:T(8,128)(2,1)S(1)} collective-permute-done((bf16[256,1024]{1,0:T(8,128)(2,1)}, bf16[256,1024]{1,0:T(8,128)(2,1)S(1)}, u32[]{:S(2)}, u32[]{:S(2)}) %collective-permute-start) | collective-permute-done | bytes 524320 | tf_op jit(solution)/shard_map/ppermute | solution.py:22
  28.4 0.8 slice.19
  29.2 6.1 %collective-permute-start.4 = (bf16[192,1024]{1,0:T(8,128)(2,1)}, bf16[192,1024]{1,0:T(8,128)(2,1)S(1)}, u32[]{:S(2)}, u32[]{:S(2)}) collective-permute-start(bf16[192,1024]{1,0:T(8,128)(2,1)} %slice.19), channel_id=1, source_target_pairs={{0,48},{16,0},{32,16},{48,32},{1,49},{17,1},{33,17},{49,33},{2,50}... | collective-permute-start | bytes 1179656 | tf_op jit(solution)/shard_map/ppermute | solution.py:22
  35.3 0.0 collective-permute-done.1.refs_2_
  35.3 1.9 %collective-permute-start.3 = (bf16[64,1024]{1,0:T(8,128)(2,1)S(1)}, bf16[64,1024]{1,0:T(8,128)(2,1)S(1)}, u32[]{:S(2)}, u32[]{:S(2)}) collective-permute-start(bf16[64,1024]{1,0:T(8,128)(2,1)S(1)} %slice.18), channel_id=1, source_target_pairs={{0,16},{16,32},{32,48},{48,0},{1,17},{17,33},{33,49},{49,1},{2,18}... | collective-permute-start | bytes 393224 | tf_op jit(solution)/shard_map/ppermute | solution.py:22
  37.3 12.8 %all-to-all-done.refs_0_ = bf16[8,64,1024]{2,1,0:T(8,128)(2,1)S(1)} async-done(((bf16[8,64,1024]{2,1,0:T(8,128)(2,1)}), bf16[8,64,1024]{2,1,0:T(8,128)(2,1)S(1)}, u32[]{:S(2)}, u32[]{:S(2)}) %all-to-all-start) | async-done | bytes 1048608 | tf_op jit(solution)/shard_map/all_to_all | solution.py:170
  50.0 2.4 %collective-permute-start.2 = (bf16[8,64,1024]{2,1,0:T(8,128)(2,1)S(1)}, bf16[8,64,1024]{2,1,0:T(8,128)(2,1)S(1)}, u32[]{:S(2)}, u32[]{:S(2)}) collective-permute-start(bf16[8,64,1024]{2,1,0:T(8,128)(2,1)S(1)} %all-to-all-done.refs_0_), channel_id=1, source_target_pairs={{0,1},{1,0},{2,3},{3,2},{4,5},{5,4},{6,7},{7,6},{8,9},{9,8},{10,11... | collective-permute-start | bytes 3145736 | tf_op jit(solution)/shard_map/ppermute | solution.py:172
  52.4 1.1 %shard_map.38.refs_4_ = bf16[8,8,2,64,128]{4,3,2,1,0:T(8,128)(2,1)S(1)} custom-call(bf16[8,64,1024]{2,1,0:T(8,128)(2,1)S(1)} %all-to-all-done.refs_0_, bf16[256,1024]{1,0:T(8,128)(2,1)S(1)} %bitcast.9, bf16[256,1024]{1,0:T(8,128)(2,1)S(1)} %collective-permute-done.1.refs_2_, bf16[256,1024]{1,0:T(8,128)(2,1)S(1)} %collective-permute-done.refs_3_, ...), custom_call_target="tpu_custom_call" | custom-call | flops 99999997952 | bytes 5242880 | tf_op jit(solution)/shard_map/pallas_call | solution.py:90
  53.6 1.1 %collective-permute-done.2.refs_0_.refs_1_ = bf16[8,64,1024]{2,1,0:T(8,128)(2,1)S(1)} collective-permute-done((bf16[8,64,1024]{2,1,0:T(8,128)(2,1)S(1)}, bf16[8,64,1024]{2,1,0:T(8,128)(2,1)S(1)}, u32[]{:S(2)}, u32[]{:S(2)}) %collective-permute-start.2) | collective-permute-done | bytes 1048608 | tf_op jit(solution)/shard_map/ppermute | solution.py:172
  54.7 1.1 %shard_map.39.refs_4_ = bf16[8,8,2,64,128]{4,3,2,1,0:T(8,128)(2,1)S(1)} custom-call(bf16[8,64,1024]{2,1,0:T(8,128)(2,1)S(1)} %collective-permute-done.2.refs_0_.refs_1_, bf16[256,1024]{1,0:T(8,128)(2,1)S(1)} %bitcast.10, bf16[256,1024]{1,0:T(8,128)(2,1)S(1)} %collective-permute-done.1.refs_2_, ...), custom_call_target="tpu_custom_call", output_to_operand_aliasing={{}: (4, {})} | custom-call | flops 805306368 | bytes 5242880 | tf_op jit(solution)/shard_map/pallas_call | solution.py:90
  55.8 0.0 collective-permute-done.3.refs_2_
  55.9 0.0 collective-permute-done.4.refs_3_
  55.9 0.9 shard_map.40
  56.7 30.0 %all_to_all.15.refs_0_ = bf16[8,16,64,128]{3,2,1,0:T(8,128)(2,1)S(1)} all-to-all(bf16[8,16,64,128]{3,2,1,0:T(8,128)(2,1)S(1)} %bitcast.6), channel_id=1, replica_groups=mesh['x'=4,'yl'=2,'yh'=4,'z'=8,'core'=2] {'x','yl'}, dimensions={0} | all-to-all | bytes 4194304 | tf_op jit(solution)/shard_map/all_to_all | solution.py:183
  86.7 0.5 shard_map.41
  87.2 18.6 %all_to_all.16.terms_ref = bf16[16,64,128]{2,1,0:T(8,128)(2,1)S(1)} all-to-all(bf16[16,64,128]{2,1,0:T(8,128)(2,1)S(1)} %shard_map.41), channel_id=1, replica_groups=mesh['x'=4,'yl'=2,'yh'=4,'z'=8,'core'=2] {'z','core'}, dimensions={0} | all-to-all | bytes 524288 | tf_op jit(solution)/shard_map/all_to_all | solution.py:184
  105.9 0.8 shard_map.42
  (6 shorter events, 0.0 us)
Async XLA Ops:
  0.0 20.8 %copy-start.1 = (f32[1024]{0:T(1024)S(1)}, f32[1024]{0:T(1024)}, u32[]{:S(2)}) copy-start(f32[1024]{0:T(1024)} %param.5) | copy-start | bytes 12292
  0.0 28.4 %collective-permute-start = (bf16[256,1024]{1,0:T(8,128)(2,1)}, bf16[256,1024]{1,0:T(8,128)(2,1)S(1)}, u32[]{:S(2)}, u32[]{:S(2)}) collective-permute-start(bf16[256,1024]{1,0:T(8,128)(2,1)} %bitcast.7), channel_id=1, source_target_pairs={{0,48},{16,0},{32,16},{48,32},{1,49},{17,1},{33,17},{49,33},{2,50}... | collective-permute-start | bytes 1572872 | tf_op jit(solution)/shard_map/ppermute | solution.py:22
  6.8 28.4 %collective-permute-start.1 = (bf16[256,1024]{1,0:T(8,128)(2,1)}, bf16[256,1024]{1,0:T(8,128)(2,1)S(1)}, u32[]{:S(2)}, u32[]{:S(2)}) collective-permute-start(bf16[256,1024]{1,0:T(8,128)(2,1)} %bitcast.8), channel_id=1, source_target_pairs={{0,16},{16,32},{32,48},{48,0},{1,17},{17,33},{33,49},{49,1},{2,18}... | collective-permute-start | bytes 1572872 | tf_op jit(solution)/shard_map/ppermute | solution.py:22
  10.8 39.2 %all-to-all-start = ((bf16[8,64,1024]{2,1,0:T(8,128)(2,1)}), bf16[8,64,1024]{2,1,0:T(8,128)(2,1)S(1)}, u32[]{:S(2)}, u32[]{:S(2)}) async-start(bf16[8,64,1024]{2,1,0:T(8,128)(2,1)} %broadcast_in_dim.13), calls=%async_computation | async-start | bytes 2097152 | tf_op jit(solution)/shard_map/all_to_all | solution.py:170
  20.8 31.6 %copy-start = (bf16[1,256,1024]{2,1,0:T(8,128)(2,1)S(1)}, bf16[1,256,1024]{2,1,0:T(8,128)(2,1)}, u32[]{:S(2)}) copy-start(bf16[1,256,1024]{2,1,0:T(8,128)(2,1)} %param.4) | copy-start | bytes 1572868
  29.2 26.7 %collective-permute-start.4 = (bf16[192,1024]{1,0:T(8,128)(2,1)}, bf16[192,1024]{1,0:T(8,128)(2,1)S(1)}, u32[]{:S(2)}, u32[]{:S(2)}) collective-permute-start(bf16[192,1024]{1,0:T(8,128)(2,1)} %slice.19), channel_id=1, source_target_pairs={{0,48},{16,0},{32,16},{48,32},{1,49},{17,1},{33,17},{49,33},{2,50}... | collective-permute-start | bytes 1179656 | tf_op jit(solution)/shard_map/ppermute | solution.py:22
  35.3 20.5 %collective-permute-start.3 = (bf16[64,1024]{1,0:T(8,128)(2,1)S(1)}, bf16[64,1024]{1,0:T(8,128)(2,1)S(1)}, u32[]{:S(2)}, u32[]{:S(2)}) collective-permute-start(bf16[64,1024]{1,0:T(8,128)(2,1)S(1)} %slice.18), channel_id=1, source_target_pairs={{0,16},{16,32},{32,48},{48,0},{1,17},{17,33},{33,49},{49,1},{2,18}... | collective-permute-start | bytes 393224 | tf_op jit(solution)/shard_map/ppermute | solution.py:22
  50.0 4.7 %collective-permute-start.2 = (bf16[8,64,1024]{2,1,0:T(8,128)(2,1)S(1)}, bf16[8,64,1024]{2,1,0:T(8,128)(2,1)S(1)}, u32[]{:S(2)}, u32[]{:S(2)}) collective-permute-start(bf16[8,64,1024]{2,1,0:T(8,128)(2,1)S(1)} %all-to-all-done.refs_0_), channel_id=1, source_target_pairs={{0,1},{1,0},{2,3},{3,2},{4,5},{5,4},{6,7},{7,6},{8,9},{9,8},{10,11... | collective-permute-start | bytes 3145736 | tf_op jit(solution)/shard_map/ppermute | solution.py:172
